TPU v7x, 256 devices: a whole 4x4x8 slice. The times are simulated.
256 devices in a mesh: gx: 8 (over z), gy: 4 (over y), gz: 8 (over x, core).
Axes of the slice: x: 4, y: 4, z: 8, core: 2. Of those that a mesh axis runs over, the one named last changes fastest.
Arguments:
- populations: float32 [19, 32, 128, 1024], P(None, 'gx', 'gy', 'gz'), may hold values from 0.02 to 0.12
- solid: int32 [32, 128, 1024], P('gx', 'gy', 'gz'), may hold values 0 or 1
- link_cell: int32 [8, 4, 8, 1024], P('gx', 'gy', 'gz'), may hold values from 0 to 16383, as said below
- link_dir: int32 [8, 4, 8, 1024], P('gx', 'gy', 'gz'), may hold values from 1 to 18
- link_store: int32 [8, 4, 8, 1024], P('gx', 'gy', 'gz'), may hold values from 0 to 32768, as said below
- store_body: int32 [32768], replicated, may hold values from 0 to 7
- motion: float32 [8, 6], replicated, may hold values from -0.75 to 0.75
- inv_mass: float32 [8], replicated, may hold values from 1 to 8
- inv_inertia: float32 [8, 3], replicated, may hold values from 1 to 8
- centre: float32 [8, 3], replicated, may hold values from 0.2 to 0.8
- rates: float32 [15], replicated, may hold values from 0.5 to 1.9
Outputs:
- moved: float32 [19, 32, 128, 1024], P(None, 'gx', 'gy', 'gz')
- store_load: float32 [6, 32768], P(None, ('gx', 'gy', 'gz'))
- motion_next: float32 [8, 6], replicated
Inputs may be any that keep to these rules, and one draw needn't show every extreme that they name: `link_cell`: within one device's list the cells are distinct, counted over its 4 x 32 x 128 block with the last dimension fastest. `link_store`: the value 32768 marks an empty slot; in each device's list the live slots come first, from a quarter of 1024 to all of them, and the first device's list is full.
All inputs are finite; a program needn't handle non-finite values. No bound on the sum of `solid` on one device may be relied on, other than what follows from the above.
Results may differ from a plain program's by a relative error of at most 0.0001.
Values sent between devices are 32-bit elements; how exact they have to be, the bound alone decides.
No kernel may reach another device: no remote copies, remote signals or barrier semaphores. Data moves between devices by JAX's collectives and lax.ppermute only.
A program may use at most 64 MiB of HBM per device.

v0:
```python
import math

import jax
import jax.numpy as jnp
import numpy as np
from jax import lax
from jax.sharding import PartitionSpec as P


def with_halo(x, sides, width, wrap):
    for axis, dim in sides:
        devices, length = (lax.axis_size(axis), x.shape[dim])
        up = [(i, (i + 1) % devices) for i in range(devices if wrap else devices - 1)]
        down = [(j, i) for i, j in up]
        last = lax.slice_in_dim(x, length - width, length, axis=dim)
        first = lax.slice_in_dim(x, 0, width, axis=dim)
        before = lax.ppermute(last, axis, up)
        after = lax.ppermute(first, axis, down)
        x = jnp.concatenate([before, x, after], axis=dim)
    return x


def lattice_tables():
    speed_list = [
        [0, 0, 0],
        [1, 0, 0],
        [-1, 0, 0],
        [0, 1, 0],
        [0, -1, 0],
        [0, 0, 1],
        [0, 0, -1],
        [1, 1, 0],
        [-1, -1, 0],
        [1, -1, 0],
        [-1, 1, 0],
        [1, 0, 1],
        [-1, 0, -1],
        [1, 0, -1],
        [-1, 0, 1],
        [0, 1, 1],
        [0, -1, -1],
        [0, 1, -1],
        [0, -1, 1],
    ]
    speeds = np.array(speed_list) * 1.0
    weights = np.array([1.0 / 3.0] + [1.0 / 18.0] * 6 + [1.0 / 36.0] * 12)
    along_x = speeds[:, 0]
    along_y = speeds[:, 1]
    along_z = speeds[:, 2]
    square = along_x * along_x + along_y * along_y + along_z * along_z
    polynomials = np.stack(
        [
            np.ones(19),
            along_x,
            along_y,
            along_z,
            square,
            3 * along_x * along_x - square,
            along_y * along_y - along_z * along_z,
            along_x * along_y,
            along_y * along_z,
            along_x * along_z,
            along_x * square,
            along_y * square,
            along_z * square,
            square * square,
            (3 * along_x * along_x - square) * square,
            (along_y * along_y - along_z * along_z) * square,
            along_x * (along_y * along_y - along_z * along_z),
            along_y * (along_z * along_z - along_x * along_x),
            along_z * (along_x * along_x - along_y * along_y),
        ],
        axis=1,
    )
    columns = []
    for column_index in range(19):
        vector = polynomials[:, column_index] * 1.0
        for repeat in range(2):
            for earlier in columns:
                vector = vector - np.dot(earlier, vector) * earlier
        columns.append(vector / math.sqrt(float(np.dot(vector, vector))))
    return (speeds, weights, np.stack(columns))


def collide(flat, rates):
    speeds, weights, moments = lattice_tables()
    highest = lax.Precision.HIGHEST
    velocity = jnp.asarray(speeds, jnp.float32)
    weight = jnp.asarray(weights, jnp.float32)
    upper_moments = jnp.asarray(moments[4:], jnp.float32)
    relax = jnp.dot(
        upper_moments.T * rates[None, :],
        upper_moments,
        precision=highest,
        preferred_element_type=jnp.float32,
    )
    density = jnp.sum(flat, axis=0)
    momentum = jnp.dot(velocity.T, flat, precision=highest, preferred_element_type=jnp.float32)
    projected = jnp.dot(velocity, momentum, precision=highest, preferred_element_type=jnp.float32)
    magnitude = jnp.sum(momentum * momentum, axis=0)
    equilibrium = weight[:, None] * (
        density[None, :] + 3.0 * projected + 4.5 * projected * projected - 1.5 * magnitude[None, :]
    )
    return flat - jnp.dot(
        relax, flat - equilibrium, precision=highest, preferred_element_type=jnp.float32
    )


def stream(extended, size_x, size_y, size_z):
    speeds = lattice_tables()[0]
    result = []
    for direction in range(19):
        start_x = 1 - int(speeds[direction, 0])
        start_y = 1 - int(speeds[direction, 1])
        start_z = 1 - int(speeds[direction, 2])
        result.append(
            extended[
                direction,
                start_x : start_x + size_x,
                start_y : start_y + size_y,
                start_z : start_z + size_z,
            ]
        )
    return jnp.stack(result)


def wall_terms(
    picked, direction, place_x, place_y, place_z, body_index, motion, centre, live, grid
):
    speeds, weights, moments = lattice_tables()
    highest = lax.Precision.HIGHEST
    velocity = jnp.asarray(speeds, jnp.float32)
    weight = jnp.asarray(weights, jnp.float32)
    choose = (direction[:, None] == jnp.arange(19, dtype=jnp.int32)[None, :]).astype(jnp.float32)
    link_speed = jnp.dot(choose, velocity, precision=highest, preferred_element_type=jnp.float32)
    link_weight = jnp.dot(choose, weight, precision=highest, preferred_element_type=jnp.float32)
    pick_body = (
        body_index[:, None] == jnp.arange(motion.shape[0], dtype=jnp.int32)[None, :]
    ).astype(jnp.float32)
    link_motion = jnp.dot(pick_body, motion, precision=highest, preferred_element_type=jnp.float32)
    link_centre = jnp.dot(pick_body, centre, precision=highest, preferred_element_type=jnp.float32)
    extents = jnp.asarray([grid[0], grid[1], grid[2]], jnp.float32)
    position = jnp.stack([place_x, place_y, place_z], axis=1).astype(jnp.float32) + 0.5 * link_speed
    radius = (position - link_centre * extents[None, :]) / extents[1]
    wall = link_motion[:, 0:3] + jnp.cross(link_motion[:, 3:6], radius)
    normal_speed = jnp.sum(link_speed * wall, axis=1)
    values = picked - 6.0 * link_weight * normal_speed
    push = link_speed * (2.0 * picked - 6.0 * link_weight * normal_speed)[:, None]
    turn = jnp.cross(radius, push)
    loads = jnp.concatenate([push, turn], axis=1) * live.astype(jnp.float32)[:, None]
    return (values, loads, pick_body)


def advance(motion, body_load, inv_mass, inv_inertia, area):
    linear = motion[:, 0:3] + inv_mass[:, None] * body_load[:, 0:3] / area
    angular = motion[:, 3:6] + inv_inertia * body_load[:, 3:6] / area
    return jnp.concatenate([linear, angular], axis=1)


def body(
    populations,
    solid,
    link_cell,
    link_dir,
    link_store,
    store_body,
    motion,
    inv_mass,
    inv_inertia,
    centre,
    rates,
):
    highest = lax.Precision.HIGHEST
    width_x = populations.shape[1]
    width_y = populations.shape[2]
    width_z = populations.shape[3]
    cells = width_x * width_y * width_z
    flat = populations.reshape(19, cells)
    post = collide(flat, rates)
    post = jnp.where(solid.reshape(1, cells) == 1, flat, post)
    post_grid = post.reshape(19, width_x, width_y, width_z)
    spanned = with_halo(post_grid, (("gz", 3),), 1, True)
    extended = with_halo(spanned, (("gx", 1), ("gy", 2)), 1, False)
    moved = stream(extended, width_x, width_y, width_z)
    count_x = lax.axis_size("gx")
    count_y = lax.axis_size("gy")
    count_z = lax.axis_size("gz")
    place_x = lax.axis_index("gx")
    place_y = lax.axis_index("gy")
    place_z = lax.axis_index("gz")
    count_links = link_cell.shape[-1]
    cell_index = link_cell.reshape(count_links)
    direction = link_dir.reshape(count_links)
    store = link_store.reshape(count_links)
    stores_all = store_body.shape[0]
    live = store < stores_all
    store_index = jnp.minimum(store, stores_all - 1)
    body_index = store_body[store_index]
    cell_x = cell_index // (width_y * width_z) + place_x * width_x
    cell_y = cell_index // width_z % width_y + place_y * width_y
    cell_z = cell_index % width_z + place_z * width_z
    grid = (width_x * count_x, width_y * count_y, width_z * count_z)
    picked = post.reshape(-1)[direction * cells + cell_index]
    values, loads, pick_body = wall_terms(
        picked, direction, cell_x, cell_y, cell_z, body_index, motion, centre, live, grid
    )
    opposite = direction + 1 - 2 * ((direction + 1) % 2)
    target = jnp.where(live, opposite * cells + cell_index, 19 * cells)
    moved = (
        moved.reshape(-1).at[target].set(values, mode="drop").reshape(19, width_x, width_y, width_z)
    )
    partial_loads = jax.ops.segment_sum(loads, store_index, num_segments=stores_all).T
    own_loads = lax.psum_scatter(partial_loads, ("gx", "gy", "gz"), scatter_dimension=1, tiled=True)
    devices_all = count_x * count_y * count_z
    area = count_links * devices_all // motion.shape[0]
    own_count = own_loads.shape[1]
    linear_index = (place_x * count_y + place_y) * count_z + place_z
    own_body = lax.dynamic_slice_in_dim(
        store_body, (linear_index * own_count).astype(jnp.int32), own_count
    )
    pick_own = (own_body[:, None] == jnp.arange(motion.shape[0], dtype=jnp.int32)[None, :]).astype(
        jnp.float32
    )
    body_part = jnp.dot(own_loads, pick_own, precision=highest, preferred_element_type=jnp.float32)
    body_load = lax.psum(body_part, ("gx", "gy", "gz"))
    motion_next = advance(motion, body_load.T, inv_mass, inv_inertia, area)
    return (moved, own_loads, motion_next)


def solution(mesh):
    return jax.shard_map(
        body,
        mesh=mesh,
        in_specs=(
            P(None, "gx", "gy", "gz"),
            P("gx", "gy", "gz"),
            P("gx", "gy", "gz", None),
            P("gx", "gy", "gz", None),
            P("gx", "gy", "gz", None),
            P(),
            P(),
            P(),
            P(),
            P(),
            P(),
        ),
        out_specs=(P(None, "gx", "gy", "gz"), P(None, ("gx", "gy", "gz")), P()),
        check_vma=False,
    )
```

profile of v0, /device:TPU:2, one launch (start us, length us, event | category | flops | bytes accessed | tf_op | source)
XLA Modules:
  0.0 1444.8 jit_solution(2243766362573452154)
XLA Ops:
  7.2 1.5 reduce_sum.27
  9.0 0.9 copy.35
  10.0 1.1 multiply_reduce_fusion
  11.1 1.4 fusion.51
  12.8 1.9 fusion
  15.0 0.9 copy-done.4
  16.0 1.5 fusion.50
  17.5 1.8 copy.34
  20.3 1.6 reshape.515
  23.0 6.2 gather_fusion
  29.2 6.2 gather_fusion.1
  36.6 1.0 copy.30
  38.1 1.6 copy.26
  39.7 2.7 pad_maximum_fusion
  42.3 3.8 collective-permute-start.2
  46.2 1.5 collective-permute-start.3
  47.7 14.1 scatter_custom_fusion.1
  61.8 1.1 slice.193
  63.0 2.3 collective-permute-done.3
  65.3 1.8 pad_maximum_fusion.3
  67.1 3.5 collective-permute-start.4
  70.6 1.3 collective-permute-start.5
  73.4 4.0 collective-permute-done.5
  78.6 0.9 maximum_dynamic-update-slice_fusion.6
  79.4 0.9 maximum_dynamic-update-slice_fusion.5
  81.2 0.9 maximum_dynamic-update-slice_fusion.2
  83.5 1.0 copy-done.3
  84.5 6.6 scatter_fusion
  91.2 1264.9 %reduce-scatter.2.cloned.1.call-done = f32[6,128]{0,1:T(8,128)} async-done(((f32[6,32768]{0,1:T(8,128)}), f32[6,128]{0,1:T(8,128)}) %reduce-scatter.2.cloned.1.call-update) | async-done | bytes 3088 | tf_op jit(solution)/shard_map/reduce_scatter | solution.py:213
  1356.1 1.1 fusion.30
  1357.2 78.5 %psum.7 = f32[8,6]{1,0:T(8,128)S(1)} all-reduce(f32[8,6]{1,0:T(8,128)S(1)} %fusion.30), channel_id=1, replica_groups=mesh['gx'=8,'gy'=4,'gz'=8] {'gx','gy','gz'}, use_global_device_ids=true, to_apply=%region_6.8 | all-reduce | flops 48 | bytes 384 | tf_op jit(solution)/shard_map/psum | solution.py:225
  1436.5 1.5 copy.32
  (88 shorter events, 10.6 us)
Async XLA Ops:
  7.2 28.7 %copy-start = (f32[8,3]{0,1:T(4,128)S(1)}, f32[8,3]{0,1:T(4,128)}, u32[]{:S(2)}) copy-start(f32[8,3]{0,1:T(4,128)} %param.28) | copy-start | bytes 292
  7.2 1.7 copy-start.5
  7.2 1348.9 %reduce-scatter.2.cloned.1.call-start = ((), (), s32[]{:S(2)}) async-start(), calls=%async_computation.1 | async-start | bytes 16842752 | tf_op jit(solution)/shard_map/reduce_scatter | solution.py:213
  9.0 0.9 copy-start.7
  11.0 1.5 copy-start.6
  11.0 1.5 copy-start.15
  11.1 1.5 copy-start.16
  11.1 1.8 copy-start.14
  14.7 1.2 copy-start.4
  19.3 18.3 %collective-permute-start.1 = (f32[19,4,32,1]{2,1,3,0:T(4,128)S(1)}, f32[19,4,32,1]{2,1,3,0:T(4,128)S(1)}, u32[]{:S(2)}, u32[]{:S(2)}) collective-permute-start(f32[19,4,32,1]{2,1,3,0:T(4,128)S(1)} %copy.34), channel_id=1, source_target_pairs={{1,0},{2,1},{3,2},{4,3},{5,4},{6,5},{7,6},{0,7},{9,8},{10,9},{11,1... | collective-permute-start | bytes 29192 | tf_op jit(solution)/shard_map/ppermute | solution.py:18
  19.8 18.3 %collective-permute-start = (f32[19,4,32,1]{2,1,3,0:T(4,128)S(1)}, f32[19,4,32,1]{2,1,3,0:T(4,128)S(1)}, u32[]{:S(2)}, u32[]{:S(2)}) collective-permute-start(f32[19,4,32,1]{2,1,3,0:T(4,128)S(1)} %copy.33), channel_id=1, source_target_pairs={{0,1},{1,2},{2,3},{3,4},{4,5},{5,6},{6,7},{7,0},{8,9},{9,10},{10,1... | collective-permute-start | bytes 29192 | tf_op jit(solution)/shard_map/ppermute | solution.py:17
  20.3 1.6 copy-start.11
  20.3 2.1 copy-start.18
  20.3 2.5 copy-start.8
  20.3 2.6 copy-start.10
  23.0 6.2 copy-start.2
  29.2 6.2 copy-start.9
  29.2 6.7 copy-start.17
  42.3 20.7 %collective-permute-start.2 = (f32[19,1,32,130]{3,2,1,0:T(8,128)}, f32[19,1,32,130]{3,2,1,0:T(8,128)S(1)}, u32[]{:S(2)}, u32[]{:S(2)}) collective-permute-start(f32[19,1,32,130]{3,2,1,0:T(8,128)} %get-tuple-element.15), channel_id=1, source_target_pairs={{0,32},{32,64},{64,96},{96,128},{128,160},{160,192},{192,224},{1,3... | collective-permute-start | bytes 948488 | tf_op jit(solution)/shard_map/ppermute | solution.py:17
  46.2 19.1 %collective-permute-start.3 = (f32[19,1,32,130]{3,2,1,0:T(8,128)}, f32[19,1,32,130]{3,2,1,0:T(8,128)}, u32[]{:S(2)}, u32[]{:S(2)}) collective-permute-start(f32[19,1,32,130]{3,2,1,0:T(8,128)} %get-tuple-element.14), channel_id=1, source_target_pairs={{32,0},{64,32},{96,64},{128,96},{160,128},{192,160},{224,192},{33,... | collective-permute-start | bytes 948488 | tf_op jit(solution)/shard_map/ppermute | solution.py:18
  61.7 1.2 copy-start.12
  63.0 8.9 copy-start.1
  67.1 6.2 collective-permute-start.4
  70.6 6.8 collective-permute-start.5
  83.5 1.0 copy-start.3
  84.5 1351.2 %copy-start.13 = (f32[8]{0:T(128)S(1)}, f32[8]{0:T(128)}, u32[]{:S(2)}) copy-start(f32[8]{0:T(128)} %param.26) | copy-start | bytes 100
Sparse Core Ops, SparseCore 0:
  61.9 1294.1 reduce-scatter.1
where the time goes:
time: 1450 us; the launch traced here: 1440 us
  waiting for transfers between devices  1270 us (88%)
  blocking collectives  78.5 us (5%)
  local copies, waits for them, and re-layouts  33.8 us (2%)
  other arithmetic  28 us (2%)
  between operations  14.6 us (1%)
    reduce_scatter x1, waiting for transfers between devices, body(): lax.psum_scatter(partial_loads, ('gx', 'gy', 'gz'), scatter_dimension=1,...  1260 us
    psum x1, blocking collectives, body(): body_load = lax.psum(body_part, ('gx', 'gy', 'gz'))  78.5 us
  transfers between devices with their start and end apart: 7, of which 4 were waited for; matrix products, arithmetic and copies ran while one was open for 3% of the time, Pallas kernels for 0%

commit v1 on v0

v1 whole, which is shorter than its diff:
```python
import math

import jax
import jax.numpy as jnp
import numpy as np
from jax import lax
from jax.experimental import pallas as pl
from jax.experimental.pallas import tpu as pltpu
from jax.sharding import PartitionSpec as P

F32 = jnp.float32
BF16 = jnp.bfloat16
I32 = jnp.int32

XP, XM = (1, 7, 9, 11, 13), (2, 10, 8, 14, 12)
YP, YM = (3, 7, 10, 15, 17), (4, 9, 8, 18, 16)
ZP, ZM = (5, 11, 14, 15, 18), (6, 13, 12, 17, 16)


def lattice_tables():
    speed_list = [
        [0, 0, 0],
        [1, 0, 0],
        [-1, 0, 0],
        [0, 1, 0],
        [0, -1, 0],
        [0, 0, 1],
        [0, 0, -1],
        [1, 1, 0],
        [-1, -1, 0],
        [1, -1, 0],
        [-1, 1, 0],
        [1, 0, 1],
        [-1, 0, -1],
        [1, 0, -1],
        [-1, 0, 1],
        [0, 1, 1],
        [0, -1, -1],
        [0, 1, -1],
        [0, -1, 1],
    ]
    speeds = np.array(speed_list) * 1.0
    weights = np.array([1.0 / 3.0] + [1.0 / 18.0] * 6 + [1.0 / 36.0] * 12)
    along_x = speeds[:, 0]
    along_y = speeds[:, 1]
    along_z = speeds[:, 2]
    square = along_x * along_x + along_y * along_y + along_z * along_z
    polynomials = np.stack(
        [
            np.ones(19),
            along_x,
            along_y,
            along_z,
            square,
            3 * along_x * along_x - square,
            along_y * along_y - along_z * along_z,
            along_x * along_y,
            along_y * along_z,
            along_x * along_z,
            along_x * square,
            along_y * square,
            along_z * square,
            square * square,
            (3 * along_x * along_x - square) * square,
            (along_y * along_y - along_z * along_z) * square,
            along_x * (along_y * along_y - along_z * along_z),
            along_y * (along_z * along_z - along_x * along_x),
            along_z * (along_x * along_x - along_y * along_y),
        ],
        axis=1,
    )
    columns = []
    for column_index in range(19):
        vector = polynomials[:, column_index] * 1.0
        for repeat in range(2):
            for earlier in columns:
                vector = vector - np.dot(earlier, vector) * earlier
        columns.append(vector / math.sqrt(float(np.dot(vector, vector))))
    return (speeds, weights, np.stack(columns))


def collision_scalars(rate):
    m = lattice_tables()[2]
    r = {k: rate(k - 4) for k in range(4, 19)}
    f = lambda v: float(v)
    out = {}
    for name, column in (("rest", 0), ("axis", 1), ("diag", 7)):
        for other, column2 in (("rest", 0), ("axis", 1), ("diag", 7)):
            out[name, other] = r[4] * f(m[4, column] * m[4, column2]) + r[13] * f(
                m[13, column] * m[13, column2]
            )
    a5, b5, a14, b14 = m[5, 1] / 2, m[5, 7], m[14, 1] / 2, m[14, 7]
    out["uu"] = r[5] * f(a5 * a5) + r[14] * f(a14 * a14)
    out["uv"] = r[5] * f(a5 * b5) + r[14] * f(a14 * b14)
    out["vv"] = r[5] * f(b5 * b5) + r[14] * f(b14 * b14)
    a6, b6, a15, b15 = m[6, 3], m[6, 7], m[15, 3], m[15, 7]
    out["pp"] = r[6] * f(a6 * a6) + r[15] * f(a15 * a15)
    out["pq"] = r[6] * f(a6 * b6) + r[15] * f(a15 * b15)
    out["qq"] = r[6] * f(b6 * b6) + r[15] * f(b15 * b15)
    out["sxy"] = r[7] * f(m[7, 7] ** 2)
    out["syz"] = r[8] * f(m[8, 15] ** 2)
    out["sxz"] = r[9] * f(m[9, 11] ** 2)
    for name, row, axis, diag in (("x", 10, 1, 7), ("y", 11, 3, 7), ("z", 12, 5, 11)):
        out["aa" + name] = r[row] * f(m[row, axis] ** 2)
        out["ab" + name] = r[row] * f(m[row, axis] * m[row, diag])
        out["bb" + name] = r[row] * f(m[row, diag] ** 2)
    out["tx"] = r[16] * f(m[16, 7] ** 2)
    out["ty"] = r[17] * f(m[17, 15] ** 2)
    out["tz"] = r[18] * f(m[18, 11] ** 2)
    return out


def collide(f, k):
    w1, w2 = 1.0 / 18.0, 1.0 / 36.0
    pairs = ((1, 2), (3, 4), (5, 6), (7, 8), (9, 10), (11, 12), (13, 14), (15, 16), (17, 18))
    plus = [f[i] + f[o] for i, o in pairs]
    minus = [f[i] - f[o] for i, o in pairs]
    sx, sy, sz, sa, sb, sc, sd, se, sg = plus
    dx, dy, dz, da, db, dc, dd, de, dg = minus
    density = f[0] + ((sx + sy + sz) + (sa + sb) + (sc + sd) + (se + sg))
    jx = dx + (da + db) + (dc + dd)
    jy = dy + (da - db) + (de + dg)
    jz = dz + (dc - dd) + (de - dg)
    magnitude = jx * jx + jy * jy + jz * jz
    base = density - 1.5 * magnitude
    axis_base = (2.0 * w1) * base
    diag_base = (2.0 * w2) * base
    n0 = f[0] - (1.0 / 3.0) * base
    sx = sx - (axis_base + (9.0 * w1) * (jx * jx))
    sy = sy - (axis_base + (9.0 * w1) * (jy * jy))
    sz = sz - (axis_base + (9.0 * w1) * (jz * jz))

    def diagonal(s, project):
        return s - (diag_base + (9.0 * w2) * (project * project))

    sa, sb = diagonal(sa, jx + jy), diagonal(sb, jx - jy)
    sc, sd = diagonal(sc, jx + jz), diagonal(sd, jx - jz)
    se, sg = diagonal(se, jy + jz), diagonal(sg, jy - jz)
    dx, dy, dz = dx - (6.0 * w1) * jx, dy - (6.0 * w1) * jy, dz - (6.0 * w1) * jz
    hx, hy, hz = (6.0 * w2) * jx, (6.0 * w2) * jy, (6.0 * w2) * jz
    da, db = da - (hx + hy), db - (hx - hy)
    dc, dd = dc - (hx + hz), dd - (hx - hz)
    de, dg = de - (hy + hz), dg - (hy - hz)
    exy, exz, eyz = sa + sb, sc + sd, se + sg
    axis_sum = sx + sy + sz
    diag_sum = exy + exz + eyz
    g0 = k["rest", "rest"] * n0 + k["rest", "axis"] * axis_sum + k["rest", "diag"] * diag_sum
    ga = k["axis", "rest"] * n0 + k["axis", "axis"] * axis_sum + k["axis", "diag"] * diag_sum
    gd = k["diag", "rest"] * n0 + k["diag", "axis"] * axis_sum + k["diag", "diag"] * diag_sum
    u = 2.0 * sx - sy - sz
    v = exy + exz - 2.0 * eyz
    gu = k["uu"] * u + k["uv"] * v
    gv = k["uv"] * u + k["vv"] * v
    p = sy - sz
    q = exy - exz
    gp = k["pp"] * p + k["pq"] * q
    gq = k["pq"] * p + k["qq"] * q
    ga_u, gd_v = ga - gu, gd + gv
    even = [ga + 2.0 * gu, ga_u + gp, ga_u - gp]
    gxy, gxz, gyz = gd_v + gq, gd_v - gq, gd - 2.0 * gv
    for total, one, two, rate in ((gxy, sa, sb, "sxy"), (gxz, sc, sd, "sxz"), (gyz, se, sg, "syz")):
        shear = k[rate] * (one - two)
        even += [total + shear, total - shear]
    x_xy, x_xz = da + db, dc + dd
    y_xy, y_yz = da - db, de + dg
    z_xz, z_yz = dc - dd, de - dg
    x_all, y_all, z_all = x_xy + x_xz, y_xy + y_yz, z_xz + z_yz
    ox = k["aax"] * dx + k["abx"] * x_all
    oy = k["aay"] * dy + k["aby"] * y_all
    oz = k["aaz"] * dz + k["abz"] * z_all
    bx = k["abx"] * dx + k["bbx"] * x_all
    by = k["aby"] * dy + k["bby"] * y_all
    bz = k["abz"] * dz + k["bbz"] * z_all
    tx, ty, tz = k["tx"] * (x_xy - x_xz), k["ty"] * (y_yz - y_xy), k["tz"] * (z_xz - z_yz)
    x_on_xy, x_on_xz = bx + tx, bx - tx
    y_on_yz, y_on_xy = by + ty, by - ty
    z_on_xz, z_on_yz = bz + tz, bz - tz
    odd = [ox, oy, oz]
    odd += [x_on_xy + y_on_xy, x_on_xy - y_on_xy]
    odd += [x_on_xz + z_on_xz, x_on_xz - z_on_xz]
    odd += [y_on_yz + z_on_yz, y_on_yz - z_on_yz]
    post = [f[0] - g0]
    for (i, o), even_part, odd_part in zip(pairs, even, odd):
        post += [f[i] - (even_part + odd_part), f[o] - (even_part - odd_part)]
    return post


def halves(x):
    high = x.astype(BF16)
    return high, (x - high.astype(F32)).astype(BF16)


def rows_dot(a, b):
    return lax.dot_general(a, b, (((1,), (1,)), ((), ())), preferred_element_type=F32)


def iota(shape, dim):
    return lax.broadcasted_iota(I32, shape, dim)


def pick(conditions, values, shape):
    result = jnp.zeros(shape, F32)
    for condition, value in zip(conditions, values):
        if isinstance(value, float) and value == 0.0:
            continue
        result = jnp.where(condition, value, result)
    return result


def first_kernel(
    pop_ref,
    solid_ref,
    cell_ref,
    dir_ref,
    store_ref,
    owner_ref,
    motion_ref,
    centre_ref,
    rates_ref,
    post_ref,
    bounce_ref,
    send_ref,
    xp_ref,
    xm_ref,
    yp_ref,
    ym_ref,
    xy_ref,
    picked_ref,
    column_ref,
):
    speeds, weights, _ = lattice_tables()
    links = cell_ref.shape[1]
    place_x, place_y, place_z = (lax.axis_index(a) for a in ("gx", "gy", "gz"))
    cell = cell_ref[...]
    direction = dir_ref[...]
    store = store_ref[...]
    live = store < 32768
    row = lax.shift_right_logical(cell, 7)
    lane = cell & 127
    rows_hot = (iota((128, links), 0) == row).astype(F32)
    lanes_hot = (iota((128, links), 0) == lane).astype(F32)
    rows_hot16 = rows_hot.astype(BF16)
    lanes_hot16 = lanes_hot.astype(BF16)
    store_high = lax.shift_right_logical(store, 7)
    low_hot = (iota((128, links), 0) == (store & 127)).astype(F32).astype(BF16)
    by_high = jnp.dot(
        owner_ref[...].astype(F32).astype(BF16), low_hot, preferred_element_type=F32
    )
    body = jnp.sum(
        jnp.where(iota((256, links), 0) == store_high, by_high, 0.0), axis=0, keepdims=True
    )
    is_dir = [direction == i for i in range(19)]
    shape = direction.shape
    speed = [pick(is_dir, [float(s) for s in speeds[:, a]], shape) for a in range(3)]
    weight = jnp.where(direction <= 6, float(weights[1]), float(weights[7]))
    is_body = [body == float(b) for b in range(8)]
    move = [pick(is_body, [motion_ref[b, c] for b in range(8)], shape) for c in range(6)]
    middle = [pick(is_body, [centre_ref[b, a] for b in range(8)], shape) for a in range(3)]
    place = (
        lax.shift_right_logical(cell, 12) + place_x * 4,
        (row & 31) + place_y * 32,
        lane + place_z * 128,
    )
    extents = (32.0, 128.0, 1024.0)
    radius = [
        (place[a].astype(F32) + 0.5 * speed[a] - middle[a] * extents[a]) / 128.0 for a in range(3)
    ]

    def cross(a, b):
        return [a[(i + 1) % 3] * b[(i + 2) % 3] - a[(i + 2) % 3] * b[(i + 1) % 3] for i in range(3)]

    spin = cross(move[3:], radius)
    normal = sum(speed[a] * (move[a] + spin[a]) for a in range(3))
    wall = 6.0 * weight * normal
    coded = jnp.where(live, direction, 0).astype(F32)
    wall_high, wall_low = halves(wall)
    laid = rows_dot(
        rows_hot16,
        jnp.concatenate(
            [
                (lanes_hot * coded).astype(BF16),
                lanes_hot16 * wall_high,
                lanes_hot16 * wall_low,
            ],
            axis=0,
        ),
    )
    bounce_ref[0] = laid[:, 0:128]
    bounce_ref[1] = laid[:, 128:256] + laid[:, 256:384]

    k = collision_scalars(lambda i: rates_ref[i])
    at_lane = iota((8, 128), 1)

    def block(step, carry):
        rows = pl.ds(pl.multiple_of(step * 8, 8), 8)
        f = [pop_ref[i, rows, :] for i in range(19)]
        post = collide(f, k)
        fixed = solid_ref[rows, :] == 1
        post = [jnp.where(fixed, before, after) for before, after in zip(f, post)]
        code = bounce_ref[0, rows, :]
        found = jnp.zeros((8, 128), F32)
        for i in range(19):
            post_ref[i, rows, :] = post[i]
            if i:
                found = jnp.where(code == float(i), post[i], found)
        picked_ref[rows, :] = found
        bounce_ref[1, rows, :] = found - bounce_ref[1, rows, :]
        column = jnp.zeros((8, 128), F32)
        for n in range(5):
            column = jnp.where(at_lane == n, pltpu.roll(post[ZP[n]], n + 1, 1), column)
            turned = pltpu.roll(post[ZM[n]], 8 + n, 1)
            column = jnp.where(at_lane == 8 + n, turned, column)
        column_ref[rows, :] = column
        return carry

    lax.fori_loop(0, 16, block, 0)

    for n in range(5):
        xp_ref[n] = post_ref[XP[n], 96:128, :]
        xm_ref[n] = post_ref[XM[n], 0:32, :]
        for x in range(4):
            yp_ref[4 * n + x : 4 * n + x + 1, :] = post_ref[YP[n], 32 * x + 31 : 32 * x + 32, :]
            ym_ref[4 * n + x : 4 * n + x + 1, :] = post_ref[YM[n], 32 * x : 32 * x + 1, :]
    yp_ref[20:24, :] = jnp.zeros((4, 128), F32)
    ym_ref[20:24, :] = jnp.zeros((4, 128), F32)
    xy_ref[...] = jnp.zeros((8, 128), F32)
    xy_ref[0:1, :] = post_ref[7, 127:128, :]
    xy_ref[1:2, :] = post_ref[8, 0:1, :]
    xy_ref[2:3, :] = post_ref[9, 96:97, :]
    xy_ref[3:4, :] = post_ref[10, 31:32, :]

    found_high, found_low = halves(picked_ref[...])
    by_row = jnp.dot(
        jnp.concatenate([found_high, found_low], axis=0), lanes_hot16, preferred_element_type=F32
    )
    picked = jnp.sum((by_row[0:128] + by_row[128:256]) * rows_hot, axis=0, keepdims=True)
    strength = jnp.where(live, 2.0 * picked - wall, 0.0)
    push = [speed[a] * strength for a in range(3)]
    turn = cross(radius, push)
    record = jnp.concatenate(push + turn + [store.astype(F32), body], axis=0)
    columns = jnp.transpose(column_ref[...])
    upward = lax.rem(place_z + 1, 8)
    for j in range(8):
        for tile in range(links // 128):
            send_ref[j, tile] = record[:, tile * 128 : (tile + 1) * 128]
        send_ref[j, 8] = jnp.where(upward == j, columns[0:8], columns[8:16])


def second_kernel(got_ref, xy_ref, send_ref, total_ref, body_ref):
    place_x, place_y, place_z = (lax.axis_index(a) for a in ("gx", "gy", "gz"))
    total_ref[...] = jnp.zeros_like(total_ref)
    body_ref[...] = jnp.zeros_like(body_ref)
    links = 1024

    def one(peer, carry):
        record = jnp.concatenate([got_ref[peer, tile] for tile in range(8)], axis=1)
        store = record[6:7].astype(I32)
        body = record[7:8]
        loads = jnp.where(iota((8, links), 0) < 6, record, 0.0)
        owner = lax.shift_right_logical(store, 7)
        mine = (owner & 7) == place_z
        high = jnp.where(mine, lax.shift_right_logical(owner, 4), -1)
        low = ((lax.shift_right_logical(owner, 3) & 1) * 128) + (store & 127)
        both = jnp.concatenate(halves(loads), axis=0)
        none = jnp.zeros_like(both)
        spread = jnp.concatenate([jnp.where(high == h, both, none) for h in range(16)], axis=0)
        low_hot = (iota((256, links), 0) == low).astype(F32).astype(BF16)
        total_ref[...] += rows_dot(spread, low_hot)
        for b in range(8):
            part = jnp.where(body == float(b), loads, 0.0)
            body_ref[b] += sum(part[:, 128 * t : 128 * t + 128] for t in range(8))
        return carry

    lax.fori_loop(0, 8, one, 0)

    at_lane = iota((8, 128), 1)
    at_row = iota((8, 128), 0)
    body_row = jnp.zeros((8, 128), F32)
    for b in range(8):
        column = jnp.sum(body_ref[b], axis=1, keepdims=True)
        body_row = jnp.where(at_lane == at_row * 8 + b, column, body_row)
    body_row = jnp.where(at_row < 6, body_row, 0.0)
    body_row = jnp.sum(body_row, axis=0, keepdims=True)
    for h in range(16):
        for e in range(2):
            lanes = slice(128 * e, 128 * e + 128)
            tile = total_ref[16 * h : 16 * h + 8, lanes] + total_ref[16 * h + 8 : 16 * h + 16, lanes]
            tile = jnp.where(at_row == 6, body_row, tile)
            send_ref[2 * h + e] = jnp.where(at_row == 7, 0.0, tile)

    below = got_ref[lax.rem(place_z + 7, 8), 8]
    above = got_ref[lax.rem(place_z + 1, 8), 8]
    lane = iota((1, 128), 1)

    def turned(x, by):
        return pltpu.roll(x, by, 1)

    to_xp = jnp.where(lane < 32, turned(below[1:2], 32), turned(above[1:2], 64))
    to_xm = jnp.where(lane < 32, below[2:3], turned(above[2:3], 32))
    in_row = lane & 31
    to_yp = jnp.where(in_row == 0, turned(below[3:4], 97), turned(above[3:4], 98))
    to_ym = jnp.where(in_row == 0, below[4:5], turned(above[4:5], 1))
    me = place_x * 4 + place_y
    has_xp, has_xm = place_x < 7, place_x > 0
    has_yp, has_ym = place_y < 3, place_y > 0
    for there, step, line in (
        (has_xp, 4, to_xp),
        (has_xm, -4, to_xm),
        (has_yp, 1, to_yp),
        (has_ym, -1, to_ym),
        (has_xp & has_yp, 5, xy_ref[0:1, :]),
        (has_xm & has_ym, -5, xy_ref[1:2, :]),
        (has_xp & has_ym, 3, xy_ref[2:3, :]),
        (has_xm & has_yp, -3, xy_ref[3:4, :]),
    ):

        @pl.when(there)
        def _(step=step, line=line):
            send_ref[me + step, 7:8, :] = line


def third_kernel(
    post_ref,
    bounce_ref,
    got1_ref,
    got2_ref,
    xp_ref,
    xm_ref,
    yp_ref,
    ym_ref,
    motion_ref,
    mass_ref,
    inertia_ref,
    moved_ref,
    load_ref,
    next_ref,
):
    speeds = lattice_tables()[0].astype(int)
    place_x, place_y, place_z = (lax.axis_index(a) for a in ("gx", "gy", "gz"))
    has_xp, has_xm = place_x < 7, place_x > 0
    has_yp, has_ym = place_y < 3, place_y > 0
    me = place_x * 4 + place_y
    total = got2_ref[0]
    for j in range(1, 32):
        total = total + got2_ref[j]
    load_ref[...] = total[0:6]
    at_lane = iota((8, 128), 1)
    at_row = iota((8, 128), 0)
    own = jnp.where((at_lane & 7) == at_row, total[6:7], 0.0)
    body_load = jnp.zeros((8, 128), F32)
    scale = jnp.zeros((8, 128), F32)
    for c in range(6):
        column = jnp.sum(
            jnp.where(lax.shift_right_logical(at_lane, 3) == c, own, 0.0), axis=1, keepdims=True
        )
        body_load = jnp.where(at_lane == c, column, body_load)
        for b in range(8):
            value = mass_ref[b] if c < 3 else inertia_ref[b, c - 3]
            scale = jnp.where((at_lane == c) & (at_row == b), value, scale)
    next_ref[...] = motion_ref[...] + (scale * body_load)[:, 0:6] / 32768.0

    def edge(there, step):
        line = got2_ref[jnp.where(there, me + step, me), 7:8, :]
        return jnp.where(there, line, 0.0)

    lane = iota((1, 128), 1)
    row_in_plane = lane & 31
    from_x = {1: edge(has_xm, -4), -1: edge(has_xp, 4)}
    from_y = {1: edge(has_ym, -1), -1: edge(has_yp, 1)}
    from_xy = {
        (1, 1): edge(has_xm & has_ym, -5),
        (-1, -1): edge(has_xp & has_yp, 5),
        (1, -1): edge(has_xm & has_yp, -3),
        (-1, 1): edge(has_xp & has_ym, 3),
    }
    entering = {}
    for dirs, face in (
        (ZP, got1_ref[lax.rem(place_z + 7, 8), 8]),
        (ZM, got1_ref[lax.rem(place_z + 1, 8), 8]),
    ):
        for n, i in enumerate(dirs):
            line = face[n : n + 1]
            cx, cy, cz = (int(s) for s in speeds[i])
            if cx == 1:
                came = from_x[1] if cz == 1 else pltpu.roll(from_x[1], 96, 1)
                line = jnp.where(lane < 32, came, pltpu.roll(line, 32, 1))
            if cx == -1:
                came = pltpu.roll(from_x[-1], 96 if cz == 1 else 64, 1)
                line = jnp.where(lane >= 96, came, pltpu.roll(line, 96, 1))
            if cy == 1:
                came = from_y[1] if cz == 1 else pltpu.roll(from_y[1], 127, 1)
                line = jnp.where(row_in_plane == 0, came, pltpu.roll(line, 1, 1))
            if cy == -1:
                came = pltpu.roll(from_y[-1], 31 if cz == 1 else 30, 1)
                line = jnp.where(row_in_plane == 31, came, pltpu.roll(line, 127, 1))
            entering[i] = line
    order = ZP + ZM
    lines = jnp.concatenate(
        [entering[i] for i in order] + [jnp.zeros((118, 128), F32)], axis=0
    )
    columns = jnp.transpose(lines)

    plane_lane = iota((32, 128), 1)
    plane_row = iota((32, 128), 0)
    for x in range(4):
        rows = slice(32 * x, 32 * x + 32)
        code = bounce_ref[0, rows, :]
        value = bounce_ref[1, rows, :]
        for i in range(19):
            cx, cy, cz = (int(s) for s in speeds[i])
            source = x - cx
            if 0 <= source < 4:
                plane = post_ref[i, 32 * source : 32 * source + 32, :]
            elif source < 0:
                plane = jnp.where(has_xm, xp_ref[XP.index(i)], 0.0)
            else:
                plane = jnp.where(has_xp, xm_ref[XM.index(i)], 0.0)
            if cy:
                if 0 <= source < 4:
                    face_ref, n = (yp_ref, YP.index(i)) if cy == 1 else (ym_ref, YM.index(i))
                    line = face_ref[4 * n + source : 4 * n + source + 1, :]
                    line = jnp.where(has_ym if cy == 1 else has_yp, line, 0.0)
                else:
                    line = from_xy[cx, cy]
                plane = pltpu.roll(plane, 1 if cy == 1 else 31, 0)
                plane = jnp.where(plane_row == (0 if cy == 1 else 31), line, plane)
            if cz:
                n = order.index(i)
                plane = pltpu.roll(plane, 1 if cz == 1 else 127, 1)
                at = 0 if cz == 1 else 127
                plane = jnp.where(plane_lane == at, columns[rows, n : n + 1], plane)
            if i:
                opposite = i + 1 if i % 2 else i - 1
                plane = jnp.where(code == float(opposite), value, plane)
            moved_ref[i, x] = plane


def body(
    populations,
    solid,
    link_cell,
    link_dir,
    link_store,
    store_body,
    motion,
    inv_mass,
    inv_inertia,
    centre,
    rates,
):
    vmem = pl.BlockSpec(memory_space=pltpu.VMEM)
    smem = pl.BlockSpec(memory_space=pltpu.SMEM)
    links = link_cell.shape[-1]

    def array(*shape):
        return jax.ShapeDtypeStruct(shape, F32)

    params = pltpu.CompilerParams(vmem_limit_bytes=40 * 1024 * 1024)
    post, bounce, send1, xp, xm, yp, ym, xy = pl.pallas_call(
        first_kernel,
        out_shape=(
            array(19, 128, 128),
            array(2, 128, 128),
            array(8, 9, 8, 128),
            array(5, 32, 128),
            array(5, 32, 128),
            array(24, 128),
            array(24, 128),
            array(8, 128),
        ),
        in_specs=[vmem] * 6 + [smem] * 3,
        out_specs=(vmem,) * 8,
        scratch_shapes=[pltpu.VMEM((128, 128), F32), pltpu.VMEM((128, 128), F32)],
        compiler_params=params,
        name="collide",
    )(
        populations.reshape(19, 128, 128),
        solid.reshape(128, 128),
        link_cell.reshape(1, links),
        link_dir.reshape(1, links),
        link_store.reshape(1, links),
        store_body.reshape(256, 128),
        motion,
        centre,
        rates,
    )

    def shift(x, axis, by):
        size = lax.axis_size(axis)
        return lax.ppermute(x, axis, [(i, (i + by) % size) for i in range(size)])

    xp, xm = shift(xp, "gx", 1), shift(xm, "gx", -1)
    yp, ym = shift(yp, "gy", 1), shift(ym, "gy", -1)
    got1 = lax.all_to_all(send1, "gz", 0, 0, tiled=True)
    send2 = pl.pallas_call(
        second_kernel,
        out_shape=array(32, 8, 128),
        in_specs=[vmem] * 2,
        out_specs=vmem,
        scratch_shapes=[pltpu.VMEM((256, 256), F32), pltpu.VMEM((8, 8, 128), F32)],
        compiler_params=params,
        name="bins",
    )(got1, xy)
    got2 = lax.all_to_all(send2, ("gx", "gy"), 0, 0, tiled=True)
    moved, own_loads, motion_next = pl.pallas_call(
        third_kernel,
        out_shape=(array(19, 4, 32, 128), array(6, 128), array(8, 6)),
        in_specs=[vmem] * 9 + [smem] * 2,
        out_specs=(vmem,) * 3,
        compiler_params=params,
        name="move",
    )(post, bounce, got1, got2, xp, xm, yp, ym, motion, inv_mass, inv_inertia)
    return (moved, own_loads, motion_next)


def solution(mesh):
    return jax.shard_map(
        body,
        mesh=mesh,
        in_specs=(
            P(None, "gx", "gy", "gz"),
            P("gx", "gy", "gz"),
            P("gx", "gy", "gz", None),
            P("gx", "gy", "gz", None),
            P("gx", "gy", "gz", None),
            P(),
            P(),
            P(),
            P(),
            P(),
            P(),
        ),
        out_specs=(P(None, "gx", "gy", "gz"), P(None, ("gx", "gy", "gz")), P()),
        check_vma=False,
    )
```

time: 1450 us -> 53.4 us (0.04)
  waiting for transfers between devices: 1270 us -> 4.7 us
  blocking collectives: 78.5 us -> 11.1 us
  other arithmetic: 28 us -> 0 us
  local copies, waits for them, and re-layouts: 33.8 us -> 7.28 us
    reduce_scatter x1 -> x0, waiting for transfers between devices: 1260 us -> none  [body(): lax.psum_scatter(partial_loads, ('gx', 'gy', 'gz'), scatter_dimension=1,...]
    psum x1 -> x0, blocking collectives: 78.5 us -> none  [body(): body_load = lax.psum(body_part, ('gx', 'gy', 'gz'))]
  transfers between devices with their start and end apart: 7 -> 5, of which waited for: 4 -> 3; matrix products, arithmetic and copies ran while one was open for 3% -> 0% of each run, Pallas kernels for 0% -> 0%
where the time goes in v1:
time: 53.4 us; the launch traced here: 52.9 us
  starting transfers between devices  18 us (34%)
  Pallas kernels  11.2 us (21%)
  blocking collectives  11.1 us (21%)
  local copies, waits for them, and re-layouts  7.28 us (14%)
  waiting for transfers between devices  4.7 us (9%)
  between operations  0.66 us (1%)
    all_to_all x1, starting transfers between devices, body(): got2 = lax.all_to_all(send2, ('gx', 'gy'), 0, 0, tiled=True)  11.5 us
    all_to_all x1, blocking collectives, body(): got1 = lax.all_to_all(send1, 'gz', 0, 0, tiled=True)  11.1 us
    unnamed x24, local copies, waits for them, and re-layouts  7.28 us
    ppermute x4, starting transfers between devices, shift(): return lax.ppermute(x, axis, [(i, (i + by) % size) for i in range(size)])  6.55 us
    pallas_call x1, Pallas kernels, body(): pl.pallas_call(second_kernel, out_shape=array(32, 8, 128), in_specs=[vmem...  4.82 us
    pallas_call x1, Pallas kernels, body(): pl.pallas_call(first_kernel, out_shape=(array(19, 128, 128), array(2, 128...  4.06 us
    all_to_all x1, waiting for transfers between devices, body(): got2 = lax.all_to_all(send2, ('gx', 'gy'), 0, 0, tiled=True)  2.53 us
    pallas_call x1, Pallas kernels, body(): pl.pallas_call(third_kernel, out_shape=(array(19, 4, 32, 128), array(6, 1...  2.33 us
  transfers between devices with their start and end apart: 5, of which 3 were waited for; matrix products, arithmetic and copies ran while one was open for 0% of the time, Pallas kernels for 0%

profile of v1, /device:TPU:2, one launch (start us, length us, event | category | flops | bytes accessed | tf_op | source)
XLA Modules:
  0.0 52.9 jit_solution(3140318488313565937)
XLA Ops:
  0.6 0.8 %copy.14.centre_ref = f32[8,3]{1,0:T(8,128)S(1)} copy(f32[8,3]{0,1:T(4,128)} %param.20) | data formatting | bytes 192 | tf_op args[9]
  1.4 0.0 copy-start
  1.4 1.3 %copy-done = f32[19,4,32,128]{3,2,1,0:T(8,128)S(1)} copy-done((f32[19,4,32,128]{3,2,1,0:T(8,128)S(1)}, f32[19,4,32,128]{3,2,1,0:T(8,128)}, u32[]{:S(2)}) %copy-start) | copy-done | bytes 1245208
  2.7 0.0 copy-start.1
  2.7 0.9 %copy-done.1 = s32[32768]{0:T(1024)S(1)} copy-done((s32[32768]{0:T(1024)S(1)}, s32[32768]{0:T(1024)}, u32[]{:S(2)}) %copy-start.1) | copy-done | bytes 131096
  3.6 0.0 copy-start.2
  3.6 0.8 %copy-done.2 = s32[4,32,128]{2,1,0:T(8,128)S(1)} copy-done((s32[4,32,128]{2,1,0:T(8,128)S(1)}, s32[4,32,128]{2,1,0:T(8,128)}, u32[]{:S(2)}) %copy-start.2) | copy-done | bytes 65560
  4.4 0.0 copy-start.3
  4.4 0.7 %copy-done.3 = f32[8,6]{1,0:T(8,128)S(1)} copy-done((f32[8,6]{1,0:T(8,128)S(1)}, f32[8,6]{1,0:T(8,128)}, u32[]{:S(2)}) %copy-start.3) | copy-done | bytes 216
  5.1 0.0 copy-start.5
  5.1 0.7 %copy-done.5 = s32[1,1,1,1024]{3,2,1,0:T(1,128)S(1)} copy-done((s32[1,1,1,1024]{3,2,1,0:T(1,128)S(1)}, s32[1,1,1,1024]{3,2,1,0:T(1,128)}, u32[]{:S(2)}) %copy-start.5) | copy-done | bytes 4120
  5.8 0.7 %copy-done.6 = s32[1,1,1,1024]{3,2,1,0:T(1,128)S(1)} copy-done((s32[1,1,1,1024]{3,2,1,0:T(1,128)S(1)}, s32[1,1,1,1024]{3,2,1,0:T(1,128)}, u32[]{:S(2)}) %copy-start.6) | copy-done | bytes 4120
  6.5 0.7 %copy-done.7 = s32[1,1,1,1024]{3,2,1,0:T(1,128)S(1)} copy-done((s32[1,1,1,1024]{3,2,1,0:T(1,128)S(1)}, s32[1,1,1,1024]{3,2,1,0:T(1,128)}, u32[]{:S(2)}) %copy-start.7) | copy-done | bytes 4120
  7.2 0.7 %copy-done.8 = f32[15]{0:T(128)S(1)} copy-done((f32[15]{0:T(128)S(1)}, f32[15]{0:T(128)}, u32[]{:S(2)}) %copy-start.8) | copy-done | bytes 84
  7.8 4.1 %collide.1 = (f32[19,128,128]{2,1,0:T(8,128)S(1)}, f32[2,128,128]{2,1,0:T(8,128)S(1)}, f32[8,9,8,128]{3,2,1,0:T(8,128)S(1)}, f32[5,32,128]{2,1,0:T(8,128)S(1)}, ...) custom-call(f32[19,128,128]{2,1,0:T(8,128)S(1)} %bitcast.6, ...), custom_call_target="tpu_custom_call" | custom-call | tf_op jit(solution)/shard_map/collide/pallas_call | solution.py:559
  11.9 11.1 %all_to_all.10.got_ref.got1_ref = f32[8,9,8,128]{3,2,1,0:T(8,128)S(1)} all-to-all(f32[8,9,8,128]{3,2,1,0:T(8,128)S(1)} %get-tuple-element.13), channel_id=1, replica_groups=mesh['gx'=8,'gy'=4,'gz'=8] {'gz'}, dimensions={0} | all-to-all | bytes 589824 | tf_op jit(solution)/shard_map/all_to_all | solution.py:594
  23.0 4.8 %bins.1 = f32[32,8,128]{2,1,0:T(8,128)} custom-call(f32[8,9,8,128]{3,2,1,0:T(8,128)S(1)} %all_to_all.10.got_ref.got1_ref, f32[8,128]{1,0:T(8,128)S(1)} %get-tuple-element.14.xy_ref), custom_call_target="tpu_custom_call" | custom-call | tf_op jit(solution)/shard_map/bins/pallas_call | solution.py:595
  27.8 11.5 %all-to-all-start.1 = ((f32[32,8,128]{2,1,0:T(8,128)}), f32[32,8,128]{2,1,0:T(8,128)S(1)}, u32[]{:S(2)}, u32[]{:S(2)}) async-start(f32[32,8,128]{2,1,0:T(8,128)} %bins.1), calls=%async_computation.1 | async-start | bytes 262144 | tf_op jit(solution)/shard_map/all_to_all | solution.py:604
  39.3 1.9 %collective-permute-start = (f32[5,32,128]{2,1,0:T(8,128)S(1)}, f32[5,32,128]{2,1,0:T(8,128)S(1)}, u32[]{:S(2)}, u32[]{:S(2)}) collective-permute-start(f32[5,32,128]{2,1,0:T(8,128)S(1)} %get-tuple-element.15), channel_id=1, source_target_pairs={{0,32},{32,64},{64,96},{96,128},{128,160},{160,192},{192,224},{224... | collective-permute-start | bytes 245768 | tf_op jit(solution)/shard_map/ppermute | solution.py:590
  41.1 1.4 %collective-permute-start.1 = (f32[5,32,128]{2,1,0:T(8,128)S(1)}, f32[5,32,128]{2,1,0:T(8,128)S(1)}, u32[]{:S(2)}, u32[]{:S(2)}) collective-permute-start(f32[5,32,128]{2,1,0:T(8,128)S(1)} %get-tuple-element.16), channel_id=1, source_target_pairs={{0,224},{32,0},{64,32},{96,64},{128,96},{160,128},{192,160},{224,1... | collective-permute-start | bytes 245768 | tf_op jit(solution)/shard_map/ppermute | solution.py:590
  42.6 1.8 %collective-permute-start.2 = (f32[24,128]{1,0:T(8,128)S(1)}, f32[24,128]{1,0:T(8,128)S(1)}, u32[]{:S(2)}, u32[]{:S(2)}) collective-permute-start(f32[24,128]{1,0:T(8,128)S(1)} %get-tuple-element.17), channel_id=1, source_target_pairs={{0,8},{8,16},{16,24},{24,0},{1,9},{9,17},{17,25},{25,1},{2,10},{10... | collective-permute-start | bytes 36872 | tf_op jit(solution)/shard_map/ppermute | solution.py:590
  44.4 1.4 %collective-permute-start.3 = (f32[24,128]{1,0:T(8,128)S(1)}, f32[24,128]{1,0:T(8,128)S(1)}, u32[]{:S(2)}, u32[]{:S(2)}) collective-permute-start(f32[24,128]{1,0:T(8,128)S(1)} %get-tuple-element.18), channel_id=1, source_target_pairs={{0,24},{8,0},{16,8},{24,16},{1,25},{9,1},{17,9},{25,17},{2,26},{10... | collective-permute-start | bytes 36872 | tf_op jit(solution)/shard_map/ppermute | solution.py:590
  45.8 0.0 copy-done.10
  45.8 0.1 copy.15.inertia_ref
  45.9 1.7 %collective-permute-done.2.yp_ref = f32[24,128]{1,0:T(8,128)S(1)} collective-permute-done((f32[24,128]{1,0:T(8,128)S(1)}, f32[24,128]{1,0:T(8,128)S(1)}, u32[]{:S(2)}, u32[]{:S(2)}) %collective-permute-start.2) | collective-permute-done | bytes 12320 | tf_op jit(solution)/shard_map/ppermute | solution.py:590
  47.6 0.4 collective-permute-done.3.ym_ref
  48.1 0.0 collective-permute-done.xp_ref
  48.1 0.0 collective-permute-done.1.xm_ref
  48.1 2.5 %all-to-all-done.1.got2_ref = f32[32,8,128]{2,1,0:T(8,128)S(1)} async-done(((f32[32,8,128]{2,1,0:T(8,128)}), f32[32,8,128]{2,1,0:T(8,128)S(1)}, u32[]{:S(2)}, u32[]{:S(2)}) %all-to-all-start.1) | async-done | bytes 131104 | tf_op jit(solution)/shard_map/all_to_all | solution.py:604
  50.6 0.0 copy-done.4
  50.6 0.0 copy-done.9
  50.6 2.3 %move.1 = (f32[19,4,32,128]{3,2,1,0:T(8,128)}, f32[6,128]{1,0:T(8,128)}, f32[8,6]{1,0:T(8,128)}) custom-call(f32[19,128,128]{2,1,0:T(8,128)S(1)} %get-tuple-element.11.post_ref, f32[2,128,128]{2,1,0:T(8,128)S(1)} %get-tuple-element.12.bounce_ref, f32[8,9,8,128]{3,2,1,0:T(8,128)S(1)} %all_to_all.10.got_ref.got1_ref, ...), custom_call_target="tpu_custom_call" | custom-call | tf_op jit(solution)/shard_map/move/pallas_call | solution.py:605
  (6 shorter events, 0.0 us)
Async XLA Ops:
  1.4 1.3 %copy-start = (f32[19,4,32,128]{3,2,1,0:T(8,128)S(1)}, f32[19,4,32,128]{3,2,1,0:T(8,128)}, u32[]{:S(2)}) copy-start(f32[19,4,32,128]{3,2,1,0:T(8,128)} %param.11) | copy-start | bytes 3735556
  2.7 0.9 %copy-start.1 = (s32[32768]{0:T(1024)S(1)}, s32[32768]{0:T(1024)}, u32[]{:S(2)}) copy-start(s32[32768]{0:T(1024)} %param.16) | copy-start | bytes 393220
  3.6 0.8 %copy-start.2 = (s32[4,32,128]{2,1,0:T(8,128)S(1)}, s32[4,32,128]{2,1,0:T(8,128)}, u32[]{:S(2)}) copy-start(s32[4,32,128]{2,1,0:T(8,128)} %param.12) | copy-start | bytes 196612
  4.4 0.7 %copy-start.3 = (f32[8,6]{1,0:T(8,128)S(1)}, f32[8,6]{1,0:T(8,128)}, u32[]{:S(2)}) copy-start(f32[8,6]{1,0:T(8,128)} %motion_ref.3) | copy-start | bytes 580
  5.1 0.7 %copy-start.5 = (s32[1,1,1,1024]{3,2,1,0:T(1,128)S(1)}, s32[1,1,1,1024]{3,2,1,0:T(1,128)}, u32[]{:S(2)}) copy-start(s32[1,1,1,1024]{3,2,1,0:T(1,128)} %param.13) | copy-start | bytes 12292
  5.8 0.7 %copy-start.6 = (s32[1,1,1,1024]{3,2,1,0:T(1,128)S(1)}, s32[1,1,1,1024]{3,2,1,0:T(1,128)}, u32[]{:S(2)}) copy-start(s32[1,1,1,1024]{3,2,1,0:T(1,128)} %param.14) | copy-start | bytes 12292
  6.5 0.7 %copy-start.7 = (s32[1,1,1,1024]{3,2,1,0:T(1,128)S(1)}, s32[1,1,1,1024]{3,2,1,0:T(1,128)}, u32[]{:S(2)}) copy-start(s32[1,1,1,1024]{3,2,1,0:T(1,128)} %param.15) | copy-start | bytes 12292
  7.2 0.7 %copy-start.8 = (f32[15]{0:T(128)S(1)}, f32[15]{0:T(128)}, u32[]{:S(2)}) copy-start(f32[15]{0:T(128)} %rates_ref.1) | copy-start | bytes 184
  7.8 38.0 %copy-start.10 = (f32[8,3]{0,1:T(4,128)S(1)}, f32[8,3]{0,1:T(4,128)}, u32[]{:S(2)}) copy-start(f32[8,3]{0,1:T(4,128)} %param.19) | copy-start | bytes 292
  7.8 42.8 %copy-start.4 = (f32[8,6]{1,0:T(8,128)S(1)}, f32[8,6]{1,0:T(8,128)}, u32[]{:S(2)}) copy-start(f32[8,6]{1,0:T(8,128)} %motion_ref.3) | copy-start | bytes 580
  7.8 42.8 %copy-start.9 = (f32[8]{0:T(128)S(1)}, f32[8]{0:T(128)}, u32[]{:S(2)}) copy-start(f32[8]{0:T(128)} %mass_ref.1) | copy-start | bytes 100
  27.8 22.8 %all-to-all-start.1 = ((f32[32,8,128]{2,1,0:T(8,128)}), f32[32,8,128]{2,1,0:T(8,128)S(1)}, u32[]{:S(2)}, u32[]{:S(2)}) async-start(f32[32,8,128]{2,1,0:T(8,128)} %bins.1), calls=%async_computation.1 | async-start | bytes 262144 | tf_op jit(solution)/shard_map/all_to_all | solution.py:604
  39.3 8.8 %collective-permute-start = (f32[5,32,128]{2,1,0:T(8,128)S(1)}, f32[5,32,128]{2,1,0:T(8,128)S(1)}, u32[]{:S(2)}, u32[]{:S(2)}) collective-permute-start(f32[5,32,128]{2,1,0:T(8,128)S(1)} %get-tuple-element.15), channel_id=1, source_target_pairs={{0,32},{32,64},{64,96},{96,128},{128,160},{160,192},{192,224},{224... | collective-permute-start | bytes 245768 | tf_op jit(solution)/shard_map/ppermute | solution.py:590
  41.1 6.9 %collective-permute-start.1 = (f32[5,32,128]{2,1,0:T(8,128)S(1)}, f32[5,32,128]{2,1,0:T(8,128)S(1)}, u32[]{:S(2)}, u32[]{:S(2)}) collective-permute-start(f32[5,32,128]{2,1,0:T(8,128)S(1)} %get-tuple-element.16), channel_id=1, source_target_pairs={{0,224},{32,0},{64,32},{96,64},{128,96},{160,128},{192,160},{224,1... | collective-permute-start | bytes 245768 | tf_op jit(solution)/shard_map/ppermute | solution.py:590
  42.6 5.0 %collective-permute-start.2 = (f32[24,128]{1,0:T(8,128)S(1)}, f32[24,128]{1,0:T(8,128)S(1)}, u32[]{:S(2)}, u32[]{:S(2)}) collective-permute-start(f32[24,128]{1,0:T(8,128)S(1)} %get-tuple-element.17), channel_id=1, source_target_pairs={{0,8},{8,16},{16,24},{24,0},{1,9},{9,17},{17,25},{25,1},{2,10},{10... | collective-permute-start | bytes 36872 | tf_op jit(solution)/shard_map/ppermute | solution.py:590
  44.4 3.7 %collective-permute-start.3 = (f32[24,128]{1,0:T(8,128)S(1)}, f32[24,128]{1,0:T(8,128)S(1)}, u32[]{:S(2)}, u32[]{:S(2)}) collective-permute-start(f32[24,128]{1,0:T(8,128)S(1)} %get-tuple-element.18), channel_id=1, source_target_pairs={{0,24},{8,0},{16,8},{24,16},{1,25},{9,1},{17,9},{25,17},{2,26},{10... | collective-permute-start | bytes 36872 | tf_op jit(solution)/shard_map/ppermute | solution.py:590

commit v2 on v1

--- a/solution.py
+++ b/solution.py
@@ -208,6 +208,23 @@
 
 
 def first_kernel(
+    pop_hbm,
+    solid_hbm,
+    cell_hbm,
+    dir_hbm,
+    store_hbm,
+    owner_hbm,
+    motion_hbm,
+    centre_hbm,
+    rates_hbm,
+    post_ref,
+    bounce_ref,
+    send_ref,
+    xp_ref,
+    xm_ref,
+    yp_ref,
+    ym_ref,
+    xy_ref,
     pop_ref,
     solid_ref,
     cell_ref,
@@ -217,17 +234,35 @@
     motion_ref,
     centre_ref,
     rates_ref,
-    post_ref,
-    bounce_ref,
-    send_ref,
-    xp_ref,
-    xm_ref,
-    yp_ref,
-    ym_ref,
-    xy_ref,
     picked_ref,
     column_ref,
+    pop_sem,
+    sems,
 ):
+    small = (
+        (cell_hbm, cell_ref),
+        (dir_hbm, dir_ref),
+        (store_hbm, store_ref),
+        (owner_hbm, owner_ref),
+        (motion_hbm, motion_ref),
+        (centre_hbm, centre_ref),
+        (rates_hbm, rates_ref),
+        (solid_hbm, solid_ref),
+    )
+    copies = [pltpu.make_async_copy(a, b, sems.at[n]) for n, (a, b) in enumerate(small)]
+
+    def plane(x):
+        rows = pl.ds(x * 32, 32)
+        return pltpu.make_async_copy(
+            pop_hbm.at[:, rows, :], pop_ref.at[:, rows, :], pop_sem.at[x]
+        )
+
+    for copy in copies:
+        copy.start()
+    for x in range(4):
+        plane(x).start()
+    for copy in copies:
+        copy.wait()
     speeds, weights, _ = lattice_tables()
     links = cell_ref.shape[1]
     place_x, place_y, place_z = (lax.axis_index(a) for a in ("gx", "gy", "gz"))
@@ -255,7 +290,7 @@
     weight = jnp.where(direction <= 6, float(weights[1]), float(weights[7]))
     is_body = [body == float(b) for b in range(8)]
     move = [pick(is_body, [motion_ref[b, c] for b in range(8)], shape) for c in range(6)]
-    middle = [pick(is_body, [centre_ref[b, a] for b in range(8)], shape) for a in range(3)]
+    middle = [pick(is_body, [centre_ref[a, b] for b in range(8)], shape) for a in range(3)]
     place = (
         lax.shift_right_logical(cell, 12) + place_x * 4,
         (row & 31) + place_y * 32,
@@ -292,6 +327,10 @@
     at_lane = iota((8, 128), 1)
 
     def block(step, carry):
+        @pl.when((step & 3) == 0)
+        def _():
+            plane(lax.shift_right_logical(step, 2)).wait()
+
         rows = pl.ds(pl.multiple_of(step * 8, 8), 8)
         f = [pop_ref[i, rows, :] for i in range(19)]
         post = collide(f, k)
@@ -363,8 +402,19 @@
         low = ((lax.shift_right_logical(owner, 3) & 1) * 128) + (store & 127)
         both = jnp.concatenate(halves(loads), axis=0)
         none = jnp.zeros_like(both)
-        spread = jnp.concatenate([jnp.where(high == h, both, none) for h in range(16)], axis=0)
-        low_hot = (iota((256, links), 0) == low).astype(F32).astype(BF16)
+        high = jnp.broadcast_to(high.astype(F32), (16, links)).astype(BF16)
+        spread = jnp.concatenate(
+            [jnp.where(high == jnp.bfloat16(h), both, none) for h in range(16)], axis=0
+        )
+        low = jnp.broadcast_to(low.astype(F32), (16, links)).astype(BF16)
+        one = jnp.ones((16, links), BF16)
+        low_hot = jnp.concatenate(
+            [
+                jnp.where(low == (iota((16, links), 0) + 16 * g).astype(F32).astype(BF16), one, none)
+                for g in range(16)
+            ],
+            axis=0,
+        )
         total_ref[...] += rows_dot(spread, low_hot)
         for b in range(8):
             part = jnp.where(body == float(b), loads, 0.0)
@@ -455,7 +505,7 @@
         )
         body_load = jnp.where(at_lane == c, column, body_load)
         for b in range(8):
-            value = mass_ref[b] if c < 3 else inertia_ref[b, c - 3]
+            value = mass_ref[b] if c < 3 else inertia_ref[c - 3, b]
             scale = jnp.where((at_lane == c) & (at_row == b), value, scale)
     next_ref[...] = motion_ref[...] + (scale * body_load)[:, 0:6] / 32768.0
 
@@ -568,30 +618,53 @@
             array(24, 128),
             array(8, 128),
         ),
-        in_specs=[vmem] * 6 + [smem] * 3,
+        in_specs=[pl.BlockSpec(memory_space=pltpu.HBM)] * 9,
         out_specs=(vmem,) * 8,
-        scratch_shapes=[pltpu.VMEM((128, 128), F32), pltpu.VMEM((128, 128), F32)],
+        scratch_shapes=[
+            pltpu.VMEM((19, 128, 128), F32),
+            pltpu.VMEM((128, 128), I32),
+            pltpu.VMEM((1, links), I32),
+            pltpu.VMEM((1, links), I32),
+            pltpu.VMEM((1, links), I32),
+            pltpu.VMEM((256, 128), I32),
+            pltpu.SMEM((8, 6), F32),
+            pltpu.SMEM((3, 8), F32),
+            pltpu.SMEM((15,), F32),
+            pltpu.VMEM((128, 128), F32),
+            pltpu.VMEM((128, 128), F32),
+            pltpu.SemaphoreType.DMA((4,)),
+            pltpu.SemaphoreType.DMA((8,)),
+        ],
         compiler_params=params,
         name="collide",
     )(
-        populations.reshape(19, 128, 128),
-        solid.reshape(128, 128),
-        link_cell.reshape(1, links),
-        link_dir.reshape(1, links),
-        link_store.reshape(1, links),
-        store_body.reshape(256, 128),
-        motion,
-        centre,
-        rates,
+        *(
+            pltpu.with_memory_space_constraint(x, pltpu.HBM)
+            for x in (
+                populations.reshape(19, 128, 128),
+                solid.reshape(128, 128),
+                link_cell.reshape(1, links),
+                link_dir.reshape(1, links),
+                link_store.reshape(1, links),
+                store_body.reshape(256, 128),
+                motion,
+                centre.T,
+                rates,
+            )
+        )
     )
 
     def shift(x, axis, by):
         size = lax.axis_size(axis)
         return lax.ppermute(x, axis, [(i, (i + by) % size) for i in range(size)])
 
-    xp, xm = shift(xp, "gx", 1), shift(xm, "gx", -1)
-    yp, ym = shift(yp, "gy", 1), shift(ym, "gy", -1)
+    after = lax.optimization_barrier
+    xp = shift(xp, "gx", 1)
+    yp = shift(yp, "gy", 1)
     got1 = lax.all_to_all(send1, "gz", 0, 0, tiled=True)
+    xm, ym, got1 = after((xm, ym, got1))
+    xm = shift(xm, "gx", -1)
+    ym = shift(ym, "gy", -1)
     send2 = pl.pallas_call(
         second_kernel,
         out_shape=array(32, 8, 128),
@@ -599,8 +672,12 @@
         out_specs=vmem,
         scratch_shapes=[pltpu.VMEM((256, 256), F32), pltpu.VMEM((8, 8, 128), F32)],
         compiler_params=params,
+        cost_estimate=pl.CostEstimate(
+            flops=2 * 256 * 256 * 8192, bytes_accessed=4 * 8 * 8192, transcendentals=0
+        ),
         name="bins",
     )(got1, xy)
+    send2, xp, xm, yp, ym = after((send2, xp, xm, yp, ym))
     got2 = lax.all_to_all(send2, ("gx", "gy"), 0, 0, tiled=True)
     moved, own_loads, motion_next = pl.pallas_call(
         third_kernel,
@@ -609,7 +686,7 @@
         out_specs=(vmem,) * 3,
         compiler_params=params,
         name="move",
-    )(post, bounce, got1, got2, xp, xm, yp, ym, motion, inv_mass, inv_inertia)
+    )(post, bounce, got1, got2, xp, xm, yp, ym, motion, inv_mass, inv_inertia.T)
     return (moved, own_loads, motion_next)
 
 

time: 53.4 us -> 46.8 us (0.88)
  local copies, waits for them, and re-layouts: 7.28 us -> 0.01 us
  blocking collectives: 11.1 us -> 14.9 us
  starting transfers between devices: 18 us -> 16.4 us
  waiting for transfers between devices: 4.7 us -> 3.75 us
    unnamed x24 -> x6, local copies, waits for them, and re-layouts: 7.28 us -> 0.01 us
    all_to_all x1, starting transfers between devices: 11.5 us -> 5.61 us  [body(): got1 = lax.all_to_all(send1, 'gz', 0, 0, tiled=True)]
    ppermute x4, starting transfers between devices: 6.55 us -> 10.8 us  [shift(): return lax.ppermute(x, axis, [(i, (i + by) % size) for i in range(size)])]
    all_to_all x1, blocking collectives: 11.1 us -> 14.9 us  [body(): got2 = lax.all_to_all(send2, ('gx', 'gy'), 0, 0, tiled=True)]
    ppermute x4, waiting for transfers between devices: 2.17 us -> 0.01 us  [shift(): return lax.ppermute(x, axis, [(i, (i + by) % size) for i in range(size)])]
    pallas_call x1, Pallas kernels: 4.82 us -> 2.99 us  [body(): pl.pallas_call(second_kernel, out_shape=array(32, 8, 128), in_specs=[vmem...]
    pallas_call x1, Pallas kernels: 4.06 us -> 5.47 us  [body(): pl.pallas_call(first_kernel, out_shape=(array(19, 128, 128), array(2, 128...]
    all_to_all x1, waiting for transfers between devices: 2.53 us -> 3.74 us  [body(): got1 = lax.all_to_all(send1, 'gz', 0, 0, tiled=True)]
  transfers between devices with their start and end apart: 5 -> 5, of which waited for: 3 -> 1; matrix products, arithmetic and copies ran while one was open for 0% -> 0% of each run, Pallas kernels for 0% -> 6%
where the time goes in v2:
time: 46.8 us; the launch traced here: 46.5 us
  starting transfers between devices  16.4 us (35%)
  blocking collectives  14.9 us (32%)
  Pallas kernels  10.8 us (23%)
  waiting for transfers between devices  3.75 us (8%)
  between operations  0.69 us (1%)
    all_to_all x1, blocking collectives, body(): got2 = lax.all_to_all(send2, ('gx', 'gy'), 0, 0, tiled=True)  14.9 us
    ppermute x4, starting transfers between devices, shift(): return lax.ppermute(x, axis, [(i, (i + by) % size) for i in range(size)])  10.8 us
    all_to_all x1, starting transfers between devices, body(): got1 = lax.all_to_all(send1, 'gz', 0, 0, tiled=True)  5.61 us
    pallas_call x1, Pallas kernels, body(): pl.pallas_call(first_kernel, out_shape=(array(19, 128, 128), array(2, 128...  5.47 us
    all_to_all x1, waiting for transfers between devices, body(): got1 = lax.all_to_all(send1, 'gz', 0, 0, tiled=True)  3.74 us
    pallas_call x1, Pallas kernels, body(): pl.pallas_call(second_kernel, out_shape=array(32, 8, 128), in_specs=[vmem...  2.99 us
    pallas_call x1, Pallas kernels, body(): pl.pallas_call(third_kernel, out_shape=(array(19, 4, 32, 128), array(6, 1...  2.3 us
  transfers between devices with their start and end apart: 5, of which 1 were waited for; matrix products, arithmetic and copies ran while one was open for 0% of the time, Pallas kernels for 6%

profile of v2, /device:TPU:2, one launch (start us, length us, event | category | flops | bytes accessed | tf_op | source)
XLA Modules:
  0.0 46.5 jit_solution(71076881787603143)
XLA Ops:
  0.6 5.5 %collide.1 = (f32[19,128,128]{2,1,0:T(8,128)S(1)}, f32[2,128,128]{2,1,0:T(8,128)S(1)}, f32[8,9,8,128]{3,2,1,0:T(8,128)}, f32[5,32,128]{2,1,0:T(8,128)S(1)}, f32[...) custom-call(f32[19,128,128]{2,1,0:T(8,128)} %bitcast.9, ...), custom_call_target="tpu_custom_call" | custom-call | tf_op jit(solution)/shard_map/collide/pallas_call | solution.py:609
  6.1 5.6 %all-to-all-start = ((f32[8,9,8,128]{3,2,1,0:T(8,128)}), f32[8,9,8,128]{3,2,1,0:T(8,128)S(1)}, u32[]{:S(2)}, u32[]{:S(2)}) async-start(f32[8,9,8,128]{3,2,1,0:T(8,128)} %get-tuple-element.23), calls=%async_computation | async-start | bytes 589824 | tf_op jit(solution)/shard_map/all_to_all | solution.py:664
  11.7 0.8 %collective-permute-start.2 = (f32[24,128]{1,0:T(8,128)S(1)}, f32[24,128]{1,0:T(8,128)S(1)}, u32[]{:S(2)}, u32[]{:S(2)}) collective-permute-start(f32[24,128]{1,0:T(8,128)S(1)} %get-tuple-element.28), channel_id=1, source_target_pairs={{0,8},{8,16},{16,24},{24,0},{1,9},{9,17},{17,25},{25,1},{2,10},{10... | collective-permute-start | bytes 36872 | tf_op jit(solution)/shard_map/ppermute | solution.py:659
  12.5 1.9 %collective-permute-start = (f32[5,32,128]{2,1,0:T(8,128)S(1)}, f32[5,32,128]{2,1,0:T(8,128)S(1)}, u32[]{:S(2)}, u32[]{:S(2)}) collective-permute-start(f32[5,32,128]{2,1,0:T(8,128)S(1)} %get-tuple-element.26), channel_id=1, source_target_pairs={{0,32},{32,64},{64,96},{96,128},{128,160},{160,192},{192,224},{224... | collective-permute-start | bytes 245768 | tf_op jit(solution)/shard_map/ppermute | solution.py:659
  14.4 3.7 %all-to-all-done.got_ref.got1_ref = f32[8,9,8,128]{3,2,1,0:T(8,128)S(1)} async-done(((f32[8,9,8,128]{3,2,1,0:T(8,128)}), f32[8,9,8,128]{3,2,1,0:T(8,128)S(1)}, u32[]{:S(2)}, u32[]{:S(2)}) %all-to-all-start) | async-done | bytes 294944 | tf_op jit(solution)/shard_map/all_to_all | solution.py:664
  18.2 2.2 %collective-permute-start.3 = (f32[24,128]{1,0:T(8,128)S(1)}, f32[24,128]{1,0:T(8,128)S(1)}, u32[]{:S(2)}, u32[]{:S(2)}) collective-permute-start(f32[24,128]{1,0:T(8,128)S(1)} %get-tuple-element.29), channel_id=1, source_target_pairs={{0,24},{8,0},{16,8},{24,16},{1,25},{9,1},{17,9},{25,17},{2,26},{10... | collective-permute-start | bytes 36872 | tf_op jit(solution)/shard_map/ppermute | solution.py:659
  20.4 5.9 %collective-permute-start.1 = (f32[5,32,128]{2,1,0:T(8,128)S(1)}, f32[5,32,128]{2,1,0:T(8,128)S(1)}, u32[]{:S(2)}, u32[]{:S(2)}) collective-permute-start(f32[5,32,128]{2,1,0:T(8,128)S(1)} %get-tuple-element.27), channel_id=1, source_target_pairs={{0,224},{32,0},{64,32},{96,64},{128,96},{160,128},{192,160},{224,1... | collective-permute-start | bytes 245768 | tf_op jit(solution)/shard_map/ppermute | solution.py:659
  26.3 0.0 copy-start
  26.3 0.0 copy-start.1
  26.3 0.0 copy-start.2
  26.3 3.0 %bins.1 = f32[32,8,128]{2,1,0:T(8,128)S(1)} custom-call(f32[8,9,8,128]{3,2,1,0:T(8,128)S(1)} %all-to-all-done.got_ref.got1_ref, f32[8,128]{1,0:T(8,128)S(1)} %get-tuple-element.25.xy_ref), custom_call_target="tpu_custom_call" | custom-call | flops 1073741824 | bytes 262144 | tf_op jit(solution)/shard_map/bins/pallas_call | solution.py:668
  29.3 0.0 collective-permute-done.2.yp_ref
  29.3 0.0 collective-permute-done.xp_ref
  29.3 0.0 collective-permute-done.3.ym_ref
  29.3 0.0 collective-permute-done.1.xm_ref
  29.3 14.9 %all_to_all.10.got2_ref = f32[32,8,128]{2,1,0:T(8,128)S(1)} all-to-all(f32[32,8,128]{2,1,0:T(8,128)S(1)} %bins.1), channel_id=1, replica_groups=mesh['gx'=8,'gy'=4,'gz'=8] {'gx','gy'}, dimensions={0} | all-to-all | bytes 262144 | tf_op jit(solution)/shard_map/all_to_all | solution.py:681
  44.2 0.0 copy-done
  44.2 0.0 copy-done.1
  44.2 0.0 copy-done.2
  44.2 2.3 %move.1 = (f32[19,4,32,128]{3,2,1,0:T(8,128)}, f32[6,128]{1,0:T(8,128)}, f32[8,6]{1,0:T(8,128)}) custom-call(f32[19,128,128]{2,1,0:T(8,128)S(1)} %get-tuple-element.19.post_ref, f32[2,128,128]{2,1,0:T(8,128)S(1)} %get-tuple-element.20.bounce_ref, f32[8,9,8,128]{3,2,1,0:T(8,128)S(1)} %all-to-all-done.got_ref.got1_ref, f32[32,8,128]{2,1,0:T(8,128)S(1)} %all_to_all.10.got2_ref, ...), custom_call_target="tpu_custom_call" | custom-call | tf_op jit(solution)/shard_map/move/pallas_call | solution.py:682
Async XLA Ops:
  6.1 12.1 %all-to-all-start = ((f32[8,9,8,128]{3,2,1,0:T(8,128)}), f32[8,9,8,128]{3,2,1,0:T(8,128)S(1)}, u32[]{:S(2)}, u32[]{:S(2)}) async-start(f32[8,9,8,128]{3,2,1,0:T(8,128)} %get-tuple-element.23), calls=%async_computation | async-start | bytes 589824 | tf_op jit(solution)/shard_map/all_to_all | solution.py:664
  11.7 17.5 %collective-permute-start.2 = (f32[24,128]{1,0:T(8,128)S(1)}, f32[24,128]{1,0:T(8,128)S(1)}, u32[]{:S(2)}, u32[]{:S(2)}) collective-permute-start(f32[24,128]{1,0:T(8,128)S(1)} %get-tuple-element.28), channel_id=1, source_target_pairs={{0,8},{8,16},{16,24},{24,0},{1,9},{9,17},{17,25},{25,1},{2,10},{10... | collective-permute-start | bytes 36872 | tf_op jit(solution)/shard_map/ppermute | solution.py:659
  12.5 16.7 %collective-permute-start = (f32[5,32,128]{2,1,0:T(8,128)S(1)}, f32[5,32,128]{2,1,0:T(8,128)S(1)}, u32[]{:S(2)}, u32[]{:S(2)}) collective-permute-start(f32[5,32,128]{2,1,0:T(8,128)S(1)} %get-tuple-element.26), channel_id=1, source_target_pairs={{0,32},{32,64},{64,96},{96,128},{128,160},{160,192},{192,224},{224... | collective-permute-start | bytes 245768 | tf_op jit(solution)/shard_map/ppermute | solution.py:659
  18.2 11.1 %collective-permute-start.3 = (f32[24,128]{1,0:T(8,128)S(1)}, f32[24,128]{1,0:T(8,128)S(1)}, u32[]{:S(2)}, u32[]{:S(2)}) collective-permute-start(f32[24,128]{1,0:T(8,128)S(1)} %get-tuple-element.29), channel_id=1, source_target_pairs={{0,24},{8,0},{16,8},{24,16},{1,25},{9,1},{17,9},{25,17},{2,26},{10... | collective-permute-start | bytes 36872 | tf_op jit(solution)/shard_map/ppermute | solution.py:659
  20.4 8.9 %collective-permute-start.1 = (f32[5,32,128]{2,1,0:T(8,128)S(1)}, f32[5,32,128]{2,1,0:T(8,128)S(1)}, u32[]{:S(2)}, u32[]{:S(2)}) collective-permute-start(f32[5,32,128]{2,1,0:T(8,128)S(1)} %get-tuple-element.27), channel_id=1, source_target_pairs={{0,224},{32,0},{64,32},{96,64},{128,96},{160,128},{192,160},{224,1... | collective-permute-start | bytes 245768 | tf_op jit(solution)/shard_map/ppermute | solution.py:659
  26.3 17.9 %copy-start = (f32[8,6]{1,0:T(8,128)S(1)}, f32[8,6]{1,0:T(8,128)}, u32[]{:S(2)}) copy-start(f32[8,6]{1,0:T(8,128)} %motion_ref.1) | copy-start | bytes 580
  26.3 17.9 %copy-start.1 = (f32[8,3]{0,1:T(4,128)S(1)}, f32[8,3]{0,1:T(4,128)}, u32[]{:S(2)}) copy-start(f32[8,3]{0,1:T(4,128)} %param.19) | copy-start | bytes 292
  26.3 17.9 %copy-start.2 = (f32[8]{0:T(128)S(1)}, f32[8]{0:T(128)}, u32[]{:S(2)}) copy-start(f32[8]{0:T(128)} %mass_ref.1) | copy-start | bytes 100

commit v3 on v2

--- a/solution.py
+++ b/solution.py
@@ -235,7 +235,6 @@
     centre_ref,
     rates_ref,
     picked_ref,
-    column_ref,
     pop_sem,
     sems,
 ):
@@ -272,12 +271,23 @@
     live = store < 32768
     row = lax.shift_right_logical(cell, 7)
     lane = cell & 127
-    rows_hot = (iota((128, links), 0) == row).astype(F32)
-    lanes_hot = (iota((128, links), 0) == lane).astype(F32)
-    rows_hot16 = rows_hot.astype(BF16)
-    lanes_hot16 = lanes_hot.astype(BF16)
+    one = jnp.ones((16, links), BF16)
+    none = jnp.zeros((16, links), BF16)
+
+    def groups(index, value):
+        index = jnp.broadcast_to(index.astype(F32), (16, links)).astype(BF16)
+        return [
+            jnp.where(index == (iota((16, links), 0) + 16 * g).astype(F32).astype(BF16), value, none)
+            for g in range(8)
+        ]
+
+    def hot(index):
+        return jnp.concatenate(groups(index, one), axis=0)
+
+    rows_hot16 = hot(row)
+    lanes_hot16 = hot(lane)
     store_high = lax.shift_right_logical(store, 7)
-    low_hot = (iota((128, links), 0) == (store & 127)).astype(F32).astype(BF16)
+    low_hot = hot(store & 127)
     by_high = jnp.dot(
         owner_ref[...].astype(F32).astype(BF16), low_hot, preferred_element_type=F32
     )
@@ -309,22 +319,14 @@
     wall = 6.0 * weight * normal
     coded = jnp.where(live, direction, 0).astype(F32)
     wall_high, wall_low = halves(wall)
-    laid = rows_dot(
-        rows_hot16,
-        jnp.concatenate(
-            [
-                (lanes_hot * coded).astype(BF16),
-                lanes_hot16 * wall_high,
-                lanes_hot16 * wall_low,
-            ],
-            axis=0,
-        ),
-    )
+    spread = []
+    for value in (coded.astype(BF16), wall_high, wall_low):
+        spread += groups(lane, jnp.broadcast_to(value.astype(F32), (16, links)).astype(BF16))
+    laid = rows_dot(rows_hot16, jnp.concatenate(spread, axis=0))
     bounce_ref[0] = laid[:, 0:128]
     bounce_ref[1] = laid[:, 128:256] + laid[:, 256:384]
 
     k = collision_scalars(lambda i: rates_ref[i])
-    at_lane = iota((8, 128), 1)
 
     def block(step, carry):
         @pl.when((step & 3) == 0)
@@ -344,16 +346,16 @@
                 found = jnp.where(code == float(i), post[i], found)
         picked_ref[rows, :] = found
         bounce_ref[1, rows, :] = found - bounce_ref[1, rows, :]
-        column = jnp.zeros((8, 128), F32)
-        for n in range(5):
-            column = jnp.where(at_lane == n, pltpu.roll(post[ZP[n]], n + 1, 1), column)
-            turned = pltpu.roll(post[ZM[n]], 8 + n, 1)
-            column = jnp.where(at_lane == 8 + n, turned, column)
-        column_ref[rows, :] = column
         return carry
 
-    lax.fori_loop(0, 16, block, 0)
-
+    lax.fori_loop(0, 16, block, 0, unroll=2)
+
+    at_lane = iota((128, 128), 1)
+    column = jnp.zeros((128, 128), F32)
+    for n in range(5):
+        column = jnp.where(at_lane == n, pltpu.roll(post_ref[ZP[n]], n + 1, 1), column)
+        column = jnp.where(at_lane == 8 + n, pltpu.roll(post_ref[ZM[n]], 8 + n, 1), column)
+    columns = jnp.transpose(column)
     for n in range(5):
         xp_ref[n] = post_ref[XP[n], 96:128, :]
         xm_ref[n] = post_ref[XM[n], 0:32, :]
@@ -372,12 +374,12 @@
     by_row = jnp.dot(
         jnp.concatenate([found_high, found_low], axis=0), lanes_hot16, preferred_element_type=F32
     )
-    picked = jnp.sum((by_row[0:128] + by_row[128:256]) * rows_hot, axis=0, keepdims=True)
+    by_row = jnp.where(iota((128, links), 0) == row, by_row[0:128] + by_row[128:256], 0.0)
+    picked = jnp.sum(by_row, axis=0, keepdims=True)
     strength = jnp.where(live, 2.0 * picked - wall, 0.0)
     push = [speed[a] * strength for a in range(3)]
     turn = cross(radius, push)
     record = jnp.concatenate(push + turn + [store.astype(F32), body], axis=0)
-    columns = jnp.transpose(column_ref[...])
     upward = lax.rem(place_z + 1, 8)
     for j in range(8):
         for tile in range(links // 128):
@@ -421,7 +423,7 @@
             body_ref[b] += sum(part[:, 128 * t : 128 * t + 128] for t in range(8))
         return carry
 
-    lax.fori_loop(0, 8, one, 0)
+    lax.fori_loop(0, 8, one, 0, unroll=4)
 
     at_lane = iota((8, 128), 1)
     at_row = iota((8, 128), 0)
@@ -478,36 +480,56 @@
     xm_ref,
     yp_ref,
     ym_ref,
+    motion_hbm,
+    mass_hbm,
+    inertia_hbm,
+    moved_hbm,
+    load_hbm,
+    next_hbm,
+    moved_ref,
+    load_ref,
+    next_ref,
     motion_ref,
     mass_ref,
     inertia_ref,
-    moved_ref,
-    load_ref,
-    next_ref,
+    sems,
 ):
     speeds = lattice_tables()[0].astype(int)
     place_x, place_y, place_z = (lax.axis_index(a) for a in ("gx", "gy", "gz"))
     has_xp, has_xm = place_x < 7, place_x > 0
     has_yp, has_ym = place_y < 3, place_y > 0
     me = place_x * 4 + place_y
+    fetches = [
+        pltpu.make_async_copy(motion_hbm, motion_ref, sems.at[6]),
+        pltpu.make_async_copy(mass_hbm, mass_ref, sems.at[7]),
+        pltpu.make_async_copy(inertia_hbm, inertia_ref, sems.at[8]),
+    ]
+    for fetch in fetches:
+        fetch.start()
     total = got2_ref[0]
     for j in range(1, 32):
         total = total + got2_ref[j]
     load_ref[...] = total[0:6]
-    at_lane = iota((8, 128), 1)
-    at_row = iota((8, 128), 0)
-    own = jnp.where((at_lane & 7) == at_row, total[6:7], 0.0)
-    body_load = jnp.zeros((8, 128), F32)
-    scale = jnp.zeros((8, 128), F32)
-    for c in range(6):
-        column = jnp.sum(
-            jnp.where(lax.shift_right_logical(at_lane, 3) == c, own, 0.0), axis=1, keepdims=True
-        )
-        body_load = jnp.where(at_lane == c, column, body_load)
-        for b in range(8):
-            value = mass_ref[b] if c < 3 else inertia_ref[c - 3, b]
-            scale = jnp.where((at_lane == c) & (at_row == b), value, scale)
-    next_ref[...] = motion_ref[...] + (scale * body_load)[:, 0:6] / 32768.0
+    copies = [pltpu.make_async_copy(load_ref, load_hbm, sems.at[4])]
+    copies[0].start()
+
+    def advance():
+        at_lane = iota((8, 128), 1)
+        at_row = iota((8, 128), 0)
+        own = jnp.where((at_lane & 7) == at_row, total[6:7], 0.0)
+        body_load = jnp.zeros((8, 128), F32)
+        scale = jnp.zeros((8, 128), F32)
+        for c in range(6):
+            here = lax.shift_right_logical(at_lane, 3) == c
+            column = jnp.sum(jnp.where(here, own, 0.0), axis=1, keepdims=True)
+            body_load = jnp.where(at_lane == c, column, body_load)
+            for b in range(8):
+                value = mass_ref[b] if c < 3 else inertia_ref[c - 3, b]
+                scale = jnp.where((at_lane == c) & (at_row == b), value, scale)
+        next_ref[...] = motion_ref[...] + (scale * body_load)[:, 0:6] / 32768.0
+        copy = pltpu.make_async_copy(next_ref, next_hbm, sems.at[5])
+        copy.start()
+        copies.append(copy)
 
     def edge(there, step):
         line = got2_ref[jnp.where(there, me + step, me), 7:8, :]
@@ -553,6 +575,10 @@
     plane_lane = iota((32, 128), 1)
     plane_row = iota((32, 128), 0)
     for x in range(4):
+        if x == 2:
+            for fetch in fetches:
+                fetch.wait()
+            advance()
         rows = slice(32 * x, 32 * x + 32)
         code = bounce_ref[0, rows, :]
         value = bounce_ref[1, rows, :]
@@ -583,6 +609,11 @@
                 opposite = i + 1 if i % 2 else i - 1
                 plane = jnp.where(code == float(opposite), value, plane)
             moved_ref[i, x] = plane
+        copy = pltpu.make_async_copy(moved_ref.at[:, x], moved_hbm.at[:, x], sems.at[x])
+        copy.start()
+        copies.append(copy)
+    for copy in copies:
+        copy.wait()
 
 
 def body(
@@ -599,7 +630,6 @@
     rates,
 ):
     vmem = pl.BlockSpec(memory_space=pltpu.VMEM)
-    smem = pl.BlockSpec(memory_space=pltpu.SMEM)
     links = link_cell.shape[-1]
 
     def array(*shape):
@@ -631,7 +661,6 @@
             pltpu.SMEM((3, 8), F32),
             pltpu.SMEM((15,), F32),
             pltpu.VMEM((128, 128), F32),
-            pltpu.VMEM((128, 128), F32),
             pltpu.SemaphoreType.DMA((4,)),
             pltpu.SemaphoreType.DMA((8,)),
         ],
@@ -682,11 +711,26 @@
     moved, own_loads, motion_next = pl.pallas_call(
         third_kernel,
         out_shape=(array(19, 4, 32, 128), array(6, 128), array(8, 6)),
-        in_specs=[vmem] * 9 + [smem] * 2,
-        out_specs=(vmem,) * 3,
+        in_specs=[vmem] * 8 + [pl.BlockSpec(memory_space=pltpu.HBM)] * 3,
+        out_specs=(pl.BlockSpec(memory_space=pltpu.HBM),) * 3,
+        scratch_shapes=[
+            pltpu.VMEM((19, 4, 32, 128), F32),
+            pltpu.VMEM((6, 128), F32),
+            pltpu.VMEM((8, 6), F32),
+            pltpu.VMEM((8, 6), F32),
+            pltpu.SMEM((8,), F32),
+            pltpu.SMEM((3, 8), F32),
+            pltpu.SemaphoreType.DMA((9,)),
+        ],
         compiler_params=params,
         name="move",
-    )(post, bounce, got1, got2, xp, xm, yp, ym, motion, inv_mass, inv_inertia.T)
+    )(
+        *(post, bounce, got1, got2, xp, xm, yp, ym),
+        *(
+            pltpu.with_memory_space_constraint(x, pltpu.HBM)
+            for x in (motion, inv_mass, inv_inertia.T)
+        ),
+    )
     return (moved, own_loads, motion_next)
 
 

time: 46.8 us -> 45.4 us (0.970)
  Pallas kernels: 10.8 us -> 8.18 us
  blocking collectives: 14.9 us -> 15.9 us
    pallas_call x1, Pallas kernels: 2.99 us -> 1.78 us  [body(): pl.pallas_call(second_kernel, out_shape=array(32, 8, 128), in_specs=[vmem...]
    pallas_call x1, Pallas kernels: 5.47 us -> 4.36 us  [body(): pl.pallas_call(first_kernel, out_shape=(array(19, 128, 128), array(2, 128...]
    all_to_all x1, blocking collectives: 14.9 us -> 15.9 us  [body(): got2 = lax.all_to_all(send2, ('gx', 'gy'), 0, 0, tiled=True)]
  transfers between devices with their start and end apart: 5 -> 5, of which waited for: 1 -> 2; matrix products, arithmetic and copies ran while one was open for 0% -> 0% of each run, Pallas kernels for 6% -> 4%
where the time goes in v3:
time: 45.4 us; the launch traced here: 45.1 us
  starting transfers between devices  16.4 us (36%)
  blocking collectives  15.9 us (35%)
  Pallas kernels  8.18 us (18%)
  waiting for transfers between devices  3.98 us (9%)
  between operations  0.68 us (1%)
    all_to_all x1, blocking collectives, body(): got2 = lax.all_to_all(send2, ('gx', 'gy'), 0, 0, tiled=True)  15.9 us
    ppermute x4, starting transfers between devices, shift(): return lax.ppermute(x, axis, [(i, (i + by) % size) for i in range(size)])  10.8 us
    all_to_all x1, starting transfers between devices, body(): got1 = lax.all_to_all(send1, 'gz', 0, 0, tiled=True)  5.61 us
    pallas_call x1, Pallas kernels, body(): pl.pallas_call(first_kernel, out_shape=(array(19, 128, 128), array(2, 128...  4.36 us
    all_to_all x1, waiting for transfers between devices, body(): got1 = lax.all_to_all(send1, 'gz', 0, 0, tiled=True)  3.73 us
    pallas_call x1, Pallas kernels, body(): pl.pallas_call(third_kernel, out_shape=(array(19, 4, 32, 128), array(6, 1...  2.04 us
    pallas_call x1, Pallas kernels, body(): pl.pallas_call(second_kernel, out_shape=array(32, 8, 128), in_specs=[vmem...  1.78 us
  transfers between devices with their start and end apart: 5, of which 2 were waited for; matrix products, arithmetic and copies ran while one was open for 0% of the time, Pallas kernels for 4%

profile of v3, /device:TPU:2, one launch (start us, length us, event | category | flops | bytes accessed | tf_op | source)
XLA Modules:
  0.0 45.1 jit_solution(15413576193724539951)
XLA Ops:
  0.6 4.4 %collide.1 = (f32[19,128,128]{2,1,0:T(8,128)S(1)}, f32[2,128,128]{2,1,0:T(8,128)S(1)}, f32[8,9,8,128]{3,2,1,0:T(8,128)}, f32[5,32,128]{2,1,0:T(8,128)S(1)}, f32[...) custom-call(f32[19,128,128]{2,1,0:T(8,128)} %bitcast.8, ...), custom_call_target="tpu_custom_call" | custom-call | tf_op jit(solution)/shard_map/collide/pallas_call | solution.py:639
  5.0 5.6 %all-to-all-start = ((f32[8,9,8,128]{3,2,1,0:T(8,128)}), f32[8,9,8,128]{3,2,1,0:T(8,128)S(1)}, u32[]{:S(2)}, u32[]{:S(2)}) async-start(f32[8,9,8,128]{3,2,1,0:T(8,128)} %get-tuple-element.23), calls=%async_computation | async-start | bytes 589824 | tf_op jit(solution)/shard_map/all_to_all | solution.py:693
  10.6 0.8 %collective-permute-start.2 = (f32[24,128]{1,0:T(8,128)S(1)}, f32[24,128]{1,0:T(8,128)S(1)}, u32[]{:S(2)}, u32[]{:S(2)}) collective-permute-start(f32[24,128]{1,0:T(8,128)S(1)} %get-tuple-element.28), channel_id=1, source_target_pairs={{0,8},{8,16},{16,24},{24,0},{1,9},{9,17},{17,25},{25,1},{2,10},{10... | collective-permute-start | bytes 36872 | tf_op jit(solution)/shard_map/ppermute | solution.py:688
  11.4 1.9 %collective-permute-start = (f32[5,32,128]{2,1,0:T(8,128)S(1)}, f32[5,32,128]{2,1,0:T(8,128)S(1)}, u32[]{:S(2)}, u32[]{:S(2)}) collective-permute-start(f32[5,32,128]{2,1,0:T(8,128)S(1)} %get-tuple-element.26), channel_id=1, source_target_pairs={{0,32},{32,64},{64,96},{96,128},{128,160},{160,192},{192,224},{224... | collective-permute-start | bytes 245768 | tf_op jit(solution)/shard_map/ppermute | solution.py:688
  13.3 3.7 %all-to-all-done.got_ref.got1_ref = f32[8,9,8,128]{3,2,1,0:T(8,128)S(1)} async-done(((f32[8,9,8,128]{3,2,1,0:T(8,128)}), f32[8,9,8,128]{3,2,1,0:T(8,128)S(1)}, u32[]{:S(2)}, u32[]{:S(2)}) %all-to-all-start) | async-done | bytes 294944 | tf_op jit(solution)/shard_map/all_to_all | solution.py:693
  17.1 2.2 %collective-permute-start.3 = (f32[24,128]{1,0:T(8,128)S(1)}, f32[24,128]{1,0:T(8,128)S(1)}, u32[]{:S(2)}, u32[]{:S(2)}) collective-permute-start(f32[24,128]{1,0:T(8,128)S(1)} %get-tuple-element.29), channel_id=1, source_target_pairs={{0,24},{8,0},{16,8},{24,16},{1,25},{9,1},{17,9},{25,17},{2,26},{10... | collective-permute-start | bytes 36872 | tf_op jit(solution)/shard_map/ppermute | solution.py:688
  19.3 5.9 %collective-permute-start.1 = (f32[5,32,128]{2,1,0:T(8,128)S(1)}, f32[5,32,128]{2,1,0:T(8,128)S(1)}, u32[]{:S(2)}, u32[]{:S(2)}) collective-permute-start(f32[5,32,128]{2,1,0:T(8,128)S(1)} %get-tuple-element.27), channel_id=1, source_target_pairs={{0,224},{32,0},{64,32},{96,64},{128,96},{160,128},{192,160},{224,1... | collective-permute-start | bytes 245768 | tf_op jit(solution)/shard_map/ppermute | solution.py:688
  25.2 1.8 %bins.1 = f32[32,8,128]{2,1,0:T(8,128)S(1)} custom-call(f32[8,9,8,128]{3,2,1,0:T(8,128)S(1)} %all-to-all-done.got_ref.got1_ref, f32[8,128]{1,0:T(8,128)S(1)} %get-tuple-element.25.xy_ref), custom_call_target="tpu_custom_call" | custom-call | flops 1073741824 | bytes 262144 | tf_op jit(solution)/shard_map/bins/pallas_call | solution.py:697
  26.9 0.0 collective-permute-done.2.yp_ref
  27.0 0.0 collective-permute-done.xp_ref
  27.0 0.0 collective-permute-done.3.ym_ref
  27.0 0.2 collective-permute-done.1.xm_ref
  27.2 15.9 %all_to_all.10.got2_ref = f32[32,8,128]{2,1,0:T(8,128)S(1)} all-to-all(f32[32,8,128]{2,1,0:T(8,128)S(1)} %bins.1), channel_id=1, replica_groups=mesh['gx'=8,'gy'=4,'gz'=8] {'gx','gy'}, dimensions={0} | all-to-all | bytes 262144 | tf_op jit(solution)/shard_map/all_to_all | solution.py:710
  43.1 2.0 %move.1 = (f32[19,4,32,128]{3,2,1,0:T(8,128)}, f32[6,128]{1,0:T(8,128)}, f32[8,6]{1,0:T(8,128)}) custom-call(f32[19,128,128]{2,1,0:T(8,128)S(1)} %get-tuple-element.19.post_ref, f32[2,128,128]{2,1,0:T(8,128)S(1)} %get-tuple-element.20.bounce_ref, f32[8,9,8,128]{3,2,1,0:T(8,128)S(1)} %all-to-all-done.got_ref.got1_ref, f32[32,8,128]{2,1,0:T(8,128)S(1)} %all_to_all.10.got2_ref, ...), custom_call_target="tpu_custom_call" | custom-call | tf_op jit(solution)/shard_map/move/pallas_call | solution.py:711
Async XLA Ops:
  5.0 12.1 %all-to-all-start = ((f32[8,9,8,128]{3,2,1,0:T(8,128)}), f32[8,9,8,128]{3,2,1,0:T(8,128)S(1)}, u32[]{:S(2)}, u32[]{:S(2)}) async-start(f32[8,9,8,128]{3,2,1,0:T(8,128)} %get-tuple-element.23), calls=%async_computation | async-start | bytes 589824 | tf_op jit(solution)/shard_map/all_to_all | solution.py:693
  10.6 16.3 %collective-permute-start.2 = (f32[24,128]{1,0:T(8,128)S(1)}, f32[24,128]{1,0:T(8,128)S(1)}, u32[]{:S(2)}, u32[]{:S(2)}) collective-permute-start(f32[24,128]{1,0:T(8,128)S(1)} %get-tuple-element.28), channel_id=1, source_target_pairs={{0,8},{8,16},{16,24},{24,0},{1,9},{9,17},{17,25},{25,1},{2,10},{10... | collective-permute-start | bytes 36872 | tf_op jit(solution)/shard_map/ppermute | solution.py:688
  11.4 15.5 %collective-permute-start = (f32[5,32,128]{2,1,0:T(8,128)S(1)}, f32[5,32,128]{2,1,0:T(8,128)S(1)}, u32[]{:S(2)}, u32[]{:S(2)}) collective-permute-start(f32[5,32,128]{2,1,0:T(8,128)S(1)} %get-tuple-element.26), channel_id=1, source_target_pairs={{0,32},{32,64},{64,96},{96,128},{128,160},{160,192},{192,224},{224... | collective-permute-start | bytes 245768 | tf_op jit(solution)/shard_map/ppermute | solution.py:688
  17.1 9.9 %collective-permute-start.3 = (f32[24,128]{1,0:T(8,128)S(1)}, f32[24,128]{1,0:T(8,128)S(1)}, u32[]{:S(2)}, u32[]{:S(2)}) collective-permute-start(f32[24,128]{1,0:T(8,128)S(1)} %get-tuple-element.29), channel_id=1, source_target_pairs={{0,24},{8,0},{16,8},{24,16},{1,25},{9,1},{17,9},{25,17},{2,26},{10... | collective-permute-start | bytes 36872 | tf_op jit(solution)/shard_map/ppermute | solution.py:688
  19.3 7.9 %collective-permute-start.1 = (f32[5,32,128]{2,1,0:T(8,128)S(1)}, f32[5,32,128]{2,1,0:T(8,128)S(1)}, u32[]{:S(2)}, u32[]{:S(2)}) collective-permute-start(f32[5,32,128]{2,1,0:T(8,128)S(1)} %get-tuple-element.27), channel_id=1, source_target_pairs={{0,224},{32,0},{64,32},{96,64},{128,96},{160,128},{192,160},{224,1... | collective-permute-start | bytes 245768 | tf_op jit(solution)/shard_map/ppermute | solution.py:688

commit v4 on v3

--- a/solution.py
+++ b/solution.py
@@ -194,6 +194,18 @@
     return lax.dot_general(a, b, (((1,), (1,)), ((), ())), preferred_element_type=F32)
 
 
+def flat(x):
+    return jnp.concatenate([x[s : s + 1] for s in range(8)], axis=1)
+
+
+def fold(x):
+    return jnp.concatenate([x[:, 128 * s : 128 * s + 128] for s in range(8)], axis=0)
+
+
+def cross(a, b):
+    return [a[(i + 1) % 3] * b[(i + 2) % 3] - a[(i + 2) % 3] * b[(i + 1) % 3] for i in range(3)]
+
+
 def iota(shape, dim):
     return lax.broadcasted_iota(I32, shape, dim)
 
@@ -225,6 +237,7 @@
     yp_ref,
     ym_ref,
     xy_ref,
+    own_ref,
     pop_ref,
     solid_ref,
     cell_ref,
@@ -263,7 +276,7 @@
     for copy in copies:
         copy.wait()
     speeds, weights, _ = lattice_tables()
-    links = cell_ref.shape[1]
+    links = 1024
     place_x, place_y, place_z = (lax.axis_index(a) for a in ("gx", "gy", "gz"))
     cell = cell_ref[...]
     direction = dir_ref[...]
@@ -271,6 +284,7 @@
     live = store < 32768
     row = lax.shift_right_logical(cell, 7)
     lane = cell & 127
+    flat_row = flat(row)
     one = jnp.ones((16, links), BF16)
     none = jnp.zeros((16, links), BF16)
 
@@ -284,16 +298,16 @@
     def hot(index):
         return jnp.concatenate(groups(index, one), axis=0)
 
-    rows_hot16 = hot(row)
-    lanes_hot16 = hot(lane)
-    store_high = lax.shift_right_logical(store, 7)
-    low_hot = hot(store & 127)
+    flat_lane = flat(lane)
+    rows_hot16 = hot(flat_row)
+    lanes_hot16 = hot(flat_lane)
+    flat_store = flat(store)
+    low_hot = hot(flat_store & 127)
     by_high = jnp.dot(
         owner_ref[...].astype(F32).astype(BF16), low_hot, preferred_element_type=F32
     )
-    body = jnp.sum(
-        jnp.where(iota((256, links), 0) == store_high, by_high, 0.0), axis=0, keepdims=True
-    )
+    here = iota((256, links), 0) == lax.shift_right_logical(flat_store, 7)
+    body = fold(jnp.sum(jnp.where(here, by_high, 0.0), axis=0, keepdims=True))
     is_dir = [direction == i for i in range(19)]
     shape = direction.shape
     speed = [pick(is_dir, [float(s) for s in speeds[:, a]], shape) for a in range(3)]
@@ -311,17 +325,14 @@
         (place[a].astype(F32) + 0.5 * speed[a] - middle[a] * extents[a]) / 128.0 for a in range(3)
     ]
 
-    def cross(a, b):
-        return [a[(i + 1) % 3] * b[(i + 2) % 3] - a[(i + 2) % 3] * b[(i + 1) % 3] for i in range(3)]
-
     spin = cross(move[3:], radius)
     normal = sum(speed[a] * (move[a] + spin[a]) for a in range(3))
     wall = 6.0 * weight * normal
     coded = jnp.where(live, direction, 0).astype(F32)
-    wall_high, wall_low = halves(wall)
     spread = []
-    for value in (coded.astype(BF16), wall_high, wall_low):
-        spread += groups(lane, jnp.broadcast_to(value.astype(F32), (16, links)).astype(BF16))
+    for value in (coded, *halves(wall)):
+        value = jnp.broadcast_to(flat(value.astype(F32)), (16, links)).astype(BF16)
+        spread += groups(flat_lane, value)
     laid = rows_dot(rows_hot16, jnp.concatenate(spread, axis=0))
     bounce_ref[0] = laid[:, 0:128]
     bounce_ref[1] = laid[:, 128:256] + laid[:, 256:384]
@@ -374,74 +385,95 @@
     by_row = jnp.dot(
         jnp.concatenate([found_high, found_low], axis=0), lanes_hot16, preferred_element_type=F32
     )
-    by_row = jnp.where(iota((128, links), 0) == row, by_row[0:128] + by_row[128:256], 0.0)
-    picked = jnp.sum(by_row, axis=0, keepdims=True)
+    by_row = jnp.where(
+        iota((128, links), 0) == flat_row, by_row[0:128] + by_row[128:256], 0.0
+    )
+    picked = fold(jnp.sum(by_row, axis=0, keepdims=True))
     strength = jnp.where(live, 2.0 * picked - wall, 0.0)
     push = [speed[a] * strength for a in range(3)]
-    turn = cross(radius, push)
-    record = jnp.concatenate(push + turn + [store.astype(F32), body], axis=0)
+    sums = []
+    for load in push + cross(radius, push):
+        for b in range(8):
+            sums.append(jnp.sum(jnp.where(is_body[b], load, 0.0), axis=0, keepdims=True))
+    sums = jnp.sum(jnp.concatenate(sums, axis=0), axis=1, keepdims=True)
+    sums = jnp.where(iota((48, 128), 0) == iota((48, 128), 1), sums, 0.0)
+    body_row = jnp.sum(sums, axis=0, keepdims=True)
     upward = lax.rem(place_z + 1, 8)
+    records = (strength, direction.astype(F32), cell.astype(F32), store.astype(F32))
     for j in range(8):
-        for tile in range(links // 128):
-            send_ref[j, tile] = record[:, tile * 128 : (tile + 1) * 128]
-        send_ref[j, 8] = jnp.where(upward == j, columns[0:8], columns[8:16])
-
-
-def second_kernel(got_ref, xy_ref, send_ref, total_ref, body_ref):
+        for n, record in enumerate(records):
+            send_ref[j, n] = record
+        face = jnp.where(upward == j, columns[0:8], columns[8:16])
+        send_ref[j, 4] = jnp.where(iota((8, 128), 0) == 5, body_row, face)
+    own = owner_ref[pl.ds((place_x * 4 + place_y) * 8 + place_z, 1), :]
+    own_ref[...] = jnp.zeros((8, 128), F32)
+    for a in range(3):
+        middle = pick([own == b for b in range(8)], [centre_ref[a, b] for b in range(8)], (1, 128))
+        own_ref[a : a + 1, :] = (middle - 0.5) * (extents[a] / 128.0)
+
+
+def second_kernel(got_ref, xy_ref, send_ref, total_ref):
+    speeds = lattice_tables()[0]
     place_x, place_y, place_z = (lax.axis_index(a) for a in ("gx", "gy", "gz"))
     total_ref[...] = jnp.zeros_like(total_ref)
-    body_ref[...] = jnp.zeros_like(body_ref)
-    links = 1024
-
-    def one(peer, carry):
-        record = jnp.concatenate([got_ref[peer, tile] for tile in range(8)], axis=1)
-        store = record[6:7].astype(I32)
-        body = record[7:8]
-        loads = jnp.where(iota((8, links), 0) < 6, record, 0.0)
+    count = iota((16, 128), 0).astype(F32)
+    counts = [(count + 16.0 * g).astype(BF16) for g in range(16)]
+    one = jnp.ones((16, 128), BF16)
+    none = jnp.zeros((16, 128), BF16)
+
+    def gather(peer, carry):
+        strength, direction = got_ref[peer, 0], got_ref[peer, 1]
+        cell, store = got_ref[peer, 2].astype(I32), got_ref[peer, 3].astype(I32)
+        is_dir = [direction == float(i) for i in range(19)]
+        speed = [pick(is_dir, [float(v) for v in speeds[:, a]], (8, 128)) for a in range(3)]
+        place = (
+            lax.shift_right_logical(cell, 12) + (place_x * 4 - 16),
+            (lax.shift_right_logical(cell, 7) & 31) + (place_y * 32 - 64),
+            (cell & 127) + (peer * 128 - 512),
+        )
+        arm = [(place[a].astype(F32) + 0.5 * speed[a]) * (1.0 / 128.0) for a in range(3)]
+        push = [speed[a] * strength for a in range(3)]
+        loads = push + cross(arm, push)
+        upper = [load.astype(BF16).astype(F32) for load in loads]
+        rows = upper + [load - part for load, part in zip(loads, upper)]
         owner = lax.shift_right_logical(store, 7)
         mine = (owner & 7) == place_z
-        high = jnp.where(mine, lax.shift_right_logical(owner, 4), -1)
+        high = jnp.where(mine, lax.shift_right_logical(owner, 4), 255).astype(F32)
         low = ((lax.shift_right_logical(owner, 3) & 1) * 128) + (store & 127)
-        both = jnp.concatenate(halves(loads), axis=0)
-        none = jnp.zeros_like(both)
-        high = jnp.broadcast_to(high.astype(F32), (16, links)).astype(BF16)
-        spread = jnp.concatenate(
-            [jnp.where(high == jnp.bfloat16(h), both, none) for h in range(16)], axis=0
+        low = low.astype(F32)
+        left, right = [], []
+        for s in range(8):
+
+            def line(x, s=s):
+                return jnp.broadcast_to(x[s : s + 1], (16, 128)).astype(BF16)
+
+            at = line(high) == counts[0]
+            left.append(jnp.concatenate([jnp.where(at, line(x), none) for x in rows], axis=0))
+            at = line(low)
+            right.append(
+                jnp.concatenate([jnp.where(at == number, one, none) for number in counts], axis=0)
+            )
+        total_ref[...] += rows_dot(
+            jnp.concatenate(left, axis=1), jnp.concatenate(right, axis=1)
         )
-        low = jnp.broadcast_to(low.astype(F32), (16, links)).astype(BF16)
-        one = jnp.ones((16, links), BF16)
-        low_hot = jnp.concatenate(
-            [
-                jnp.where(low == (iota((16, links), 0) + 16 * g).astype(F32).astype(BF16), one, none)
-                for g in range(16)
-            ],
-            axis=0,
-        )
-        total_ref[...] += rows_dot(spread, low_hot)
-        for b in range(8):
-            part = jnp.where(body == float(b), loads, 0.0)
-            body_ref[b] += sum(part[:, 128 * t : 128 * t + 128] for t in range(8))
         return carry
 
-    lax.fori_loop(0, 8, one, 0, unroll=4)
-
-    at_lane = iota((8, 128), 1)
-    at_row = iota((8, 128), 0)
-    body_row = jnp.zeros((8, 128), F32)
-    for b in range(8):
-        column = jnp.sum(body_ref[b], axis=1, keepdims=True)
-        body_row = jnp.where(at_lane == at_row * 8 + b, column, body_row)
-    body_row = jnp.where(at_row < 6, body_row, 0.0)
-    body_row = jnp.sum(body_row, axis=0, keepdims=True)
-    for h in range(16):
+    lax.fori_loop(0, 8, gather, 0, unroll=4)
+
+    body_row = sum(got_ref[peer, 4, 5:6, :] for peer in range(8))
+    for c in range(6):
         for e in range(2):
             lanes = slice(128 * e, 128 * e + 128)
-            tile = total_ref[16 * h : 16 * h + 8, lanes] + total_ref[16 * h + 8 : 16 * h + 16, lanes]
-            tile = jnp.where(at_row == 6, body_row, tile)
-            send_ref[2 * h + e] = jnp.where(at_row == 7, 0.0, tile)
-
-    below = got_ref[lax.rem(place_z + 7, 8), 8]
-    above = got_ref[lax.rem(place_z + 1, 8), 8]
+            upper = total_ref[16 * c : 16 * c + 16, lanes]
+            both = upper + total_ref[96 + 16 * c : 112 + 16 * c, lanes]
+            for h in range(16):
+                send_ref[2 * h + e, c : c + 1, :] = both[h : h + 1]
+    last = jnp.concatenate([body_row, jnp.zeros((1, 128), F32)], axis=0)
+    for j in range(32):
+        send_ref[j, 6:8, :] = last
+
+    below = got_ref[lax.rem(place_z + 7, 8), 4]
+    above = got_ref[lax.rem(place_z + 1, 8), 4]
     lane = iota((1, 128), 1)
 
     def turned(x, by):
@@ -474,6 +506,7 @@
 def third_kernel(
     post_ref,
     bounce_ref,
+    own_ref,
     got1_ref,
     got2_ref,
     xp_ref,
@@ -509,7 +542,10 @@
     total = got2_ref[0]
     for j in range(1, 32):
         total = total + got2_ref[j]
-    load_ref[...] = total[0:6]
+    push = [total[a : a + 1] for a in range(3)]
+    away = cross([own_ref[a : a + 1, :] for a in range(3)], push)
+    turn = [total[3 + a : 4 + a] - away[a] for a in range(3)]
+    load_ref[...] = jnp.concatenate(push + turn, axis=0)
     copies = [pltpu.make_async_copy(load_ref, load_hbm, sems.at[4])]
     copies[0].start()
 
@@ -547,8 +583,8 @@
     }
     entering = {}
     for dirs, face in (
-        (ZP, got1_ref[lax.rem(place_z + 7, 8), 8]),
-        (ZM, got1_ref[lax.rem(place_z + 1, 8), 8]),
+        (ZP, got1_ref[lax.rem(place_z + 7, 8), 4]),
+        (ZM, got1_ref[lax.rem(place_z + 1, 8), 4]),
     ):
         for n, i in enumerate(dirs):
             line = face[n : n + 1]
@@ -630,32 +666,32 @@
     rates,
 ):
     vmem = pl.BlockSpec(memory_space=pltpu.VMEM)
-    links = link_cell.shape[-1]
 
     def array(*shape):
         return jax.ShapeDtypeStruct(shape, F32)
 
     params = pltpu.CompilerParams(vmem_limit_bytes=40 * 1024 * 1024)
-    post, bounce, send1, xp, xm, yp, ym, xy = pl.pallas_call(
+    post, bounce, send1, xp, xm, yp, ym, xy, own = pl.pallas_call(
         first_kernel,
         out_shape=(
             array(19, 128, 128),
             array(2, 128, 128),
-            array(8, 9, 8, 128),
+            array(8, 5, 8, 128),
             array(5, 32, 128),
             array(5, 32, 128),
             array(24, 128),
             array(24, 128),
             array(8, 128),
+            array(8, 128),
         ),
         in_specs=[pl.BlockSpec(memory_space=pltpu.HBM)] * 9,
-        out_specs=(vmem,) * 8,
+        out_specs=(vmem,) * 9,
         scratch_shapes=[
             pltpu.VMEM((19, 128, 128), F32),
             pltpu.VMEM((128, 128), I32),
-            pltpu.VMEM((1, links), I32),
-            pltpu.VMEM((1, links), I32),
-            pltpu.VMEM((1, links), I32),
+            pltpu.VMEM((8, 128), I32),
+            pltpu.VMEM((8, 128), I32),
+            pltpu.VMEM((8, 128), I32),
             pltpu.VMEM((256, 128), I32),
             pltpu.SMEM((8, 6), F32),
             pltpu.SMEM((3, 8), F32),
@@ -672,9 +708,9 @@
             for x in (
                 populations.reshape(19, 128, 128),
                 solid.reshape(128, 128),
-                link_cell.reshape(1, links),
-                link_dir.reshape(1, links),
-                link_store.reshape(1, links),
+                link_cell.reshape(8, 128),
+                link_dir.reshape(8, 128),
+                link_store.reshape(8, 128),
                 store_body.reshape(256, 128),
                 motion,
                 centre.T,
@@ -688,30 +724,27 @@
         return lax.ppermute(x, axis, [(i, (i + by) % size) for i in range(size)])
 
     after = lax.optimization_barrier
-    xp = shift(xp, "gx", 1)
-    yp = shift(yp, "gy", 1)
+    xp, xm = shift(xp, "gx", 1), shift(xm, "gx", -1)
     got1 = lax.all_to_all(send1, "gz", 0, 0, tiled=True)
-    xm, ym, got1 = after((xm, ym, got1))
-    xm = shift(xm, "gx", -1)
-    ym = shift(ym, "gy", -1)
     send2 = pl.pallas_call(
         second_kernel,
         out_shape=array(32, 8, 128),
         in_specs=[vmem] * 2,
         out_specs=vmem,
-        scratch_shapes=[pltpu.VMEM((256, 256), F32), pltpu.VMEM((8, 8, 128), F32)],
+        scratch_shapes=[pltpu.VMEM((192, 256), F32)],
         compiler_params=params,
         cost_estimate=pl.CostEstimate(
-            flops=2 * 256 * 256 * 8192, bytes_accessed=4 * 8 * 8192, transcendentals=0
+            flops=2 * 192 * 256 * 8192, bytes_accessed=4 * 4 * 8192, transcendentals=0
         ),
         name="bins",
     )(got1, xy)
     send2, xp, xm, yp, ym = after((send2, xp, xm, yp, ym))
+    yp, ym = shift(yp, "gy", 1), shift(ym, "gy", -1)
     got2 = lax.all_to_all(send2, ("gx", "gy"), 0, 0, tiled=True)
     moved, own_loads, motion_next = pl.pallas_call(
         third_kernel,
         out_shape=(array(19, 4, 32, 128), array(6, 128), array(8, 6)),
-        in_specs=[vmem] * 8 + [pl.BlockSpec(memory_space=pltpu.HBM)] * 3,
+        in_specs=[vmem] * 9 + [pl.BlockSpec(memory_space=pltpu.HBM)] * 3,
         out_specs=(pl.BlockSpec(memory_space=pltpu.HBM),) * 3,
         scratch_shapes=[
             pltpu.VMEM((19, 4, 32, 128), F32),
@@ -725,7 +758,7 @@
         compiler_params=params,
         name="move",
     )(
-        *(post, bounce, got1, got2, xp, xm, yp, ym),
+        *(post, bounce, own, got1, got2, xp, xm, yp, ym),
         *(
             pltpu.with_memory_space_constraint(x, pltpu.HBM)
             for x in (motion, inv_mass, inv_inertia.T)

time: 45.4 us -> 41.9 us (0.923)
  blocking collectives: 15.9 us -> 0 us
  starting transfers between devices: 16.4 us -> 24.4 us
  waiting for transfers between devices: 3.98 us -> 7.48 us
  Pallas kernels: 8.18 us -> 8.98 us
    all_to_all x1 -> x0, blocking collectives: 15.9 us -> none  [body(): got2 = lax.all_to_all(send2, ('gx', 'gy'), 0, 0, tiled=True)]
    all_to_all x0 -> x1, starting transfers between devices: none -> 10.4 us  [body(): got2 = lax.all_to_all(send2, ('gx', 'gy'), 0, 0, tiled=True)]
    all_to_all x0 -> x1, waiting for transfers between devices: none -> 4.88 us  [body(): got2 = lax.all_to_all(send2, ('gx', 'gy'), 0, 0, tiled=True)]
    all_to_all x1, waiting for transfers between devices: 3.73 us -> 0.01 us  [body(): got1 = lax.all_to_all(send1, 'gz', 0, 0, tiled=True)]
    ppermute x4, starting transfers between devices: 10.8 us -> 8.45 us  [shift(): return lax.ppermute(x, axis, [(i, (i + by) % size) for i in range(size)])]
    ppermute x4, waiting for transfers between devices: 0.25 us -> 2.6 us  [shift(): return lax.ppermute(x, axis, [(i, (i + by) % size) for i in range(size)])]
    pallas_call x1, Pallas kernels: 1.78 us -> 2.48 us  [body(): pl.pallas_call(second_kernel, out_shape=array(32, 8, 128), in_specs=[vmem...]
  transfers between devices with their start and end apart: 5 -> 6, of which waited for: 2 -> 4; matrix products, arithmetic and copies ran while one was open for 0% -> 0% of each run, Pallas kernels for 4% -> 6%
where the time goes in v4:
time: 41.9 us; the launch traced here: 41.5 us
  starting transfers between devices  24.4 us (58%)
  Pallas kernels  8.98 us (21%)
  waiting for transfers between devices  7.48 us (18%)
  between operations  0.66 us (2%)
    all_to_all x1, starting transfers between devices, body(): got2 = lax.all_to_all(send2, ('gx', 'gy'), 0, 0, tiled=True)  10.4 us
    ppermute x4, starting transfers between devices, shift(): return lax.ppermute(x, axis, [(i, (i + by) % size) for i in range(size)])  8.45 us
    all_to_all x1, starting transfers between devices, body(): got1 = lax.all_to_all(send1, 'gz', 0, 0, tiled=True)  5.57 us
    all_to_all x1, waiting for transfers between devices, body(): got2 = lax.all_to_all(send2, ('gx', 'gy'), 0, 0, tiled=True)  4.88 us
    pallas_call x1, Pallas kernels, body(): pl.pallas_call(first_kernel, out_shape=(array(19, 128, 128), array(2, 128...  4.24 us
    ppermute x4, waiting for transfers between devices, shift(): return lax.ppermute(x, axis, [(i, (i + by) % size) for i in range(size)])  2.6 us
    pallas_call x1, Pallas kernels, body(): pl.pallas_call(second_kernel, out_shape=array(32, 8, 128), in_specs=[vmem...  2.48 us
    pallas_call x1, Pallas kernels, body(): pl.pallas_call(third_kernel, out_shape=(array(19, 4, 32, 128), array(6, 1...  2.25 us
  transfers between devices with their start and end apart: 6, of which 4 were waited for; matrix products, arithmetic and copies ran while one was open for 0% of the time, Pallas kernels for 6%

profile of v4, /device:TPU:2, one launch (start us, length us, event | category | flops | bytes accessed | tf_op | source)
XLA Modules:
  0.0 41.5 jit_solution(15657212931362761197)
XLA Ops:
  0.6 4.2 %collide.1 = (f32[19,128,128]{2,1,0:T(8,128)S(1)}, f32[2,128,128]{2,1,0:T(8,128)S(1)}, f32[8,5,8,128]{3,2,1,0:T(8,128)}, f32[5,32,128]{2,1,0:T(8,128)S(1)}, f32[...) custom-call(f32[19,128,128]{2,1,0:T(8,128)} %bitcast.8, ...), custom_call_target="tpu_custom_call" | custom-call | tf_op jit(solution)/shard_map/collide/pallas_call | solution.py:674
  4.9 5.6 %all-to-all-start = ((f32[8,5,8,128]{3,2,1,0:T(8,128)}), f32[8,5,8,128]{3,2,1,0:T(8,128)S(1)}, u32[]{:S(2)}, u32[]{:S(2)}) async-start(f32[8,5,8,128]{3,2,1,0:T(8,128)} %get-tuple-element.20), calls=%async_computation | async-start | bytes 327680 | tf_op jit(solution)/shard_map/all_to_all | solution.py:728
  10.5 1.2 %collective-permute-start = (f32[5,32,128]{2,1,0:T(8,128)S(1)}, f32[5,32,128]{2,1,0:T(8,128)S(1)}, u32[]{:S(2)}, u32[]{:S(2)}) collective-permute-start(f32[5,32,128]{2,1,0:T(8,128)S(1)} %get-tuple-element.22), channel_id=1, source_target_pairs={{0,32},{32,64},{64,96},{96,128},{128,160},{160,192},{192,224},{224... | collective-permute-start | bytes 245768 | tf_op jit(solution)/shard_map/ppermute | solution.py:724
  11.6 3.9 %collective-permute-start.1 = (f32[5,32,128]{2,1,0:T(8,128)S(1)}, f32[5,32,128]{2,1,0:T(8,128)S(1)}, u32[]{:S(2)}, u32[]{:S(2)}) collective-permute-start(f32[5,32,128]{2,1,0:T(8,128)S(1)} %get-tuple-element.23), channel_id=1, source_target_pairs={{0,224},{32,0},{64,32},{96,64},{128,96},{160,128},{192,160},{224,1... | collective-permute-start | bytes 245768 | tf_op jit(solution)/shard_map/ppermute | solution.py:724
  15.6 0.0 all-to-all-done.got_ref.got1_ref
  15.6 2.5 %bins.1 = f32[32,8,128]{2,1,0:T(8,128)} custom-call(f32[8,5,8,128]{3,2,1,0:T(8,128)S(1)} %all-to-all-done.got_ref.got1_ref, f32[8,128]{1,0:T(8,128)S(1)} %get-tuple-element.21.xy_ref), custom_call_target="tpu_custom_call" | custom-call | flops 805306368 | bytes 131072 | tf_op jit(solution)/shard_map/bins/pallas_call | solution.py:729
  18.1 0.3 collective-permute-done.xp_ref
  18.3 0.0 collective-permute-done.1.xm_ref
  18.3 10.4 %all-to-all-start.1 = ((f32[32,8,128]{2,1,0:T(8,128)}), f32[32,8,128]{2,1,0:T(8,128)S(1)}, u32[]{:S(2)}, u32[]{:S(2)}) async-start(f32[32,8,128]{2,1,0:T(8,128)} %bins.1), calls=%async_computation.1 | async-start | bytes 262144 | tf_op jit(solution)/shard_map/all_to_all | solution.py:743
  28.7 1.9 %collective-permute-start.2 = (f32[24,128]{1,0:T(8,128)S(1)}, f32[24,128]{1,0:T(8,128)S(1)}, u32[]{:S(2)}, u32[]{:S(2)}) collective-permute-start(f32[24,128]{1,0:T(8,128)S(1)} %get-tuple-element.29), channel_id=1, source_target_pairs={{0,8},{8,16},{16,24},{24,0},{1,9},{9,17},{17,25},{25,1},{2,10},{10... | collective-permute-start | bytes 36872 | tf_op jit(solution)/shard_map/ppermute | solution.py:724
  30.6 1.4 %collective-permute-start.3 = (f32[24,128]{1,0:T(8,128)S(1)}, f32[24,128]{1,0:T(8,128)S(1)}, u32[]{:S(2)}, u32[]{:S(2)}) collective-permute-start(f32[24,128]{1,0:T(8,128)S(1)} %get-tuple-element.30), channel_id=1, source_target_pairs={{0,24},{8,0},{16,8},{24,16},{1,25},{9,1},{17,9},{25,17},{2,26},{10... | collective-permute-start | bytes 36872 | tf_op jit(solution)/shard_map/ppermute | solution.py:724
  32.1 1.7 %collective-permute-done.2.yp_ref = f32[24,128]{1,0:T(8,128)S(1)} collective-permute-done((f32[24,128]{1,0:T(8,128)S(1)}, f32[24,128]{1,0:T(8,128)S(1)}, u32[]{:S(2)}, u32[]{:S(2)}) %collective-permute-start.2) | collective-permute-done | bytes 12320 | tf_op jit(solution)/shard_map/ppermute | solution.py:724
  33.8 0.6 %collective-permute-done.3.ym_ref = f32[24,128]{1,0:T(8,128)S(1)} collective-permute-done((f32[24,128]{1,0:T(8,128)S(1)}, f32[24,128]{1,0:T(8,128)S(1)}, u32[]{:S(2)}, u32[]{:S(2)}) %collective-permute-start.3) | collective-permute-done | bytes 12320 | tf_op jit(solution)/shard_map/ppermute | solution.py:724
  34.4 4.9 %all-to-all-done.1.got2_ref = f32[32,8,128]{2,1,0:T(8,128)S(1)} async-done(((f32[32,8,128]{2,1,0:T(8,128)}), f32[32,8,128]{2,1,0:T(8,128)S(1)}, u32[]{:S(2)}, u32[]{:S(2)}) %all-to-all-start.1) | async-done | bytes 131104 | tf_op jit(solution)/shard_map/all_to_all | solution.py:743
  39.3 2.3 %move.1 = (f32[19,4,32,128]{3,2,1,0:T(8,128)}, f32[6,128]{1,0:T(8,128)}, f32[8,6]{1,0:T(8,128)}) custom-call(f32[19,128,128]{2,1,0:T(8,128)S(1)} %get-tuple-element.17.post_ref, f32[2,128,128]{2,1,0:T(8,128)S(1)} %get-tuple-element.18.bounce_ref, f32[8,128]{1,0:T(8,128)S(1)} %get-tuple-element.19.own_ref, ...), custom_call_target="tpu_custom_call" | custom-call | tf_op jit(solution)/shard_map/move/pallas_call | solution.py:744
Async XLA Ops:
  4.9 10.7 %all-to-all-start = ((f32[8,5,8,128]{3,2,1,0:T(8,128)}), f32[8,5,8,128]{3,2,1,0:T(8,128)S(1)}, u32[]{:S(2)}, u32[]{:S(2)}) async-start(f32[8,5,8,128]{3,2,1,0:T(8,128)} %get-tuple-element.20), calls=%async_computation | async-start | bytes 327680 | tf_op jit(solution)/shard_map/all_to_all | solution.py:728
  10.5 7.9 %collective-permute-start = (f32[5,32,128]{2,1,0:T(8,128)S(1)}, f32[5,32,128]{2,1,0:T(8,128)S(1)}, u32[]{:S(2)}, u32[]{:S(2)}) collective-permute-start(f32[5,32,128]{2,1,0:T(8,128)S(1)} %get-tuple-element.22), channel_id=1, source_target_pairs={{0,32},{32,64},{64,96},{96,128},{128,160},{160,192},{192,224},{224... | collective-permute-start | bytes 245768 | tf_op jit(solution)/shard_map/ppermute | solution.py:724
  11.6 6.7 %collective-permute-start.1 = (f32[5,32,128]{2,1,0:T(8,128)S(1)}, f32[5,32,128]{2,1,0:T(8,128)S(1)}, u32[]{:S(2)}, u32[]{:S(2)}) collective-permute-start(f32[5,32,128]{2,1,0:T(8,128)S(1)} %get-tuple-element.23), channel_id=1, source_target_pairs={{0,224},{32,0},{64,32},{96,64},{128,96},{160,128},{192,160},{224,1... | collective-permute-start | bytes 245768 | tf_op jit(solution)/shard_map/ppermute | solution.py:724
  18.3 20.9 %all-to-all-start.1 = ((f32[32,8,128]{2,1,0:T(8,128)}), f32[32,8,128]{2,1,0:T(8,128)S(1)}, u32[]{:S(2)}, u32[]{:S(2)}) async-start(f32[32,8,128]{2,1,0:T(8,128)} %bins.1), calls=%async_computation.1 | async-start | bytes 262144 | tf_op jit(solution)/shard_map/all_to_all | solution.py:743
  28.7 5.0 %collective-permute-start.2 = (f32[24,128]{1,0:T(8,128)S(1)}, f32[24,128]{1,0:T(8,128)S(1)}, u32[]{:S(2)}, u32[]{:S(2)}) collective-permute-start(f32[24,128]{1,0:T(8,128)S(1)} %get-tuple-element.29), channel_id=1, source_target_pairs={{0,8},{8,16},{16,24},{24,0},{1,9},{9,17},{17,25},{25,1},{2,10},{10... | collective-permute-start | bytes 36872 | tf_op jit(solution)/shard_map/ppermute | solution.py:724
  30.6 3.8 %collective-permute-start.3 = (f32[24,128]{1,0:T(8,128)S(1)}, f32[24,128]{1,0:T(8,128)S(1)}, u32[]{:S(2)}, u32[]{:S(2)}) collective-permute-start(f32[24,128]{1,0:T(8,128)S(1)} %get-tuple-element.30), channel_id=1, source_target_pairs={{0,24},{8,0},{16,8},{24,16},{1,25},{9,1},{17,9},{25,17},{2,26},{10... | collective-permute-start | bytes 36872 | tf_op jit(solution)/shard_map/ppermute | solution.py:724

commit v5 on v4

--- a/solution.py
+++ b/solution.py
@@ -503,7 +503,73 @@
             send_ref[me + step, 7:8, :] = line
 
 
-def third_kernel(
+def arrivals(lines):
+    blank = jnp.zeros((128 - len(lines), 128), F32)
+    return jnp.transpose(jnp.concatenate(lines + [blank], axis=0))
+
+
+def shifted(line, cx, cy):
+    by = 32 * cx + cy
+    return pltpu.roll(line, by % 128, 1) if by else line
+
+
+def finish(block, i, column, code, value):
+    cz = int(lattice_tables()[0][i, 2])
+    if cz:
+        block = pltpu.roll(block, 1 if cz == 1 else 127, 1)
+        at = 0 if cz == 1 else 127
+        block = jnp.where(iota(block.shape, 1) == at, column, block)
+    if i:
+        opposite = i + 1 if i % 2 else i - 1
+        block = jnp.where(code == float(opposite), value, block)
+    return block
+
+
+def third_kernel(post_ref, bounce_ref, got1_ref, xp_ref, xm_ref, moved_hbm, moved_ref, sems):
+    speeds = lattice_tables()[0].astype(int)
+    place_x, place_z = lax.axis_index("gx"), lax.axis_index("gz")
+    has_xp, has_xm = place_x < 7, place_x > 0
+    below = got1_ref[lax.rem(place_z + 7, 8), 4]
+    above = got1_ref[lax.rem(place_z + 1, 8), 4]
+    order = ZP + ZM
+    lines = []
+    for dirs, face in ((ZP, below), (ZM, above)):
+        for n, i in enumerate(dirs):
+            lines.append(shifted(face[n : n + 1], int(speeds[i, 0]), int(speeds[i, 1])))
+    columns = arrivals(lines)
+    copies = []
+    for i in range(19):
+        cx, cy, cz = (int(v) for v in speeds[i])
+        planes = range(4)
+        if cx and cz:
+            planes = range(1, 4) if cx == 1 else range(3)
+        first, last = (8 if cy == 1 else 0), (24 if cy == -1 else 32)
+        for x in planes:
+            source = x - cx
+            rows = slice(first - cy, last - cy)
+            if 0 <= source < 4:
+                block = post_ref[i, 32 * source + rows.start : 32 * source + rows.stop, :]
+            elif source < 0:
+                block = jnp.where(has_xm, xp_ref[XP.index(i), rows, :], 0.0)
+            else:
+                block = jnp.where(has_xp, xm_ref[XM.index(i), rows, :], 0.0)
+            rows = slice(32 * x + first, 32 * x + last)
+            column = None
+            if cz:
+                n = order.index(i)
+                column = columns[rows, n : n + 1]
+            code, value = bounce_ref[0, rows, :], bounce_ref[1, rows, :]
+            moved_ref[i, x, first:last, :] = finish(block, i, column, code, value)
+        part = (i, slice(planes[0], planes[-1] + 1), slice(first, last))
+        copy = pltpu.make_async_copy(moved_ref.at[part], moved_hbm.at[part], sems.at[i])
+        copy.start()
+        copies.append(copy)
+    for copy in copies:
+        copy.wait()
+
+
+def fourth_kernel(
+    partly_hbm,
     post_ref,
     bounce_ref,
     own_ref,
@@ -519,7 +585,8 @@
     moved_hbm,
     load_hbm,
     next_hbm,
-    moved_ref,
+    row_ref,
+    edge_ref,
     load_ref,
     next_ref,
     motion_ref,
@@ -527,18 +594,26 @@
     inertia_ref,
     sems,
 ):
+    del partly_hbm
     speeds = lattice_tables()[0].astype(int)
     place_x, place_y, place_z = (lax.axis_index(a) for a in ("gx", "gy", "gz"))
     has_xp, has_xm = place_x < 7, place_x > 0
     has_yp, has_ym = place_y < 3, place_y > 0
     me = place_x * 4 + place_y
     fetches = [
-        pltpu.make_async_copy(motion_hbm, motion_ref, sems.at[6]),
-        pltpu.make_async_copy(mass_hbm, mass_ref, sems.at[7]),
-        pltpu.make_async_copy(inertia_hbm, inertia_ref, sems.at[8]),
+        pltpu.make_async_copy(motion_hbm, motion_ref, sems.at[0]),
+        pltpu.make_async_copy(mass_hbm, mass_ref, sems.at[1]),
+        pltpu.make_async_copy(inertia_hbm, inertia_ref, sems.at[2]),
     ]
     for fetch in fetches:
         fetch.start()
+    copies = []
+
+    def send(source, target):
+        copy = pltpu.make_async_copy(source, target, sems.at[3 + len(copies)])
+        copy.start()
+        copies.append(copy)
+
     total = got2_ref[0]
     for j in range(1, 32):
         total = total + got2_ref[j]
@@ -546,26 +621,7 @@
     away = cross([own_ref[a : a + 1, :] for a in range(3)], push)
     turn = [total[3 + a : 4 + a] - away[a] for a in range(3)]
     load_ref[...] = jnp.concatenate(push + turn, axis=0)
-    copies = [pltpu.make_async_copy(load_ref, load_hbm, sems.at[4])]
-    copies[0].start()
-
-    def advance():
-        at_lane = iota((8, 128), 1)
-        at_row = iota((8, 128), 0)
-        own = jnp.where((at_lane & 7) == at_row, total[6:7], 0.0)
-        body_load = jnp.zeros((8, 128), F32)
-        scale = jnp.zeros((8, 128), F32)
-        for c in range(6):
-            here = lax.shift_right_logical(at_lane, 3) == c
-            column = jnp.sum(jnp.where(here, own, 0.0), axis=1, keepdims=True)
-            body_load = jnp.where(at_lane == c, column, body_load)
-            for b in range(8):
-                value = mass_ref[b] if c < 3 else inertia_ref[c - 3, b]
-                scale = jnp.where((at_lane == c) & (at_row == b), value, scale)
-        next_ref[...] = motion_ref[...] + (scale * body_load)[:, 0:6] / 32768.0
-        copy = pltpu.make_async_copy(next_ref, next_hbm, sems.at[5])
-        copy.start()
-        copies.append(copy)
+    send(load_ref, load_hbm)
 
     def edge(there, step):
         line = got2_ref[jnp.where(there, me + step, me), 7:8, :]
@@ -581,73 +637,84 @@
         (1, -1): edge(has_xm & has_yp, -3),
         (-1, 1): edge(has_xp & has_ym, 3),
     }
-    entering = {}
+    order, lines = [], []
     for dirs, face in (
         (ZP, got1_ref[lax.rem(place_z + 7, 8), 4]),
         (ZM, got1_ref[lax.rem(place_z + 1, 8), 4]),
     ):
         for n, i in enumerate(dirs):
-            line = face[n : n + 1]
-            cx, cy, cz = (int(s) for s in speeds[i])
+            cx, cy, cz = (int(v) for v in speeds[i])
             if cx == 1:
-                came = from_x[1] if cz == 1 else pltpu.roll(from_x[1], 96, 1)
-                line = jnp.where(lane < 32, came, pltpu.roll(line, 32, 1))
-            if cx == -1:
-                came = pltpu.roll(from_x[-1], 96 if cz == 1 else 64, 1)
-                line = jnp.where(lane >= 96, came, pltpu.roll(line, 96, 1))
-            if cy == 1:
+                line = from_x[1] if cz == 1 else pltpu.roll(from_x[1], 96, 1)
+            elif cx == -1:
+                line = pltpu.roll(from_x[-1], 96 if cz == 1 else 64, 1)
+            elif cy == 1:
                 came = from_y[1] if cz == 1 else pltpu.roll(from_y[1], 127, 1)
-                line = jnp.where(row_in_plane == 0, came, pltpu.roll(line, 1, 1))
-            if cy == -1:
+                line = jnp.where(row_in_plane == 0, came, shifted(face[n : n + 1], 0, 1))
+            elif cy == -1:
                 came = pltpu.roll(from_y[-1], 31 if cz == 1 else 30, 1)
-                line = jnp.where(row_in_plane == 31, came, pltpu.roll(line, 127, 1))
-            entering[i] = line
-    order = ZP + ZM
-    lines = jnp.concatenate(
-        [entering[i] for i in order] + [jnp.zeros((118, 128), F32)], axis=0
-    )
-    columns = jnp.transpose(lines)
-
-    plane_lane = iota((32, 128), 1)
-    plane_row = iota((32, 128), 0)
-    for x in range(4):
-        if x == 2:
-            for fetch in fetches:
-                fetch.wait()
-            advance()
-        rows = slice(32 * x, 32 * x + 32)
-        code = bounce_ref[0, rows, :]
-        value = bounce_ref[1, rows, :]
-        for i in range(19):
-            cx, cy, cz = (int(s) for s in speeds[i])
+                line = jnp.where(row_in_plane == 31, came, shifted(face[n : n + 1], 0, -1))
+            else:
+                continue
+            order.append(i)
+            lines.append(line)
+    columns = arrivals(lines)
+
+    at_row = iota((8, 128), 0)
+    for number, i in enumerate(YP + YM):
+        cx, cy, cz = (int(v) for v in speeds[i])
+        first = 0 if cy == 1 else 24
+        face_ref, n = (yp_ref, YP.index(i)) if cy == 1 else (ym_ref, YM.index(i))
+        for x in range(4):
             source = x - cx
             if 0 <= source < 4:
-                plane = post_ref[i, 32 * source : 32 * source + 32, :]
-            elif source < 0:
-                plane = jnp.where(has_xm, xp_ref[XP.index(i)], 0.0)
+                block = post_ref[i, 32 * source + first : 32 * source + first + 8, :]
+                line = face_ref[4 * n + source : 4 * n + source + 1, :]
+                line = jnp.where(has_ym if cy == 1 else has_yp, line, 0.0)
             else:
-                plane = jnp.where(has_xp, xm_ref[XM.index(i)], 0.0)
-            if cy:
-                if 0 <= source < 4:
-                    face_ref, n = (yp_ref, YP.index(i)) if cy == 1 else (ym_ref, YM.index(i))
-                    line = face_ref[4 * n + source : 4 * n + source + 1, :]
-                    line = jnp.where(has_ym if cy == 1 else has_yp, line, 0.0)
+                if source < 0:
+                    block = jnp.where(has_xm, xp_ref[XP.index(i), first : first + 8, :], 0.0)
                 else:
-                    line = from_xy[cx, cy]
-                plane = pltpu.roll(plane, 1 if cy == 1 else 31, 0)
-                plane = jnp.where(plane_row == (0 if cy == 1 else 31), line, plane)
+                    block = jnp.where(has_xp, xm_ref[XM.index(i), first : first + 8, :], 0.0)
+                line = from_xy[cx, cy]
+            block = pltpu.roll(block, 1 if cy == 1 else 7, 0)
+            block = jnp.where(at_row == (0 if cy == 1 else 7), line, block)
+            rows = slice(32 * x + first, 32 * x + first + 8)
+            column = None
             if cz:
-                n = order.index(i)
-                plane = pltpu.roll(plane, 1 if cz == 1 else 127, 1)
-                at = 0 if cz == 1 else 127
-                plane = jnp.where(plane_lane == at, columns[rows, n : n + 1], plane)
-            if i:
-                opposite = i + 1 if i % 2 else i - 1
-                plane = jnp.where(code == float(opposite), value, plane)
-            moved_ref[i, x] = plane
-        copy = pltpu.make_async_copy(moved_ref.at[:, x], moved_hbm.at[:, x], sems.at[x])
-        copy.start()
-        copies.append(copy)
+                m = order.index(i)
+                column = columns[rows, m : m + 1]
+            code, value = bounce_ref[0, rows, :], bounce_ref[1, rows, :]
+            row_ref[number, x] = finish(block, i, column, code, value)
+        send(row_ref.at[number], moved_hbm.at[i, :, first : first + 8, :])
+    for number, i in enumerate((11, 13, 14, 12)):
+        cx = int(speeds[i, 0])
+        x = 0 if cx == 1 else 3
+        if cx == 1:
+            block = jnp.where(has_xm, xp_ref[XP.index(i)], 0.0)
+        else:
+            block = jnp.where(has_xp, xm_ref[XM.index(i)], 0.0)
+        rows = slice(32 * x, 32 * x + 32)
+        m = order.index(i)
+        code, value = bounce_ref[0, rows, :], bounce_ref[1, rows, :]
+        edge_ref[number] = finish(block, i, columns[rows, m : m + 1], code, value)
+        send(edge_ref.at[number], moved_hbm.at[i, x])
+
+    for fetch in fetches:
+        fetch.wait()
+    at_lane = iota((8, 128), 1)
+    own = jnp.where((at_lane & 7) == at_row, total[6:7], 0.0)
+    body_load = jnp.zeros((8, 128), F32)
+    scale = jnp.zeros((8, 128), F32)
+    for c in range(6):
+        here = lax.shift_right_logical(at_lane, 3) == c
+        column = jnp.sum(jnp.where(here, own, 0.0), axis=1, keepdims=True)
+        body_load = jnp.where(at_lane == c, column, body_load)
+        for b in range(8):
+            value = mass_ref[b] if c < 3 else inertia_ref[c - 3, b]
+            scale = jnp.where((at_lane == c) & (at_row == b), value, scale)
+    next_ref[...] = motion_ref[...] + (scale * body_load)[:, 0:6] / 32768.0
+    send(next_ref, next_hbm)
     for copy in copies:
         copy.wait()
 
@@ -723,8 +790,6 @@
         size = lax.axis_size(axis)
         return lax.ppermute(x, axis, [(i, (i + by) % size) for i in range(size)])
 
-    after = lax.optimization_barrier
-    xp, xm = shift(xp, "gx", 1), shift(xm, "gx", -1)
     got1 = lax.all_to_all(send1, "gz", 0, 0, tiled=True)
     send2 = pl.pallas_call(
         second_kernel,
@@ -738,27 +803,42 @@
         ),
         name="bins",
     )(got1, xy)
-    send2, xp, xm, yp, ym = after((send2, xp, xm, yp, ym))
+    xp, xm = shift(xp, "gx", 1), shift(xm, "gx", -1)
     yp, ym = shift(yp, "gy", 1), shift(ym, "gy", -1)
     got2 = lax.all_to_all(send2, ("gx", "gy"), 0, 0, tiled=True)
+    hbm = pl.BlockSpec(memory_space=pltpu.HBM)
+    partly = pl.pallas_call(
+        third_kernel,
+        out_shape=array(19, 4, 32, 128),
+        in_specs=[vmem] * 5,
+        out_specs=hbm,
+        scratch_shapes=[pltpu.VMEM((19, 4, 32, 128), F32), pltpu.SemaphoreType.DMA((19,))],
+        compiler_params=params,
+        cost_estimate=pl.CostEstimate(
+            flops=19 * 16384 * 4, bytes_accessed=2 * 19 * 16384 * 4, transcendentals=0
+        ),
+        name="move",
+    )(post, bounce, got1, xp, xm)
     moved, own_loads, motion_next = pl.pallas_call(
-        third_kernel,
+        fourth_kernel,
         out_shape=(array(19, 4, 32, 128), array(6, 128), array(8, 6)),
-        in_specs=[vmem] * 9 + [pl.BlockSpec(memory_space=pltpu.HBM)] * 3,
-        out_specs=(pl.BlockSpec(memory_space=pltpu.HBM),) * 3,
+        in_specs=[hbm] + [vmem] * 9 + [hbm] * 3,
+        out_specs=(hbm,) * 3,
         scratch_shapes=[
-            pltpu.VMEM((19, 4, 32, 128), F32),
+            pltpu.VMEM((10, 4, 8, 128), F32),
+            pltpu.VMEM((4, 32, 128), F32),
             pltpu.VMEM((6, 128), F32),
             pltpu.VMEM((8, 6), F32),
             pltpu.VMEM((8, 6), F32),
             pltpu.SMEM((8,), F32),
             pltpu.SMEM((3, 8), F32),
-            pltpu.SemaphoreType.DMA((9,)),
+            pltpu.SemaphoreType.DMA((19,)),
         ],
+        input_output_aliases={0: 0},
         compiler_params=params,
-        name="move",
+        name="close",
     )(
-        *(post, bounce, own, got1, got2, xp, xm, yp, ym),
+        *(partly, post, bounce, own, got1, got2, xp, xm, yp, ym),
         *(
             pltpu.with_memory_space_constraint(x, pltpu.HBM)
             for x in (motion, inv_mass, inv_inertia.T)

time: 41.9 us -> 41.2 us (0.983)
  blocking collectives: 0 us -> 9.69 us
  starting transfers between devices: 24.4 us -> 18 us
  waiting for transfers between devices: 7.48 us -> 3.37 us
    all_to_all x0 -> x1, blocking collectives: none -> 9.69 us  [body(): got1 = lax.all_to_all(send1, 'gz', 0, 0, tiled=True)]
    all_to_all x1 -> x0, starting transfers between devices: 5.57 us -> none  [body(): got1 = lax.all_to_all(send1, 'gz', 0, 0, tiled=True)]
    all_to_all x1, waiting for transfers between devices: 4.88 us -> 2.47 us  [body(): got2 = lax.all_to_all(send2, ('gx', 'gy'), 0, 0, tiled=True)]
    ppermute x4, starting transfers between devices: 8.45 us -> 6.55 us  [shift(): return lax.ppermute(x, axis, [(i, (i + by) % size) for i in range(size)])]
    ppermute x4, waiting for transfers between devices: 2.6 us -> 0.9 us  [shift(): return lax.ppermute(x, axis, [(i, (i + by) % size) for i in range(size)])]
    all_to_all x1, starting transfers between devices: 10.4 us -> 11.5 us  [body(): got2 = lax.all_to_all(send2, ('gx', 'gy'), 0, 0, tiled=True)]
    pallas_call x1 -> x2, Pallas kernels: 2.25 us -> 3.09 us  [the longest x1 1.76 us: body(): pl.pallas_call(fourth_kernel, out_shape=(array(19, 4, 32, 128), array(6,...]
    pallas_call x1, Pallas kernels: 4.24 us -> 3.58 us  [body(): pl.pallas_call(first_kernel, out_shape=(array(19, 128, 128), array(2, 128...]
  transfers between devices with their start and end apart: 6 -> 5, of which waited for: 4 -> 3; matrix products, arithmetic and copies ran while one was open for 0% -> 0% of each run, Pallas kernels for 6% -> 3%
where the time goes in v5:
time: 41.2 us; the launch traced here: 40.9 us
  starting transfers between devices  18 us (44%)
  blocking collectives  9.69 us (24%)
  Pallas kernels  9.15 us (22%)
  waiting for transfers between devices  3.37 us (8%)
  between operations  0.67 us (2%)
    all_to_all x1, starting transfers between devices, body(): got2 = lax.all_to_all(send2, ('gx', 'gy'), 0, 0, tiled=True)  11.5 us
    all_to_all x1, blocking collectives, body(): got1 = lax.all_to_all(send1, 'gz', 0, 0, tiled=True)  9.69 us
    ppermute x4, starting transfers between devices, shift(): return lax.ppermute(x, axis, [(i, (i + by) % size) for i in range(size)])  6.55 us
    pallas_call x1, Pallas kernels, body(): pl.pallas_call(first_kernel, out_shape=(array(19, 128, 128), array(2, 128...  3.58 us
    pallas_call x1, Pallas kernels, body(): pl.pallas_call(second_kernel, out_shape=array(32, 8, 128), in_specs=[vmem...  2.47 us
    all_to_all x1, waiting for transfers between devices, body(): got2 = lax.all_to_all(send2, ('gx', 'gy'), 0, 0, tiled=True)  2.47 us
    pallas_call x1, Pallas kernels, body(): pl.pallas_call(fourth_kernel, out_shape=(array(19, 4, 32, 128), array(6,...  1.76 us
    pallas_call x1, Pallas kernels, body(): pl.pallas_call(third_kernel, out_shape=array(19, 4, 32, 128), in_specs=[v...  1.33 us
  transfers between devices with their start and end apart: 5, of which 3 were waited for; matrix products, arithmetic and copies ran while one was open for 0% of the time, Pallas kernels for 3%

profile of v5, /device:TPU:2, one launch (start us, length us, event | category | flops | bytes accessed | tf_op | source)
XLA Modules:
  0.0 40.9 jit_solution(8152502973738103812)
XLA Ops:
  0.6 3.6 %collide.1 = (f32[19,128,128]{2,1,0:T(8,128)S(1)}, f32[2,128,128]{2,1,0:T(8,128)S(1)}, f32[8,5,8,128]{3,2,1,0:T(8,128)S(1)}, f32[5,32,128]{2,1,0:T(8,128)S(1)}, ...) custom-call(f32[19,128,128]{2,1,0:T(8,128)} %bitcast.8, ...), custom_call_target="tpu_custom_call" | custom-call | tf_op jit(solution)/shard_map/collide/pallas_call | solution.py:741
  4.2 9.7 %all_to_all.10.got1_ref.got_ref = f32[8,5,8,128]{3,2,1,0:T(8,128)S(1)} all-to-all(f32[8,5,8,128]{3,2,1,0:T(8,128)S(1)} %get-tuple-element.14), channel_id=1, replica_groups=mesh['gx'=8,'gy'=4,'gz'=8] {'gz'}, dimensions={0} | all-to-all | bytes 327680 | tf_op jit(solution)/shard_map/all_to_all | solution.py:793
  13.9 2.5 %bins.1 = f32[32,8,128]{2,1,0:T(8,128)} custom-call(f32[8,5,8,128]{3,2,1,0:T(8,128)S(1)} %all_to_all.10.got1_ref.got_ref, f32[8,128]{1,0:T(8,128)S(1)} %get-tuple-element.18.xy_ref), custom_call_target="tpu_custom_call" | custom-call | flops 805306368 | bytes 131072 | tf_op jit(solution)/shard_map/bins/pallas_call | solution.py:794
  16.4 11.5 %all-to-all-start.1 = ((f32[32,8,128]{2,1,0:T(8,128)}), f32[32,8,128]{2,1,0:T(8,128)S(1)}, u32[]{:S(2)}, u32[]{:S(2)}) async-start(f32[32,8,128]{2,1,0:T(8,128)} %bins.1), calls=%async_computation.1 | async-start | bytes 262144 | tf_op jit(solution)/shard_map/all_to_all | solution.py:808
  27.9 1.9 %collective-permute-start = (f32[5,32,128]{2,1,0:T(8,128)S(1)}, f32[5,32,128]{2,1,0:T(8,128)S(1)}, u32[]{:S(2)}, u32[]{:S(2)}) collective-permute-start(f32[5,32,128]{2,1,0:T(8,128)S(1)} %get-tuple-element.15), channel_id=1, source_target_pairs={{0,32},{32,64},{64,96},{96,128},{128,160},{160,192},{192,224},{224... | collective-permute-start | bytes 245768 | tf_op jit(solution)/shard_map/ppermute | solution.py:791
  29.7 1.4 %collective-permute-start.1 = (f32[5,32,128]{2,1,0:T(8,128)S(1)}, f32[5,32,128]{2,1,0:T(8,128)S(1)}, u32[]{:S(2)}, u32[]{:S(2)}) collective-permute-start(f32[5,32,128]{2,1,0:T(8,128)S(1)} %get-tuple-element.16), channel_id=1, source_target_pairs={{0,224},{32,0},{64,32},{96,64},{128,96},{160,128},{192,160},{224,1... | collective-permute-start | bytes 245768 | tf_op jit(solution)/shard_map/ppermute | solution.py:791
  31.2 1.8 %collective-permute-start.2 = (f32[24,128]{1,0:T(8,128)S(1)}, f32[24,128]{1,0:T(8,128)S(1)}, u32[]{:S(2)}, u32[]{:S(2)}) collective-permute-start(f32[24,128]{1,0:T(8,128)S(1)} %get-tuple-element.19), channel_id=1, source_target_pairs={{0,8},{8,16},{16,24},{24,0},{1,9},{9,17},{17,25},{25,1},{2,10},{10... | collective-permute-start | bytes 36872 | tf_op jit(solution)/shard_map/ppermute | solution.py:791
  33.0 1.4 %collective-permute-start.3 = (f32[24,128]{1,0:T(8,128)S(1)}, f32[24,128]{1,0:T(8,128)S(1)}, u32[]{:S(2)}, u32[]{:S(2)}) collective-permute-start(f32[24,128]{1,0:T(8,128)S(1)} %get-tuple-element.20), channel_id=1, source_target_pairs={{0,24},{8,0},{16,8},{24,16},{1,25},{9,1},{17,9},{25,17},{2,26},{10... | collective-permute-start | bytes 36872 | tf_op jit(solution)/shard_map/ppermute | solution.py:791
  34.4 0.8 %collective-permute-done.xp_ref = f32[5,32,128]{2,1,0:T(8,128)S(1)} collective-permute-done((f32[5,32,128]{2,1,0:T(8,128)S(1)}, f32[5,32,128]{2,1,0:T(8,128)S(1)}, u32[]{:S(2)}, u32[]{:S(2)}) %collective-permute-start) | collective-permute-done | bytes 81952 | tf_op jit(solution)/shard_map/ppermute | solution.py:791
  35.2 0.0 collective-permute-done.1.xm_ref
  35.2 1.3 %move.1.partly_hbm = f32[19,4,32,128]{3,2,1,0:T(8,128)} custom-call(f32[19,128,128]{2,1,0:T(8,128)S(1)} %get-tuple-element.12.post_ref, f32[2,128,128]{2,1,0:T(8,128)S(1)} %get-tuple-element.13.bounce_ref, f32[8,5,8,128]{3,2,1,0:T(8,128)S(1)} %all_to_all.10.got1_ref.got_ref, f32[5,32,128]{2,1,0:T(8,128)S(1)} %collective-permute-done.xp_ref, ...), custom_call_target="tpu_custom_call" | custom-call | flops 1245184 | bytes 2490368 | tf_op jit(solution)/shard_map/move/pallas_call | solution.py:810
  36.6 0.0 collective-permute-done.2.yp_ref
  36.6 0.1 collective-permute-done.3.ym_ref
  36.7 2.5 %all-to-all-done.1.got2_ref = f32[32,8,128]{2,1,0:T(8,128)S(1)} async-done(((f32[32,8,128]{2,1,0:T(8,128)}), f32[32,8,128]{2,1,0:T(8,128)S(1)}, u32[]{:S(2)}, u32[]{:S(2)}) %all-to-all-start.1) | async-done | bytes 131104 | tf_op jit(solution)/shard_map/all_to_all | solution.py:808
  39.1 1.8 %close.1 = (f32[19,4,32,128]{3,2,1,0:T(8,128)}, f32[6,128]{1,0:T(8,128)}, f32[8,6]{1,0:T(8,128)}) custom-call(f32[19,4,32,128]{3,2,1,0:T(8,128)} %move.1.partly_hbm, f32[19,128,128]{2,1,0:T(8,128)S(1)} %get-tuple-element.12.post_ref, f32[2,128,128]{2,1,0:T(8,128)S(1)} %get-tuple-element.13.bounce_ref, ...), custom_call_target="tpu_custom_call", output_to_operand_aliasing={{0}: (0, {})} | custom-call | tf_op jit(solution)/shard_map/close/pallas_call | solution.py:822
Async XLA Ops:
  16.4 22.7 %all-to-all-start.1 = ((f32[32,8,128]{2,1,0:T(8,128)}), f32[32,8,128]{2,1,0:T(8,128)S(1)}, u32[]{:S(2)}, u32[]{:S(2)}) async-start(f32[32,8,128]{2,1,0:T(8,128)} %bins.1), calls=%async_computation.1 | async-start | bytes 262144 | tf_op jit(solution)/shard_map/all_to_all | solution.py:808
  27.9 7.4 %collective-permute-start = (f32[5,32,128]{2,1,0:T(8,128)S(1)}, f32[5,32,128]{2,1,0:T(8,128)S(1)}, u32[]{:S(2)}, u32[]{:S(2)}) collective-permute-start(f32[5,32,128]{2,1,0:T(8,128)S(1)} %get-tuple-element.15), channel_id=1, source_target_pairs={{0,32},{32,64},{64,96},{96,128},{128,160},{160,192},{192,224},{224... | collective-permute-start | bytes 245768 | tf_op jit(solution)/shard_map/ppermute | solution.py:791
  29.7 5.5 %collective-permute-start.1 = (f32[5,32,128]{2,1,0:T(8,128)S(1)}, f32[5,32,128]{2,1,0:T(8,128)S(1)}, u32[]{:S(2)}, u32[]{:S(2)}) collective-permute-start(f32[5,32,128]{2,1,0:T(8,128)S(1)} %get-tuple-element.16), channel_id=1, source_target_pairs={{0,224},{32,0},{64,32},{96,64},{128,96},{160,128},{192,160},{224,1... | collective-permute-start | bytes 245768 | tf_op jit(solution)/shard_map/ppermute | solution.py:791
  31.2 5.4 %collective-permute-start.2 = (f32[24,128]{1,0:T(8,128)S(1)}, f32[24,128]{1,0:T(8,128)S(1)}, u32[]{:S(2)}, u32[]{:S(2)}) collective-permute-start(f32[24,128]{1,0:T(8,128)S(1)} %get-tuple-element.19), channel_id=1, source_target_pairs={{0,8},{8,16},{16,24},{24,0},{1,9},{9,17},{17,25},{25,1},{2,10},{10... | collective-permute-start | bytes 36872 | tf_op jit(solution)/shard_map/ppermute | solution.py:791
  33.0 3.7 %collective-permute-start.3 = (f32[24,128]{1,0:T(8,128)S(1)}, f32[24,128]{1,0:T(8,128)S(1)}, u32[]{:S(2)}, u32[]{:S(2)}) collective-permute-start(f32[24,128]{1,0:T(8,128)S(1)} %get-tuple-element.20), channel_id=1, source_target_pairs={{0,24},{8,0},{16,8},{24,16},{1,25},{9,1},{17,9},{25,17},{2,26},{10... | collective-permute-start | bytes 36872 | tf_op jit(solution)/shard_map/ppermute | solution.py:791

commit v6 on v5

--- a/solution.py
+++ b/solution.py
@@ -458,7 +458,7 @@
         )
         return carry
 
-    lax.fori_loop(0, 8, gather, 0, unroll=4)
+    lax.fori_loop(0, 8, gather, 0, unroll=8)
 
     body_row = sum(got_ref[peer, 4, 5:6, :] for peer in range(8))
     for c in range(6):
@@ -525,10 +525,36 @@
     return block
 
 
-def third_kernel(post_ref, bounce_ref, got1_ref, xp_ref, xm_ref, moved_hbm, moved_ref, sems):
+def third_kernel(
+    post_ref,
+    bounce_ref,
+    got1_ref,
+    xp_ref,
+    xm_ref,
+    yp_ref,
+    ym_ref,
+    motion_hbm,
+    mass_hbm,
+    inertia_hbm,
+    moved_hbm,
+    step_ref,
+    moved_ref,
+    motion_ref,
+    mass_ref,
+    inertia_ref,
+    sems,
+):
     speeds = lattice_tables()[0].astype(int)
-    place_x, place_z = lax.axis_index("gx"), lax.axis_index("gz")
+    place_x, place_y, place_z = (lax.axis_index(a) for a in ("gx", "gy", "gz"))
     has_xp, has_xm = place_x < 7, place_x > 0
+    has_yp, has_ym = place_y < 3, place_y > 0
+    fetches = [
+        pltpu.make_async_copy(motion_hbm, motion_ref, sems.at[23]),
+        pltpu.make_async_copy(mass_hbm, mass_ref, sems.at[24]),
+        pltpu.make_async_copy(inertia_hbm, inertia_ref, sems.at[25]),
+    ]
+    for fetch in fetches:
+        fetch.start()
     below = got1_ref[lax.rem(place_z + 7, 8), 4]
     above = got1_ref[lax.rem(place_z + 1, 8), 4]
     order = ZP + ZM
@@ -538,21 +564,37 @@
             lines.append(shifted(face[n : n + 1], int(speeds[i, 0]), int(speeds[i, 1])))
     columns = arrivals(lines)
     copies = []
+
+    def send(*part):
+        copy = pltpu.make_async_copy(
+            moved_ref.at[part], moved_hbm.at[part], sems.at[len(copies)]
+        )
+        copy.start()
+        copies.append(copy)
+
     for i in range(19):
         cx, cy, cz = (int(v) for v in speeds[i])
-        planes = range(4)
-        if cx and cz:
-            planes = range(1, 4) if cx == 1 else range(3)
-        first, last = (8 if cy == 1 else 0), (24 if cy == -1 else 32)
-        for x in planes:
+        for x in range(4):
             source = x - cx
+            outside = not 0 <= source < 4
+            if cx and cz and outside:
+                continue
+            first, last = (1 if cy == 1 else 0), (31 if cy == -1 else 32)
+            if cy and (cz or outside):
+                first, last = (8 if cy == 1 else 0), (24 if cy == -1 else 32)
             rows = slice(first - cy, last - cy)
-            if 0 <= source < 4:
+            if not outside:
                 block = post_ref[i, 32 * source + rows.start : 32 * source + rows.stop, :]
             elif source < 0:
                 block = jnp.where(has_xm, xp_ref[XP.index(i), rows, :], 0.0)
             else:
                 block = jnp.where(has_xp, xm_ref[XM.index(i), rows, :], 0.0)
+            if cy and not (cz or outside):
+                face_ref, n = (yp_ref, YP.index(i)) if cy == 1 else (ym_ref, YM.index(i))
+                line = face_ref[4 * n + source : 4 * n + source + 1, :]
+                line = jnp.where(has_ym if cy == 1 else has_yp, line, 0.0)
+                block = jnp.concatenate([line, block] if cy == 1 else [block, line], axis=0)
+                first, last = 0, 32
             rows = slice(32 * x + first, 32 * x + last)
             column = None
             if cz:
@@ -560,10 +602,26 @@
                 column = columns[rows, n : n + 1]
             code, value = bounce_ref[0, rows, :], bounce_ref[1, rows, :]
             moved_ref[i, x, first:last, :] = finish(block, i, column, code, value)
-        part = (i, slice(planes[0], planes[-1] + 1), slice(first, last))
-        copy = pltpu.make_async_copy(moved_ref.at[part], moved_hbm.at[part], sems.at[i])
-        copy.start()
-        copies.append(copy)
+        planes = {0: slice(0, 4), 1: slice(1, 4), -1: slice(0, 3)}[cx if cy or cz else 0]
+        rows = slice(0, 32)
+        if cy and cz:
+            rows = slice(8, 32) if cy == 1 else slice(0, 24)
+        send(i, planes, rows)
+        if cx and cy:
+            rows = slice(8, 32) if cy == 1 else slice(0, 24)
+            x = 0 if cx == 1 else 3
+            send(i, slice(x, x + 1), rows)
+
+    for fetch in fetches:
+        fetch.wait()
+    at_lane, at_row = iota((8, 128), 1), iota((8, 128), 0)
+    scale = jnp.zeros((8, 128), F32)
+    for c in range(6):
+        for b in range(8):
+            value = mass_ref[b] if c < 3 else inertia_ref[c - 3, b]
+            scale = jnp.where((at_lane == c) & (at_row == b), value, scale)
+    step_ref[0] = scale
+    step_ref[1] = jnp.concatenate([motion_ref[...], jnp.zeros((8, 122), F32)], axis=1)
     for copy in copies:
         copy.wait()
 
@@ -579,9 +637,7 @@
     xm_ref,
     yp_ref,
     ym_ref,
-    motion_hbm,
-    mass_hbm,
-    inertia_hbm,
+    step_ref,
     moved_hbm,
     load_hbm,
     next_hbm,
@@ -589,9 +645,6 @@
     edge_ref,
     load_ref,
     next_ref,
-    motion_ref,
-    mass_ref,
-    inertia_ref,
     sems,
 ):
     del partly_hbm
@@ -600,28 +653,31 @@
     has_xp, has_xm = place_x < 7, place_x > 0
     has_yp, has_ym = place_y < 3, place_y > 0
     me = place_x * 4 + place_y
-    fetches = [
-        pltpu.make_async_copy(motion_hbm, motion_ref, sems.at[0]),
-        pltpu.make_async_copy(mass_hbm, mass_ref, sems.at[1]),
-        pltpu.make_async_copy(inertia_hbm, inertia_ref, sems.at[2]),
-    ]
-    for fetch in fetches:
-        fetch.start()
     copies = []
 
     def send(source, target):
-        copy = pltpu.make_async_copy(source, target, sems.at[3 + len(copies)])
+        copy = pltpu.make_async_copy(source, target, sems.at[len(copies)])
         copy.start()
         copies.append(copy)
 
-    total = got2_ref[0]
-    for j in range(1, 32):
-        total = total + got2_ref[j]
+    parts = [got2_ref[j] for j in range(32)]
+    while len(parts) > 1:
+        parts = [a + b for a, b in zip(parts[0::2], parts[1::2])]
+    total = parts[0]
     push = [total[a : a + 1] for a in range(3)]
     away = cross([own_ref[a : a + 1, :] for a in range(3)], push)
     turn = [total[3 + a : 4 + a] - away[a] for a in range(3)]
     load_ref[...] = jnp.concatenate(push + turn, axis=0)
     send(load_ref, load_hbm)
+    at_lane, at_row = iota((8, 128), 1), iota((8, 128), 0)
+    own = jnp.where((at_lane & 7) == at_row, total[6:7], 0.0)
+    body_load = jnp.zeros((8, 128), F32)
+    for c in range(6):
+        here = lax.shift_right_logical(at_lane, 3) == c
+        column = jnp.sum(jnp.where(here, own, 0.0), axis=1, keepdims=True)
+        body_load = jnp.where(at_lane == c, column, body_load)
+    next_ref[...] = (step_ref[1] + step_ref[0] * body_load / 32768.0)[:, 0:6]
+    send(next_ref, next_hbm)
 
     def edge(there, step):
         line = got2_ref[jnp.where(there, me + step, me), 7:8, :]
@@ -660,14 +716,14 @@
             lines.append(line)
     columns = arrivals(lines)
 
-    at_row = iota((8, 128), 0)
-    for number, i in enumerate(YP + YM):
+    for i in (7, 9, 8, 10, 15, 17, 16, 18):
         cx, cy, cz = (int(v) for v in speeds[i])
         first = 0 if cy == 1 else 24
         face_ref, n = (yp_ref, YP.index(i)) if cy == 1 else (ym_ref, YM.index(i))
-        for x in range(4):
+        planes = range(4) if cz else ((0,) if cx == 1 else (3,))
+        for x in planes:
             source = x - cx
-            if 0 <= source < 4:
+            if cz:
                 block = post_ref[i, 32 * source + first : 32 * source + first + 8, :]
                 line = face_ref[4 * n + source : 4 * n + source + 1, :]
                 line = jnp.where(has_ym if cy == 1 else has_yp, line, 0.0)
@@ -685,8 +741,9 @@
                 m = order.index(i)
                 column = columns[rows, m : m + 1]
             code, value = bounce_ref[0, rows, :], bounce_ref[1, rows, :]
-            row_ref[number, x] = finish(block, i, column, code, value)
-        send(row_ref.at[number], moved_hbm.at[i, :, first : first + 8, :])
+            row_ref[i - 7, x] = finish(block, i, column, code, value)
+        part = slice(planes[0], planes[-1] + 1)
+        send(row_ref.at[i - 7, part], moved_hbm.at[i, part, first : first + 8, :])
     for number, i in enumerate((11, 13, 14, 12)):
         cx = int(speeds[i, 0])
         x = 0 if cx == 1 else 3
@@ -700,21 +757,6 @@
         edge_ref[number] = finish(block, i, columns[rows, m : m + 1], code, value)
         send(edge_ref.at[number], moved_hbm.at[i, x])
 
-    for fetch in fetches:
-        fetch.wait()
-    at_lane = iota((8, 128), 1)
-    own = jnp.where((at_lane & 7) == at_row, total[6:7], 0.0)
-    body_load = jnp.zeros((8, 128), F32)
-    scale = jnp.zeros((8, 128), F32)
-    for c in range(6):
-        here = lax.shift_right_logical(at_lane, 3) == c
-        column = jnp.sum(jnp.where(here, own, 0.0), axis=1, keepdims=True)
-        body_load = jnp.where(at_lane == c, column, body_load)
-        for b in range(8):
-            value = mass_ref[b] if c < 3 else inertia_ref[c - 3, b]
-            scale = jnp.where((at_lane == c) & (at_row == b), value, scale)
-    next_ref[...] = motion_ref[...] + (scale * body_load)[:, 0:6] / 32768.0
-    send(next_ref, next_hbm)
     for copy in copies:
         copy.wait()
 
@@ -807,43 +849,46 @@
     yp, ym = shift(yp, "gy", 1), shift(ym, "gy", -1)
     got2 = lax.all_to_all(send2, ("gx", "gy"), 0, 0, tiled=True)
     hbm = pl.BlockSpec(memory_space=pltpu.HBM)
-    partly = pl.pallas_call(
+    partly, step = pl.pallas_call(
         third_kernel,
-        out_shape=array(19, 4, 32, 128),
-        in_specs=[vmem] * 5,
-        out_specs=hbm,
-        scratch_shapes=[pltpu.VMEM((19, 4, 32, 128), F32), pltpu.SemaphoreType.DMA((19,))],
+        out_shape=(array(19, 4, 32, 128), array(2, 8, 128)),
+        in_specs=[vmem] * 7 + [hbm] * 3,
+        out_specs=(hbm, vmem),
+        scratch_shapes=[
+            pltpu.VMEM((19, 4, 32, 128), F32),
+            pltpu.VMEM((8, 6), F32),
+            pltpu.SMEM((8,), F32),
+            pltpu.SMEM((3, 8), F32),
+            pltpu.SemaphoreType.DMA((26,)),
+        ],
         compiler_params=params,
         cost_estimate=pl.CostEstimate(
             flops=19 * 16384 * 4, bytes_accessed=2 * 19 * 16384 * 4, transcendentals=0
         ),
         name="move",
-    )(post, bounce, got1, xp, xm)
-    moved, own_loads, motion_next = pl.pallas_call(
-        fourth_kernel,
-        out_shape=(array(19, 4, 32, 128), array(6, 128), array(8, 6)),
-        in_specs=[hbm] + [vmem] * 9 + [hbm] * 3,
-        out_specs=(hbm,) * 3,
-        scratch_shapes=[
-            pltpu.VMEM((10, 4, 8, 128), F32),
-            pltpu.VMEM((4, 32, 128), F32),
-            pltpu.VMEM((6, 128), F32),
-            pltpu.VMEM((8, 6), F32),
-            pltpu.VMEM((8, 6), F32),
-            pltpu.SMEM((8,), F32),
-            pltpu.SMEM((3, 8), F32),
-            pltpu.SemaphoreType.DMA((19,)),
-        ],
-        input_output_aliases={0: 0},
-        compiler_params=params,
-        name="close",
     )(
-        *(partly, post, bounce, own, got1, got2, xp, xm, yp, ym),
+        *(post, bounce, got1, xp, xm, yp, ym),
         *(
             pltpu.with_memory_space_constraint(x, pltpu.HBM)
             for x in (motion, inv_mass, inv_inertia.T)
         ),
     )
+    moved, own_loads, motion_next = pl.pallas_call(
+        fourth_kernel,
+        out_shape=(array(19, 4, 32, 128), array(6, 128), array(8, 6)),
+        in_specs=[hbm] + [vmem] * 10,
+        out_specs=(hbm,) * 3,
+        scratch_shapes=[
+            pltpu.VMEM((12, 4, 8, 128), F32),
+            pltpu.VMEM((4, 32, 128), F32),
+            pltpu.VMEM((6, 128), F32),
+            pltpu.VMEM((8, 6), F32),
+            pltpu.SemaphoreType.DMA((14,)),
+        ],
+        input_output_aliases={0: 0},
+        compiler_params=params,
+        name="close",
+    )(partly, post, bounce, own, got1, got2, xp, xm, yp, ym, step)
     return (moved, own_loads, motion_next)
 
 

time: 41.2 us -> 40.2 us (0.976)
  Pallas kernels: 9.15 us -> 8.3 us
    all_to_all x1, waiting for transfers between devices: 2.47 us -> 1.02 us  [body(): got2 = lax.all_to_all(send2, ('gx', 'gy'), 0, 0, tiled=True)]
    ppermute x4, waiting for transfers between devices: 0.9 us -> 2.25 us  [shift(): return lax.ppermute(x, axis, [(i, (i + by) % size) for i in range(size)])]
    pallas_call x1, Pallas kernels: 1.76 us -> 1.06 us  [body(): pl.pallas_call(fourth_kernel, out_shape=(array(19, 4, 32, 128), array(6,...]
  transfers between devices with their start and end apart: 5 -> 5, of which waited for: 3 -> 3; matrix products, arithmetic and copies ran while one was open for 0% -> 0% of each run, Pallas kernels for 3% -> 4%
where the time goes in v6:
time: 40.2 us; the launch traced here: 39.9 us
  starting transfers between devices  18 us (45%)
  blocking collectives  9.69 us (24%)
  Pallas kernels  8.3 us (21%)
  waiting for transfers between devices  3.28 us (8%)
  between operations  0.66 us (2%)
    all_to_all x1, starting transfers between devices, body(): got2 = lax.all_to_all(send2, ('gx', 'gy'), 0, 0, tiled=True)  11.5 us
    all_to_all x1, blocking collectives, body(): got1 = lax.all_to_all(send1, 'gz', 0, 0, tiled=True)  9.69 us
    ppermute x4, starting transfers between devices, shift(): return lax.ppermute(x, axis, [(i, (i + by) % size) for i in range(size)])  6.55 us
    pallas_call x1, Pallas kernels, body(): pl.pallas_call(first_kernel, out_shape=(array(19, 128, 128), array(2, 128...  3.58 us
    ppermute x4, waiting for transfers between devices, shift(): return lax.ppermute(x, axis, [(i, (i + by) % size) for i in range(size)])  2.25 us
    pallas_call x1, Pallas kernels, body(): pl.pallas_call(second_kernel, out_shape=array(32, 8, 128), in_specs=[vmem...  2.24 us
    pallas_call x1, Pallas kernels, body(): pl.pallas_call(third_kernel, out_shape=(array(19, 4, 32, 128), array(2, 8...  1.43 us
    pallas_call x1, Pallas kernels, body(): pl.pallas_call(fourth_kernel, out_shape=(array(19, 4, 32, 128), array(6,...  1.06 us
  transfers between devices with their start and end apart: 5, of which 3 were waited for; matrix products, arithmetic and copies ran while one was open for 0% of the time, Pallas kernels for 4%

profile of v6, /device:TPU:2, one launch (start us, length us, event | category | flops | bytes accessed | tf_op | source)
XLA Modules:
  0.0 39.9 jit_solution(17614690882622691682)
XLA Ops:
  0.6 3.6 %collide.1 = (f32[19,128,128]{2,1,0:T(8,128)S(1)}, f32[2,128,128]{2,1,0:T(8,128)S(1)}, f32[8,5,8,128]{3,2,1,0:T(8,128)S(1)}, f32[5,32,128]{2,1,0:T(8,128)S(1)}, ...) custom-call(f32[19,128,128]{2,1,0:T(8,128)} %bitcast.8, ...), custom_call_target="tpu_custom_call" | custom-call | tf_op jit(solution)/shard_map/collide/pallas_call | solution.py:783
  4.2 9.7 %all_to_all.10.got1_ref.got_ref = f32[8,5,8,128]{3,2,1,0:T(8,128)S(1)} all-to-all(f32[8,5,8,128]{3,2,1,0:T(8,128)S(1)} %get-tuple-element.16), channel_id=1, replica_groups=mesh['gx'=8,'gy'=4,'gz'=8] {'gz'}, dimensions={0} | all-to-all | bytes 327680 | tf_op jit(solution)/shard_map/all_to_all | solution.py:835
  13.9 2.2 %bins.1 = f32[32,8,128]{2,1,0:T(8,128)} custom-call(f32[8,5,8,128]{3,2,1,0:T(8,128)S(1)} %all_to_all.10.got1_ref.got_ref, f32[8,128]{1,0:T(8,128)S(1)} %get-tuple-element.23.xy_ref), custom_call_target="tpu_custom_call" | custom-call | flops 805306368 | bytes 131072 | tf_op jit(solution)/shard_map/bins/pallas_call | solution.py:836
  16.1 11.5 %all-to-all-start.1 = ((f32[32,8,128]{2,1,0:T(8,128)}), f32[32,8,128]{2,1,0:T(8,128)S(1)}, u32[]{:S(2)}, u32[]{:S(2)}) async-start(f32[32,8,128]{2,1,0:T(8,128)} %bins.1), calls=%async_computation.1 | async-start | bytes 262144 | tf_op jit(solution)/shard_map/all_to_all | solution.py:850
  27.6 1.9 %collective-permute-start = (f32[5,32,128]{2,1,0:T(8,128)S(1)}, f32[5,32,128]{2,1,0:T(8,128)S(1)}, u32[]{:S(2)}, u32[]{:S(2)}) collective-permute-start(f32[5,32,128]{2,1,0:T(8,128)S(1)} %get-tuple-element.17), channel_id=1, source_target_pairs={{0,32},{32,64},{64,96},{96,128},{128,160},{160,192},{192,224},{224... | collective-permute-start | bytes 245768 | tf_op jit(solution)/shard_map/ppermute | solution.py:833
  29.5 1.4 %collective-permute-start.1 = (f32[5,32,128]{2,1,0:T(8,128)S(1)}, f32[5,32,128]{2,1,0:T(8,128)S(1)}, u32[]{:S(2)}, u32[]{:S(2)}) collective-permute-start(f32[5,32,128]{2,1,0:T(8,128)S(1)} %get-tuple-element.18), channel_id=1, source_target_pairs={{0,224},{32,0},{64,32},{96,64},{128,96},{160,128},{192,160},{224,1... | collective-permute-start | bytes 245768 | tf_op jit(solution)/shard_map/ppermute | solution.py:833
  30.9 1.8 %collective-permute-start.2 = (f32[24,128]{1,0:T(8,128)S(1)}, f32[24,128]{1,0:T(8,128)S(1)}, u32[]{:S(2)}, u32[]{:S(2)}) collective-permute-start(f32[24,128]{1,0:T(8,128)S(1)} %get-tuple-element.19), channel_id=1, source_target_pairs={{0,8},{8,16},{16,24},{24,0},{1,9},{9,17},{17,25},{25,1},{2,10},{10... | collective-permute-start | bytes 36872 | tf_op jit(solution)/shard_map/ppermute | solution.py:833
  32.7 1.4 %collective-permute-start.3 = (f32[24,128]{1,0:T(8,128)S(1)}, f32[24,128]{1,0:T(8,128)S(1)}, u32[]{:S(2)}, u32[]{:S(2)}) collective-permute-start(f32[24,128]{1,0:T(8,128)S(1)} %get-tuple-element.20), channel_id=1, source_target_pairs={{0,24},{8,0},{16,8},{24,16},{1,25},{9,1},{17,9},{25,17},{2,26},{10... | collective-permute-start | bytes 36872 | tf_op jit(solution)/shard_map/ppermute | solution.py:833
  34.2 1.8 %collective-permute-done.2.yp_ref = f32[24,128]{1,0:T(8,128)S(1)} collective-permute-done((f32[24,128]{1,0:T(8,128)S(1)}, f32[24,128]{1,0:T(8,128)S(1)}, u32[]{:S(2)}, u32[]{:S(2)}) %collective-permute-start.2) | collective-permute-done | bytes 12320 | tf_op jit(solution)/shard_map/ppermute | solution.py:833
  35.9 0.5 %collective-permute-done.3.ym_ref = f32[24,128]{1,0:T(8,128)S(1)} collective-permute-done((f32[24,128]{1,0:T(8,128)S(1)}, f32[24,128]{1,0:T(8,128)S(1)}, u32[]{:S(2)}, u32[]{:S(2)}) %collective-permute-start.3) | collective-permute-done | bytes 12320 | tf_op jit(solution)/shard_map/ppermute | solution.py:833
  36.4 0.0 collective-permute-done.xp_ref
  36.4 0.0 collective-permute-done.1.xm_ref
  36.4 1.4 %move.1 = (f32[19,4,32,128]{3,2,1,0:T(8,128)}, f32[2,8,128]{2,1,0:T(8,128)S(1)}) custom-call(f32[19,128,128]{2,1,0:T(8,128)S(1)} %get-tuple-element.14.post_ref, f32[2,128,128]{2,1,0:T(8,128)S(1)} %get-tuple-element.15.bounce_ref, f32[8,5,8,128]{3,2,1,0:T(8,128)S(1)} %all_to_all.10.got1_ref.got_ref, f32[5,32,128]{2,1,0:T(8,128)S(1)} %collective-permute-done.xp_ref, ...), custom_call_target="tpu_custom_call" | custom-call | flops 1245184 | bytes 2490368 | tf_op jit(solution)/shard_map/move/pallas_call | solution.py:852
  37.9 1.0 %all-to-all-done.1.got2_ref = f32[32,8,128]{2,1,0:T(8,128)S(1)} async-done(((f32[32,8,128]{2,1,0:T(8,128)}), f32[32,8,128]{2,1,0:T(8,128)S(1)}, u32[]{:S(2)}, u32[]{:S(2)}) %all-to-all-start.1) | async-done | bytes 131104 | tf_op jit(solution)/shard_map/all_to_all | solution.py:850
  38.9 1.1 %close.1 = (f32[19,4,32,128]{3,2,1,0:T(8,128)}, f32[6,128]{1,0:T(8,128)}, f32[8,6]{1,0:T(8,128)}) custom-call(f32[19,4,32,128]{3,2,1,0:T(8,128)} %get-tuple-element.21.partly_hbm, f32[19,128,128]{2,1,0:T(8,128)S(1)} %get-tuple-element.14.post_ref, f32[2,128,128]{2,1,0:T(8,128)S(1)} %get-tuple-element.15.bounce_ref, ...), custom_call_target="tpu_custom_call", output_to_operand_aliasing={{0}: (0, {})} | custom-call | tf_op jit(solution)/shard_map/close/pallas_call | solution.py:876
Async XLA Ops:
  16.1 22.7 %all-to-all-start.1 = ((f32[32,8,128]{2,1,0:T(8,128)}), f32[32,8,128]{2,1,0:T(8,128)S(1)}, u32[]{:S(2)}, u32[]{:S(2)}) async-start(f32[32,8,128]{2,1,0:T(8,128)} %bins.1), calls=%async_computation.1 | async-start | bytes 262144 | tf_op jit(solution)/shard_map/all_to_all | solution.py:850
  27.6 8.8 %collective-permute-start = (f32[5,32,128]{2,1,0:T(8,128)S(1)}, f32[5,32,128]{2,1,0:T(8,128)S(1)}, u32[]{:S(2)}, u32[]{:S(2)}) collective-permute-start(f32[5,32,128]{2,1,0:T(8,128)S(1)} %get-tuple-element.17), channel_id=1, source_target_pairs={{0,32},{32,64},{64,96},{96,128},{128,160},{160,192},{192,224},{224... | collective-permute-start | bytes 245768 | tf_op jit(solution)/shard_map/ppermute | solution.py:833
  29.5 6.9 %collective-permute-start.1 = (f32[5,32,128]{2,1,0:T(8,128)S(1)}, f32[5,32,128]{2,1,0:T(8,128)S(1)}, u32[]{:S(2)}, u32[]{:S(2)}) collective-permute-start(f32[5,32,128]{2,1,0:T(8,128)S(1)} %get-tuple-element.18), channel_id=1, source_target_pairs={{0,224},{32,0},{64,32},{96,64},{128,96},{160,128},{192,160},{224,1... | collective-permute-start | bytes 245768 | tf_op jit(solution)/shard_map/ppermute | solution.py:833
  30.9 5.0 %collective-permute-start.2 = (f32[24,128]{1,0:T(8,128)S(1)}, f32[24,128]{1,0:T(8,128)S(1)}, u32[]{:S(2)}, u32[]{:S(2)}) collective-permute-start(f32[24,128]{1,0:T(8,128)S(1)} %get-tuple-element.19), channel_id=1, source_target_pairs={{0,8},{8,16},{16,24},{24,0},{1,9},{9,17},{17,25},{25,1},{2,10},{10... | collective-permute-start | bytes 36872 | tf_op jit(solution)/shard_map/ppermute | solution.py:833
  32.7 3.7 %collective-permute-start.3 = (f32[24,128]{1,0:T(8,128)S(1)}, f32[24,128]{1,0:T(8,128)S(1)}, u32[]{:S(2)}, u32[]{:S(2)}) collective-permute-start(f32[24,128]{1,0:T(8,128)S(1)} %get-tuple-element.20), channel_id=1, source_target_pairs={{0,24},{8,0},{16,8},{24,16},{1,25},{9,1},{17,9},{25,17},{2,26},{10... | collective-permute-start | bytes 36872 | tf_op jit(solution)/shard_map/ppermute | solution.py:833

commit v7 on v6

--- a/solution.py
+++ b/solution.py
@@ -206,6 +206,19 @@
     return [a[(i + 1) % 3] * b[(i + 2) % 3] - a[(i + 2) % 3] * b[(i + 1) % 3] for i in range(3)]
 
 
+def groups(index, value):
+    index = jnp.broadcast_to(index.astype(F32), value.shape).astype(BF16)
+    none = jnp.zeros_like(value)
+    return [
+        jnp.where(index == (iota(value.shape, 0) + 16 * g).astype(F32).astype(BF16), value, none)
+        for g in range(8)
+    ]
+
+
+def hot(index):
+    return jnp.concatenate(groups(index, jnp.ones((16, index.shape[1]), BF16)), axis=0)
+
+
 def iota(shape, dim):
     return lax.broadcasted_iota(I32, shape, dim)
 
@@ -238,6 +251,7 @@
     ym_ref,
     xy_ref,
     own_ref,
+    wall_ref,
     pop_ref,
     solid_ref,
     cell_ref,
@@ -247,7 +261,6 @@
     motion_ref,
     centre_ref,
     rates_ref,
-    picked_ref,
     pop_sem,
     sems,
 ):
@@ -285,19 +298,6 @@
     row = lax.shift_right_logical(cell, 7)
     lane = cell & 127
     flat_row = flat(row)
-    one = jnp.ones((16, links), BF16)
-    none = jnp.zeros((16, links), BF16)
-
-    def groups(index, value):
-        index = jnp.broadcast_to(index.astype(F32), (16, links)).astype(BF16)
-        return [
-            jnp.where(index == (iota((16, links), 0) + 16 * g).astype(F32).astype(BF16), value, none)
-            for g in range(8)
-        ]
-
-    def hot(index):
-        return jnp.concatenate(groups(index, one), axis=0)
-
     flat_lane = flat(lane)
     rows_hot16 = hot(flat_row)
     lanes_hot16 = hot(flat_lane)
@@ -328,14 +328,11 @@
     spin = cross(move[3:], radius)
     normal = sum(speed[a] * (move[a] + spin[a]) for a in range(3))
     wall = 6.0 * weight * normal
-    coded = jnp.where(live, direction, 0).astype(F32)
-    spread = []
-    for value in (coded, *halves(wall)):
-        value = jnp.broadcast_to(flat(value.astype(F32)), (16, links)).astype(BF16)
-        spread += groups(flat_lane, value)
-    laid = rows_dot(rows_hot16, jnp.concatenate(spread, axis=0))
-    bounce_ref[0] = laid[:, 0:128]
-    bounce_ref[1] = laid[:, 128:256] + laid[:, 256:384]
+    wall_ref[...] = wall
+    coded = flat(jnp.where(live, direction, 0).astype(F32))
+    coded = jnp.broadcast_to(coded, (16, links)).astype(BF16)
+    spread = jnp.concatenate(groups(flat_lane, coded), axis=0)
+    bounce_ref[0] = rows_dot(rows_hot16, spread)
 
     k = collision_scalars(lambda i: rates_ref[i])
 
@@ -355,8 +352,7 @@
             post_ref[i, rows, :] = post[i]
             if i:
                 found = jnp.where(code == float(i), post[i], found)
-        picked_ref[rows, :] = found
-        bounce_ref[1, rows, :] = found - bounce_ref[1, rows, :]
+        bounce_ref[1, rows, :] = found
         return carry
 
     lax.fori_loop(0, 16, block, 0, unroll=2)
@@ -381,7 +377,7 @@
     xy_ref[2:3, :] = post_ref[9, 96:97, :]
     xy_ref[3:4, :] = post_ref[10, 31:32, :]
 
-    found_high, found_low = halves(picked_ref[...])
+    found_high, found_low = halves(bounce_ref[1])
     by_row = jnp.dot(
         jnp.concatenate([found_high, found_low], axis=0), lanes_hot16, preferred_element_type=F32
     )
@@ -528,33 +524,41 @@
 def third_kernel(
     post_ref,
     bounce_ref,
+    wall_ref,
     got1_ref,
-    xp_ref,
-    xm_ref,
-    yp_ref,
-    ym_ref,
     motion_hbm,
     mass_hbm,
     inertia_hbm,
+    cell_hbm,
     moved_hbm,
+    value_ref,
     step_ref,
     moved_ref,
+    cell_ref,
     motion_ref,
     mass_ref,
     inertia_ref,
     sems,
 ):
     speeds = lattice_tables()[0].astype(int)
-    place_x, place_y, place_z = (lax.axis_index(a) for a in ("gx", "gy", "gz"))
-    has_xp, has_xm = place_x < 7, place_x > 0
-    has_yp, has_ym = place_y < 3, place_y > 0
+    place_z = lax.axis_index("gz")
     fetches = [
-        pltpu.make_async_copy(motion_hbm, motion_ref, sems.at[23]),
-        pltpu.make_async_copy(mass_hbm, mass_ref, sems.at[24]),
-        pltpu.make_async_copy(inertia_hbm, inertia_ref, sems.at[25]),
+        pltpu.make_async_copy(motion_hbm, motion_ref, sems.at[19]),
+        pltpu.make_async_copy(mass_hbm, mass_ref, sems.at[20]),
+        pltpu.make_async_copy(inertia_hbm, inertia_ref, sems.at[21]),
     ]
+    cells = pltpu.make_async_copy(cell_hbm, cell_ref, sems.at[22])
+    cells.start()
     for fetch in fetches:
         fetch.start()
+    cells.wait()
+    cell = flat(cell_ref[...])
+    spread = []
+    for part in halves(wall_ref[...]):
+        part = jnp.broadcast_to(flat(part.astype(F32)), (16, 1024)).astype(BF16)
+        spread += groups(cell & 127, part)
+    laid = rows_dot(hot(lax.shift_right_logical(cell, 7)), jnp.concatenate(spread, axis=0))
+    value_ref[...] = bounce_ref[1] - (laid[:, 0:128] + laid[:, 128:256])
     below = got1_ref[lax.rem(place_z + 7, 8), 4]
     above = got1_ref[lax.rem(place_z + 1, 8), 4]
     order = ZP + ZM
@@ -564,53 +568,24 @@
             lines.append(shifted(face[n : n + 1], int(speeds[i, 0]), int(speeds[i, 1])))
     columns = arrivals(lines)
     copies = []
-
-    def send(*part):
-        copy = pltpu.make_async_copy(
-            moved_ref.at[part], moved_hbm.at[part], sems.at[len(copies)]
-        )
-        copy.start()
-        copies.append(copy)
-
     for i in range(19):
         cx, cy, cz = (int(v) for v in speeds[i])
-        for x in range(4):
-            source = x - cx
-            outside = not 0 <= source < 4
-            if cx and cz and outside:
-                continue
-            first, last = (1 if cy == 1 else 0), (31 if cy == -1 else 32)
-            if cy and (cz or outside):
-                first, last = (8 if cy == 1 else 0), (24 if cy == -1 else 32)
-            rows = slice(first - cy, last - cy)
-            if not outside:
-                block = post_ref[i, 32 * source + rows.start : 32 * source + rows.stop, :]
-            elif source < 0:
-                block = jnp.where(has_xm, xp_ref[XP.index(i), rows, :], 0.0)
-            else:
-                block = jnp.where(has_xp, xm_ref[XM.index(i), rows, :], 0.0)
-            if cy and not (cz or outside):
-                face_ref, n = (yp_ref, YP.index(i)) if cy == 1 else (ym_ref, YM.index(i))
-                line = face_ref[4 * n + source : 4 * n + source + 1, :]
-                line = jnp.where(has_ym if cy == 1 else has_yp, line, 0.0)
-                block = jnp.concatenate([line, block] if cy == 1 else [block, line], axis=0)
-                first, last = 0, 32
+        planes = {0: (0, 4), 1: (1, 4), -1: (0, 3)}[cx]
+        first, last = {0: (0, 32), 1: (8, 32), -1: (0, 24)}[cy]
+        for x in range(*planes):
+            source = 32 * (x - cx) - cy
+            block = post_ref[i, source + first : source + last, :]
             rows = slice(32 * x + first, 32 * x + last)
             column = None
             if cz:
                 n = order.index(i)
                 column = columns[rows, n : n + 1]
-            code, value = bounce_ref[0, rows, :], bounce_ref[1, rows, :]
+            code, value = bounce_ref[0, rows, :], value_ref[rows, :]
             moved_ref[i, x, first:last, :] = finish(block, i, column, code, value)
-        planes = {0: slice(0, 4), 1: slice(1, 4), -1: slice(0, 3)}[cx if cy or cz else 0]
-        rows = slice(0, 32)
-        if cy and cz:
-            rows = slice(8, 32) if cy == 1 else slice(0, 24)
-        send(i, planes, rows)
-        if cx and cy:
-            rows = slice(8, 32) if cy == 1 else slice(0, 24)
-            x = 0 if cx == 1 else 3
-            send(i, slice(x, x + 1), rows)
+        part = (i, slice(*planes), slice(first, last))
+        copy = pltpu.make_async_copy(moved_ref.at[part], moved_hbm.at[part], sems.at[i])
+        copy.start()
+        copies.append(copy)
 
     for fetch in fetches:
         fetch.wait()
@@ -626,10 +601,69 @@
         copy.wait()
 
 
+def face_kernel(
+    partly_hbm,
+    post_ref,
+    bounce_ref,
+    value_ref,
+    xp_ref,
+    xm_ref,
+    yp_ref,
+    ym_ref,
+    moved_hbm,
+    moved_ref,
+    sems,
+):
+    del partly_hbm
+    speeds = lattice_tables()[0].astype(int)
+    place_x, place_y = lax.axis_index("gx"), lax.axis_index("gy")
+    has_xp, has_xm = place_x < 7, place_x > 0
+    has_yp, has_ym = place_y < 3, place_y > 0
+    copies = []
+
+    def send(*part):
+        copy = pltpu.make_async_copy(
+            moved_ref.at[part], moved_hbm.at[part], sems.at[len(copies)]
+        )
+        copy.start()
+        copies.append(copy)
+
+    for i in (1, 2, 7, 8, 9, 10):
+        cx, cy = (int(v) for v in speeds[i, :2])
+        x = 0 if cx == 1 else 3
+        first, last = {0: (0, 32), 1: (8, 32), -1: (0, 24)}[cy]
+        there, face = (has_xm, xp_ref[XP.index(i)]) if cx == 1 else (has_xp, xm_ref[XM.index(i)])
+        block = jnp.where(there, face[first - cy : last - cy], 0.0)
+        rows = slice(32 * x + first, 32 * x + last)
+        code, value = bounce_ref[0, rows, :], value_ref[rows, :]
+        moved_ref[i, x, first:last, :] = finish(block, i, None, code, value)
+        send(i, x, slice(first, last))
+    at_row = iota((8, 128), 0)
+    for i in (3, 4, 7, 8, 9, 10):
+        cx, cy = (int(v) for v in speeds[i, :2])
+        planes = {0: (0, 4), 1: (1, 4), -1: (0, 3)}[cx]
+        first = 0 if cy == 1 else 24
+        face_ref, n = (yp_ref, YP.index(i)) if cy == 1 else (ym_ref, YM.index(i))
+        for x in range(*planes):
+            source = x - cx
+            block = post_ref[i, 32 * source + first : 32 * source + first + 8, :]
+            line = face_ref[4 * n + source : 4 * n + source + 1, :]
+            line = jnp.where(has_ym if cy == 1 else has_yp, line, 0.0)
+            block = pltpu.roll(block, 1 if cy == 1 else 7, 0)
+            block = jnp.where(at_row == (0 if cy == 1 else 7), line, block)
+            rows = slice(32 * x + first, 32 * x + first + 8)
+            code, value = bounce_ref[0, rows, :], value_ref[rows, :]
+            moved_ref[i, x, first : first + 8, :] = finish(block, i, None, code, value)
+        send(i, slice(*planes), slice(first, first + 8))
+    for copy in copies:
+        copy.wait()
+
+
 def fourth_kernel(
     partly_hbm,
     post_ref,
     bounce_ref,
+    value_ref,
     own_ref,
     got1_ref,
     got2_ref,
@@ -740,7 +774,7 @@
             if cz:
                 m = order.index(i)
                 column = columns[rows, m : m + 1]
-            code, value = bounce_ref[0, rows, :], bounce_ref[1, rows, :]
+            code, value = bounce_ref[0, rows, :], value_ref[rows, :]
             row_ref[i - 7, x] = finish(block, i, column, code, value)
         part = slice(planes[0], planes[-1] + 1)
         send(row_ref.at[i - 7, part], moved_hbm.at[i, part, first : first + 8, :])
@@ -753,7 +787,7 @@
             block = jnp.where(has_xp, xm_ref[XM.index(i)], 0.0)
         rows = slice(32 * x, 32 * x + 32)
         m = order.index(i)
-        code, value = bounce_ref[0, rows, :], bounce_ref[1, rows, :]
+        code, value = bounce_ref[0, rows, :], value_ref[rows, :]
         edge_ref[number] = finish(block, i, columns[rows, m : m + 1], code, value)
         send(edge_ref.at[number], moved_hbm.at[i, x])
 
@@ -780,7 +814,7 @@
         return jax.ShapeDtypeStruct(shape, F32)
 
     params = pltpu.CompilerParams(vmem_limit_bytes=40 * 1024 * 1024)
-    post, bounce, send1, xp, xm, yp, ym, xy, own = pl.pallas_call(
+    post, bounce, send1, xp, xm, yp, ym, xy, own, wall = pl.pallas_call(
         first_kernel,
         out_shape=(
             array(19, 128, 128),
@@ -792,9 +826,10 @@
             array(24, 128),
             array(8, 128),
             array(8, 128),
+            array(8, 128),
         ),
         in_specs=[pl.BlockSpec(memory_space=pltpu.HBM)] * 9,
-        out_specs=(vmem,) * 9,
+        out_specs=(vmem,) * 10,
         scratch_shapes=[
             pltpu.VMEM((19, 128, 128), F32),
             pltpu.VMEM((128, 128), I32),
@@ -805,7 +840,6 @@
             pltpu.SMEM((8, 6), F32),
             pltpu.SMEM((3, 8), F32),
             pltpu.SMEM((15,), F32),
-            pltpu.VMEM((128, 128), F32),
             pltpu.SemaphoreType.DMA((4,)),
             pltpu.SemaphoreType.DMA((8,)),
         ],
@@ -849,17 +883,18 @@
     yp, ym = shift(yp, "gy", 1), shift(ym, "gy", -1)
     got2 = lax.all_to_all(send2, ("gx", "gy"), 0, 0, tiled=True)
     hbm = pl.BlockSpec(memory_space=pltpu.HBM)
-    partly, step = pl.pallas_call(
+    partly, value, step = pl.pallas_call(
         third_kernel,
-        out_shape=(array(19, 4, 32, 128), array(2, 8, 128)),
-        in_specs=[vmem] * 7 + [hbm] * 3,
-        out_specs=(hbm, vmem),
+        out_shape=(array(19, 4, 32, 128), array(128, 128), array(2, 8, 128)),
+        in_specs=[vmem] * 4 + [hbm] * 4,
+        out_specs=(hbm, vmem, vmem),
         scratch_shapes=[
             pltpu.VMEM((19, 4, 32, 128), F32),
+            pltpu.VMEM((8, 128), I32),
             pltpu.VMEM((8, 6), F32),
             pltpu.SMEM((8,), F32),
             pltpu.SMEM((3, 8), F32),
-            pltpu.SemaphoreType.DMA((26,)),
+            pltpu.SemaphoreType.DMA((23,)),
         ],
         compiler_params=params,
         cost_estimate=pl.CostEstimate(
@@ -867,16 +902,26 @@
         ),
         name="move",
     )(
-        *(post, bounce, got1, xp, xm, yp, ym),
+        *(post, bounce, wall, got1),
         *(
             pltpu.with_memory_space_constraint(x, pltpu.HBM)
-            for x in (motion, inv_mass, inv_inertia.T)
+            for x in (motion, inv_mass, inv_inertia.T, link_cell.reshape(8, 128))
         ),
     )
+    partly = pl.pallas_call(
+        face_kernel,
+        out_shape=array(19, 4, 32, 128),
+        in_specs=[hbm] + [vmem] * 7,
+        out_specs=hbm,
+        scratch_shapes=[pltpu.VMEM((19, 4, 32, 128), F32), pltpu.SemaphoreType.DMA((12,))],
+        input_output_aliases={0: 0},
+        compiler_params=params,
+        name="faces",
+    )(partly, post, bounce, value, xp, xm, yp, ym)
     moved, own_loads, motion_next = pl.pallas_call(
         fourth_kernel,
         out_shape=(array(19, 4, 32, 128), array(6, 128), array(8, 6)),
-        in_specs=[hbm] + [vmem] * 10,
+        in_specs=[hbm] + [vmem] * 11,
         out_specs=(hbm,) * 3,
         scratch_shapes=[
             pltpu.VMEM((12, 4, 8, 128), F32),
@@ -888,7 +933,7 @@
         input_output_aliases={0: 0},
         compiler_params=params,
         name="close",
-    )(partly, post, bounce, own, got1, got2, xp, xm, yp, ym, step)
+    )(partly, post, bounce, value, own, got1, got2, xp, xm, yp, ym, step)
     return (moved, own_loads, motion_next)
 
 

time: 40.2 us -> 39.9 us (level)
  waiting for transfers between devices: 3.28 us -> 1.79 us
  Pallas kernels: 8.3 us -> 9.52 us
    ppermute x4, waiting for transfers between devices: 2.25 us -> 0.1 us  [shift(): return lax.ppermute(x, axis, [(i, (i + by) % size) for i in range(size)])]
    pallas_call x1 -> x2, Pallas kernels: 1.43 us -> 2.9 us  [the longest x1 2.14 us: body(): pl.pallas_call(third_kernel, out_shape=(array(19, 4, 32, 128), array(128,...]
    all_to_all x1, waiting for transfers between devices: 1.02 us -> 1.69 us  [body(): got2 = lax.all_to_all(send2, ('gx', 'gy'), 0, 0, tiled=True)]
  transfers between devices with their start and end apart: 5 -> 5, of which waited for: 3 -> 2; matrix products, arithmetic and copies ran while one was open for 0% -> 0% of each run, Pallas kernels for 4% -> 7%
where the time goes in v7:
time: 39.9 us; the launch traced here: 39.7 us
  starting transfers between devices  18 us (45%)
  blocking collectives  9.69 us (24%)
  Pallas kernels  9.52 us (24%)
  waiting for transfers between devices  1.79 us (4%)
  between operations  0.68 us (2%)
    all_to_all x1, starting transfers between devices, body(): got2 = lax.all_to_all(send2, ('gx', 'gy'), 0, 0, tiled=True)  11.4 us
    all_to_all x1, blocking collectives, body(): got1 = lax.all_to_all(send1, 'gz', 0, 0, tiled=True)  9.69 us
    ppermute x4, starting transfers between devices, shift(): return lax.ppermute(x, axis, [(i, (i + by) % size) for i in range(size)])  6.55 us
    pallas_call x1, Pallas kernels, body(): pl.pallas_call(first_kernel, out_shape=(array(19, 128, 128), array(2, 128...  3.32 us
    pallas_call x1, Pallas kernels, body(): pl.pallas_call(second_kernel, out_shape=array(32, 8, 128), in_specs=[vmem...  2.24 us
    pallas_call x1, Pallas kernels, body(): pl.pallas_call(third_kernel, out_shape=(array(19, 4, 32, 128), array(128,...  2.14 us
    all_to_all x1, waiting for transfers between devices, body(): got2 = lax.all_to_all(send2, ('gx', 'gy'), 0, 0, tiled=True)  1.69 us
    pallas_call x1, Pallas kernels, body(): pl.pallas_call(fourth_kernel, out_shape=(array(19, 4, 32, 128), array(6,...  1.06 us
  transfers between devices with their start and end apart: 5, of which 2 were waited for; matrix products, arithmetic and copies ran while one was open for 0% of the time, Pallas kernels for 7%

profile of v7, /device:TPU:2, one launch (start us, length us, event | category | flops | bytes accessed | tf_op | source)
XLA Modules:
  0.0 39.7 jit_solution(15571980293302345027)
XLA Ops:
  0.6 3.3 %collide.1 = (f32[19,128,128]{2,1,0:T(8,128)S(1)}, f32[2,128,128]{2,1,0:T(8,128)S(1)}, f32[8,5,8,128]{3,2,1,0:T(8,128)S(1)}, f32[5,32,128]{2,1,0:T(8,128)S(1)}, ...) custom-call(f32[19,128,128]{2,1,0:T(8,128)} %bitcast.8, ...), custom_call_target="tpu_custom_call" | custom-call | tf_op jit(solution)/shard_map/collide/pallas_call | solution.py:817
  4.0 9.7 %all_to_all.10.got1_ref.got_ref = f32[8,5,8,128]{3,2,1,0:T(8,128)S(1)} all-to-all(f32[8,5,8,128]{3,2,1,0:T(8,128)S(1)} %get-tuple-element.19), channel_id=1, replica_groups=mesh['gx'=8,'gy'=4,'gz'=8] {'gz'}, dimensions={0} | all-to-all | bytes 327680 | tf_op jit(solution)/shard_map/all_to_all | solution.py:869
  13.7 2.2 %bins.1 = f32[32,8,128]{2,1,0:T(8,128)} custom-call(f32[8,5,8,128]{3,2,1,0:T(8,128)S(1)} %all_to_all.10.got1_ref.got_ref, f32[8,128]{1,0:T(8,128)S(1)} %get-tuple-element.27.xy_ref), custom_call_target="tpu_custom_call" | custom-call | flops 805306368 | bytes 131072 | tf_op jit(solution)/shard_map/bins/pallas_call | solution.py:870
  15.9 11.4 %all-to-all-start.1 = ((f32[32,8,128]{2,1,0:T(8,128)}), f32[32,8,128]{2,1,0:T(8,128)S(1)}, u32[]{:S(2)}, u32[]{:S(2)}) async-start(f32[32,8,128]{2,1,0:T(8,128)} %bins.1), calls=%async_computation.1 | async-start | bytes 262144 | tf_op jit(solution)/shard_map/all_to_all | solution.py:884
  27.3 1.9 %collective-permute-start = (f32[5,32,128]{2,1,0:T(8,128)S(1)}, f32[5,32,128]{2,1,0:T(8,128)S(1)}, u32[]{:S(2)}, u32[]{:S(2)}) collective-permute-start(f32[5,32,128]{2,1,0:T(8,128)S(1)} %get-tuple-element.22), channel_id=1, source_target_pairs={{0,32},{32,64},{64,96},{96,128},{128,160},{160,192},{192,224},{224... | collective-permute-start | bytes 245768 | tf_op jit(solution)/shard_map/ppermute | solution.py:867
  29.2 1.4 %collective-permute-start.1 = (f32[5,32,128]{2,1,0:T(8,128)S(1)}, f32[5,32,128]{2,1,0:T(8,128)S(1)}, u32[]{:S(2)}, u32[]{:S(2)}) collective-permute-start(f32[5,32,128]{2,1,0:T(8,128)S(1)} %get-tuple-element.23), channel_id=1, source_target_pairs={{0,224},{32,0},{64,32},{96,64},{128,96},{160,128},{192,160},{224,1... | collective-permute-start | bytes 245768 | tf_op jit(solution)/shard_map/ppermute | solution.py:867
  30.7 1.8 %collective-permute-start.2 = (f32[24,128]{1,0:T(8,128)S(1)}, f32[24,128]{1,0:T(8,128)S(1)}, u32[]{:S(2)}, u32[]{:S(2)}) collective-permute-start(f32[24,128]{1,0:T(8,128)S(1)} %get-tuple-element.24), channel_id=1, source_target_pairs={{0,8},{8,16},{16,24},{24,0},{1,9},{9,17},{17,25},{25,1},{2,10},{10... | collective-permute-start | bytes 36872 | tf_op jit(solution)/shard_map/ppermute | solution.py:867
  32.5 1.4 %collective-permute-start.3 = (f32[24,128]{1,0:T(8,128)S(1)}, f32[24,128]{1,0:T(8,128)S(1)}, u32[]{:S(2)}, u32[]{:S(2)}) collective-permute-start(f32[24,128]{1,0:T(8,128)S(1)} %get-tuple-element.25), channel_id=1, source_target_pairs={{0,24},{8,0},{16,8},{24,16},{1,25},{9,1},{17,9},{25,17},{2,26},{10... | collective-permute-start | bytes 36872 | tf_op jit(solution)/shard_map/ppermute | solution.py:867
  33.9 2.1 %move.1 = (f32[19,4,32,128]{3,2,1,0:T(8,128)}, f32[128,128]{1,0:T(8,128)S(1)}, f32[2,8,128]{2,1,0:T(8,128)S(1)}) custom-call(f32[19,128,128]{2,1,0:T(8,128)S(1)} %get-tuple-element.16.post_ref, f32[2,128,128]{2,1,0:T(8,128)S(1)} %get-tuple-element.17.bounce_ref, f32[8,128]{1,0:T(8,128)S(1)} %get-tuple-element.18.wall_ref, ...), custom_call_target="tpu_custom_call" | custom-call | flops 1245184 | bytes 2490368 | tf_op jit(solution)/shard_map/move/pallas_call | solution.py:886
  36.0 0.0 collective-permute-done.2.yp_ref
  36.1 0.1 collective-permute-done.3.ym_ref
  36.1 0.0 collective-permute-done.xp_ref
  36.2 0.0 collective-permute-done.1.xm_ref
  36.2 0.8 %faces.1.partly_hbm = f32[19,4,32,128]{3,2,1,0:T(8,128)} custom-call(f32[19,4,32,128]{3,2,1,0:T(8,128)} %get-tuple-element.20.partly_hbm, f32[19,128,128]{2,1,0:T(8,128)S(1)} %get-tuple-element.16.post_ref, f32[2,128,128]{2,1,0:T(8,128)S(1)} %get-tuple-element.17.bounce_ref, ...), custom_call_target="tpu_custom_call", output_to_operand_aliasing={{}: (0, {})} | custom-call | tf_op jit(solution)/shard_map/faces/pallas_call | solution.py:911
  36.9 1.7 %all-to-all-done.1.got2_ref = f32[32,8,128]{2,1,0:T(8,128)S(1)} async-done(((f32[32,8,128]{2,1,0:T(8,128)}), f32[32,8,128]{2,1,0:T(8,128)S(1)}, u32[]{:S(2)}, u32[]{:S(2)}) %all-to-all-start.1) | async-done | bytes 131104 | tf_op jit(solution)/shard_map/all_to_all | solution.py:884
  38.6 1.1 %close.1 = (f32[19,4,32,128]{3,2,1,0:T(8,128)}, f32[6,128]{1,0:T(8,128)}, f32[8,6]{1,0:T(8,128)}) custom-call(f32[19,4,32,128]{3,2,1,0:T(8,128)} %faces.1.partly_hbm, f32[19,128,128]{2,1,0:T(8,128)S(1)} %get-tuple-element.16.post_ref, f32[2,128,128]{2,1,0:T(8,128)S(1)} %get-tuple-element.17.bounce_ref, ...), custom_call_target="tpu_custom_call", output_to_operand_aliasing={{0}: (0, {})} | custom-call | tf_op jit(solution)/shard_map/close/pallas_call | solution.py:921
Async XLA Ops:
  15.9 22.7 %all-to-all-start.1 = ((f32[32,8,128]{2,1,0:T(8,128)}), f32[32,8,128]{2,1,0:T(8,128)S(1)}, u32[]{:S(2)}, u32[]{:S(2)}) async-start(f32[32,8,128]{2,1,0:T(8,128)} %bins.1), calls=%async_computation.1 | async-start | bytes 262144 | tf_op jit(solution)/shard_map/all_to_all | solution.py:884
  27.3 8.8 %collective-permute-start = (f32[5,32,128]{2,1,0:T(8,128)S(1)}, f32[5,32,128]{2,1,0:T(8,128)S(1)}, u32[]{:S(2)}, u32[]{:S(2)}) collective-permute-start(f32[5,32,128]{2,1,0:T(8,128)S(1)} %get-tuple-element.22), channel_id=1, source_target_pairs={{0,32},{32,64},{64,96},{96,128},{128,160},{160,192},{192,224},{224... | collective-permute-start | bytes 245768 | tf_op jit(solution)/shard_map/ppermute | solution.py:867
  29.2 6.9 %collective-permute-start.1 = (f32[5,32,128]{2,1,0:T(8,128)S(1)}, f32[5,32,128]{2,1,0:T(8,128)S(1)}, u32[]{:S(2)}, u32[]{:S(2)}) collective-permute-start(f32[5,32,128]{2,1,0:T(8,128)S(1)} %get-tuple-element.23), channel_id=1, source_target_pairs={{0,224},{32,0},{64,32},{96,64},{128,96},{160,128},{192,160},{224,1... | collective-permute-start | bytes 245768 | tf_op jit(solution)/shard_map/ppermute | solution.py:867
  30.7 5.4 %collective-permute-start.2 = (f32[24,128]{1,0:T(8,128)S(1)}, f32[24,128]{1,0:T(8,128)S(1)}, u32[]{:S(2)}, u32[]{:S(2)}) collective-permute-start(f32[24,128]{1,0:T(8,128)S(1)} %get-tuple-element.24), channel_id=1, source_target_pairs={{0,8},{8,16},{16,24},{24,0},{1,9},{9,17},{17,25},{25,1},{2,10},{10... | collective-permute-start | bytes 36872 | tf_op jit(solution)/shard_map/ppermute | solution.py:867
  32.5 3.7 %collective-permute-start.3 = (f32[24,128]{1,0:T(8,128)S(1)}, f32[24,128]{1,0:T(8,128)S(1)}, u32[]{:S(2)}, u32[]{:S(2)}) collective-permute-start(f32[24,128]{1,0:T(8,128)S(1)} %get-tuple-element.25), channel_id=1, source_target_pairs={{0,24},{8,0},{16,8},{24,16},{1,25},{9,1},{17,9},{25,17},{2,26},{10... | collective-permute-start | bytes 36872 | tf_op jit(solution)/shard_map/ppermute | solution.py:867

commit v8 on v7

--- a/solution.py
+++ b/solution.py
@@ -286,7 +286,7 @@
         copy.start()
     for x in range(4):
         plane(x).start()
-    for copy in copies:
+    for copy in copies[0:3]:
         copy.wait()
     speeds, weights, _ = lattice_tables()
     links = 1024
@@ -303,6 +303,8 @@
     lanes_hot16 = hot(flat_lane)
     flat_store = flat(store)
     low_hot = hot(flat_store & 127)
+    for copy in copies[3:6]:
+        copy.wait()
     by_high = jnp.dot(
         owner_ref[...].astype(F32).astype(BF16), low_hot, preferred_element_type=F32
     )
@@ -334,13 +336,11 @@
     spread = jnp.concatenate(groups(flat_lane, coded), axis=0)
     bounce_ref[0] = rows_dot(rows_hot16, spread)
 
+    for copy in copies[6:8]:
+        copy.wait()
     k = collision_scalars(lambda i: rates_ref[i])
 
     def block(step, carry):
-        @pl.when((step & 3) == 0)
-        def _():
-            plane(lax.shift_right_logical(step, 2)).wait()
-
         rows = pl.ds(pl.multiple_of(step * 8, 8), 8)
         f = [pop_ref[i, rows, :] for i in range(19)]
         post = collide(f, k)
@@ -355,7 +355,13 @@
         bounce_ref[1, rows, :] = found
         return carry
 
-    lax.fori_loop(0, 16, block, 0, unroll=2)
+    def slab(x, carry):
+        plane(x).wait()
+        for part in range(4):
+            block(x * 4 + part, 0)
+        return carry
+
+    lax.fori_loop(0, 4, slab, 0)
 
     at_lane = iota((128, 128), 1)
     column = jnp.zeros((128, 128), F32)

time: 39.9 us -> 39.5 us (0.990)
  Pallas kernels: 9.52 us -> 9.05 us
    pallas_call x1, Pallas kernels: 3.32 us -> 2.85 us  [body(): pl.pallas_call(first_kernel, out_shape=(array(19, 128, 128), array(2, 128...]
where the time goes in v8:
time: 39.5 us; the launch traced here: 39.2 us
  starting transfers between devices  18 us (46%)
  blocking collectives  9.69 us (25%)
  Pallas kernels  9.05 us (23%)
  waiting for transfers between devices  1.79 us (5%)
  between operations  0.68 us (2%)
    all_to_all x1, starting transfers between devices, body(): got2 = lax.all_to_all(send2, ('gx', 'gy'), 0, 0, tiled=True)  11.5 us
    all_to_all x1, blocking collectives, body(): got1 = lax.all_to_all(send1, 'gz', 0, 0, tiled=True)  9.69 us
    ppermute x4, starting transfers between devices, shift(): return lax.ppermute(x, axis, [(i, (i + by) % size) for i in range(size)])  6.55 us
    pallas_call x1, Pallas kernels, body(): pl.pallas_call(first_kernel, out_shape=(array(19, 128, 128), array(2, 128...  2.85 us
    pallas_call x1, Pallas kernels, body(): pl.pallas_call(second_kernel, out_shape=array(32, 8, 128), in_specs=[vmem...  2.24 us
    pallas_call x1, Pallas kernels, body(): pl.pallas_call(third_kernel, out_shape=(array(19, 4, 32, 128), array(128,...  2.14 us
    all_to_all x1, waiting for transfers between devices, body(): got2 = lax.all_to_all(send2, ('gx', 'gy'), 0, 0, tiled=True)  1.69 us
    pallas_call x1, Pallas kernels, body(): pl.pallas_call(fourth_kernel, out_shape=(array(19, 4, 32, 128), array(6,...  1.06 us
  transfers between devices with their start and end apart: 5, of which 2 were waited for; matrix products, arithmetic and copies ran while one was open for 0% of the time, Pallas kernels for 7%

profile of v8, /device:TPU:2, one launch (start us, length us, event | category | flops | bytes accessed | tf_op | source)
XLA Modules:
  0.0 39.2 jit_solution(11020195119657524148)
XLA Ops:
  0.6 2.9 %collide.1 = (f32[19,128,128]{2,1,0:T(8,128)S(1)}, f32[2,128,128]{2,1,0:T(8,128)S(1)}, f32[8,5,8,128]{3,2,1,0:T(8,128)S(1)}, f32[5,32,128]{2,1,0:T(8,128)S(1)}, ...) custom-call(f32[19,128,128]{2,1,0:T(8,128)} %bitcast.8, ...), custom_call_target="tpu_custom_call" | custom-call | tf_op jit(solution)/shard_map/collide/pallas_call | solution.py:823
  3.5 9.7 %all_to_all.10.got1_ref.got_ref = f32[8,5,8,128]{3,2,1,0:T(8,128)S(1)} all-to-all(f32[8,5,8,128]{3,2,1,0:T(8,128)S(1)} %get-tuple-element.19), channel_id=1, replica_groups=mesh['gx'=8,'gy'=4,'gz'=8] {'gz'}, dimensions={0} | all-to-all | bytes 327680 | tf_op jit(solution)/shard_map/all_to_all | solution.py:875
  13.2 2.2 %bins.1 = f32[32,8,128]{2,1,0:T(8,128)} custom-call(f32[8,5,8,128]{3,2,1,0:T(8,128)S(1)} %all_to_all.10.got1_ref.got_ref, f32[8,128]{1,0:T(8,128)S(1)} %get-tuple-element.27.xy_ref), custom_call_target="tpu_custom_call" | custom-call | flops 805306368 | bytes 131072 | tf_op jit(solution)/shard_map/bins/pallas_call | solution.py:876
  15.4 11.5 %all-to-all-start.1 = ((f32[32,8,128]{2,1,0:T(8,128)}), f32[32,8,128]{2,1,0:T(8,128)S(1)}, u32[]{:S(2)}, u32[]{:S(2)}) async-start(f32[32,8,128]{2,1,0:T(8,128)} %bins.1), calls=%async_computation.1 | async-start | bytes 262144 | tf_op jit(solution)/shard_map/all_to_all | solution.py:890
  26.9 1.9 %collective-permute-start = (f32[5,32,128]{2,1,0:T(8,128)S(1)}, f32[5,32,128]{2,1,0:T(8,128)S(1)}, u32[]{:S(2)}, u32[]{:S(2)}) collective-permute-start(f32[5,32,128]{2,1,0:T(8,128)S(1)} %get-tuple-element.22), channel_id=1, source_target_pairs={{0,32},{32,64},{64,96},{96,128},{128,160},{160,192},{192,224},{224... | collective-permute-start | bytes 245768 | tf_op jit(solution)/shard_map/ppermute | solution.py:873
  28.8 1.4 %collective-permute-start.1 = (f32[5,32,128]{2,1,0:T(8,128)S(1)}, f32[5,32,128]{2,1,0:T(8,128)S(1)}, u32[]{:S(2)}, u32[]{:S(2)}) collective-permute-start(f32[5,32,128]{2,1,0:T(8,128)S(1)} %get-tuple-element.23), channel_id=1, source_target_pairs={{0,224},{32,0},{64,32},{96,64},{128,96},{160,128},{192,160},{224,1... | collective-permute-start | bytes 245768 | tf_op jit(solution)/shard_map/ppermute | solution.py:873
  30.2 1.8 %collective-permute-start.2 = (f32[24,128]{1,0:T(8,128)S(1)}, f32[24,128]{1,0:T(8,128)S(1)}, u32[]{:S(2)}, u32[]{:S(2)}) collective-permute-start(f32[24,128]{1,0:T(8,128)S(1)} %get-tuple-element.24), channel_id=1, source_target_pairs={{0,8},{8,16},{16,24},{24,0},{1,9},{9,17},{17,25},{25,1},{2,10},{10... | collective-permute-start | bytes 36872 | tf_op jit(solution)/shard_map/ppermute | solution.py:873
  32.0 1.4 %collective-permute-start.3 = (f32[24,128]{1,0:T(8,128)S(1)}, f32[24,128]{1,0:T(8,128)S(1)}, u32[]{:S(2)}, u32[]{:S(2)}) collective-permute-start(f32[24,128]{1,0:T(8,128)S(1)} %get-tuple-element.25), channel_id=1, source_target_pairs={{0,24},{8,0},{16,8},{24,16},{1,25},{9,1},{17,9},{25,17},{2,26},{10... | collective-permute-start | bytes 36872 | tf_op jit(solution)/shard_map/ppermute | solution.py:873
  33.4 2.1 %move.1 = (f32[19,4,32,128]{3,2,1,0:T(8,128)}, f32[128,128]{1,0:T(8,128)S(1)}, f32[2,8,128]{2,1,0:T(8,128)S(1)}) custom-call(f32[19,128,128]{2,1,0:T(8,128)S(1)} %get-tuple-element.16.post_ref, f32[2,128,128]{2,1,0:T(8,128)S(1)} %get-tuple-element.17.bounce_ref, f32[8,128]{1,0:T(8,128)S(1)} %get-tuple-element.18.wall_ref, ...), custom_call_target="tpu_custom_call" | custom-call | flops 1245184 | bytes 2490368 | tf_op jit(solution)/shard_map/move/pallas_call | solution.py:892
  35.6 0.0 collective-permute-done.2.yp_ref
  35.6 0.1 collective-permute-done.3.ym_ref
  35.7 0.0 collective-permute-done.xp_ref
  35.7 0.0 collective-permute-done.1.xm_ref
  35.7 0.8 %faces.1.partly_hbm = f32[19,4,32,128]{3,2,1,0:T(8,128)} custom-call(f32[19,4,32,128]{3,2,1,0:T(8,128)} %get-tuple-element.20.partly_hbm, f32[19,128,128]{2,1,0:T(8,128)S(1)} %get-tuple-element.16.post_ref, f32[2,128,128]{2,1,0:T(8,128)S(1)} %get-tuple-element.17.bounce_ref, ...), custom_call_target="tpu_custom_call", output_to_operand_aliasing={{}: (0, {})} | custom-call | tf_op jit(solution)/shard_map/faces/pallas_call | solution.py:917
  36.5 1.7 %all-to-all-done.1.got2_ref = f32[32,8,128]{2,1,0:T(8,128)S(1)} async-done(((f32[32,8,128]{2,1,0:T(8,128)}), f32[32,8,128]{2,1,0:T(8,128)S(1)}, u32[]{:S(2)}, u32[]{:S(2)}) %all-to-all-start.1) | async-done | bytes 131104 | tf_op jit(solution)/shard_map/all_to_all | solution.py:890
  38.2 1.1 %close.1 = (f32[19,4,32,128]{3,2,1,0:T(8,128)}, f32[6,128]{1,0:T(8,128)}, f32[8,6]{1,0:T(8,128)}) custom-call(f32[19,4,32,128]{3,2,1,0:T(8,128)} %faces.1.partly_hbm, f32[19,128,128]{2,1,0:T(8,128)S(1)} %get-tuple-element.16.post_ref, f32[2,128,128]{2,1,0:T(8,128)S(1)} %get-tuple-element.17.bounce_ref, ...), custom_call_target="tpu_custom_call", output_to_operand_aliasing={{0}: (0, {})} | custom-call | tf_op jit(solution)/shard_map/close/pallas_call | solution.py:927
Async XLA Ops:
  15.4 22.7 %all-to-all-start.1 = ((f32[32,8,128]{2,1,0:T(8,128)}), f32[32,8,128]{2,1,0:T(8,128)S(1)}, u32[]{:S(2)}, u32[]{:S(2)}) async-start(f32[32,8,128]{2,1,0:T(8,128)} %bins.1), calls=%async_computation.1 | async-start | bytes 262144 | tf_op jit(solution)/shard_map/all_to_all | solution.py:890
  26.9 8.8 %collective-permute-start = (f32[5,32,128]{2,1,0:T(8,128)S(1)}, f32[5,32,128]{2,1,0:T(8,128)S(1)}, u32[]{:S(2)}, u32[]{:S(2)}) collective-permute-start(f32[5,32,128]{2,1,0:T(8,128)S(1)} %get-tuple-element.22), channel_id=1, source_target_pairs={{0,32},{32,64},{64,96},{96,128},{128,160},{160,192},{192,224},{224... | collective-permute-start | bytes 245768 | tf_op jit(solution)/shard_map/ppermute | solution.py:873
  28.8 6.9 %collective-permute-start.1 = (f32[5,32,128]{2,1,0:T(8,128)S(1)}, f32[5,32,128]{2,1,0:T(8,128)S(1)}, u32[]{:S(2)}, u32[]{:S(2)}) collective-permute-start(f32[5,32,128]{2,1,0:T(8,128)S(1)} %get-tuple-element.23), channel_id=1, source_target_pairs={{0,224},{32,0},{64,32},{96,64},{128,96},{160,128},{192,160},{224,1... | collective-permute-start | bytes 245768 | tf_op jit(solution)/shard_map/ppermute | solution.py:873
  30.2 5.4 %collective-permute-start.2 = (f32[24,128]{1,0:T(8,128)S(1)}, f32[24,128]{1,0:T(8,128)S(1)}, u32[]{:S(2)}, u32[]{:S(2)}) collective-permute-start(f32[24,128]{1,0:T(8,128)S(1)} %get-tuple-element.24), channel_id=1, source_target_pairs={{0,8},{8,16},{16,24},{24,0},{1,9},{9,17},{17,25},{25,1},{2,10},{10... | collective-permute-start | bytes 36872 | tf_op jit(solution)/shard_map/ppermute | solution.py:873
  32.0 3.7 %collective-permute-start.3 = (f32[24,128]{1,0:T(8,128)S(1)}, f32[24,128]{1,0:T(8,128)S(1)}, u32[]{:S(2)}, u32[]{:S(2)}) collective-permute-start(f32[24,128]{1,0:T(8,128)S(1)} %get-tuple-element.25), channel_id=1, source_target_pairs={{0,24},{8,0},{16,8},{24,16},{1,25},{9,1},{17,9},{25,17},{2,26},{10... | collective-permute-start | bytes 36872 | tf_op jit(solution)/shard_map/ppermute | solution.py:873

commit v9 on v8

--- a/solution.py
+++ b/solution.py
@@ -469,7 +469,7 @@
             upper = total_ref[16 * c : 16 * c + 16, lanes]
             both = upper + total_ref[96 + 16 * c : 112 + 16 * c, lanes]
             for h in range(16):
-                send_ref[2 * h + e, c : c + 1, :] = both[h : h + 1]
+                send_ref[(2 * h + e) % 4 * 8 + (2 * h + e) // 4, c : c + 1, :] = both[h : h + 1]
     last = jnp.concatenate([body_row, jnp.zeros((1, 128), F32)], axis=0)
     for j in range(32):
         send_ref[j, 6:8, :] = last
@@ -486,18 +486,18 @@
     in_row = lane & 31
     to_yp = jnp.where(in_row == 0, turned(below[3:4], 97), turned(above[3:4], 98))
     to_ym = jnp.where(in_row == 0, below[4:5], turned(above[4:5], 1))
-    me = place_x * 4 + place_y
+    me = place_y * 8 + place_x
     has_xp, has_xm = place_x < 7, place_x > 0
     has_yp, has_ym = place_y < 3, place_y > 0
     for there, step, line in (
-        (has_xp, 4, to_xp),
-        (has_xm, -4, to_xm),
-        (has_yp, 1, to_yp),
-        (has_ym, -1, to_ym),
-        (has_xp & has_yp, 5, xy_ref[0:1, :]),
-        (has_xm & has_ym, -5, xy_ref[1:2, :]),
-        (has_xp & has_ym, 3, xy_ref[2:3, :]),
-        (has_xm & has_yp, -3, xy_ref[3:4, :]),
+        (has_xp, 1, to_xp),
+        (has_xm, -1, to_xm),
+        (has_yp, 8, to_yp),
+        (has_ym, -8, to_ym),
+        (has_xp & has_yp, 9, xy_ref[0:1, :]),
+        (has_xm & has_ym, -9, xy_ref[1:2, :]),
+        (has_xp & has_ym, -7, xy_ref[2:3, :]),
+        (has_xm & has_yp, 7, xy_ref[3:4, :]),
     ):
 
         @pl.when(there)
@@ -692,7 +692,7 @@
     place_x, place_y, place_z = (lax.axis_index(a) for a in ("gx", "gy", "gz"))
     has_xp, has_xm = place_x < 7, place_x > 0
     has_yp, has_ym = place_y < 3, place_y > 0
-    me = place_x * 4 + place_y
+    me = place_y * 8 + place_x
     copies = []
 
     def send(source, target):
@@ -725,13 +725,13 @@
 
     lane = iota((1, 128), 1)
     row_in_plane = lane & 31
-    from_x = {1: edge(has_xm, -4), -1: edge(has_xp, 4)}
-    from_y = {1: edge(has_ym, -1), -1: edge(has_yp, 1)}
+    from_x = {1: edge(has_xm, -1), -1: edge(has_xp, 1)}
+    from_y = {1: edge(has_ym, -8), -1: edge(has_yp, 8)}
     from_xy = {
-        (1, 1): edge(has_xm & has_ym, -5),
-        (-1, -1): edge(has_xp & has_yp, 5),
-        (1, -1): edge(has_xm & has_yp, -3),
-        (-1, 1): edge(has_xp & has_ym, 3),
+        (1, 1): edge(has_xm & has_ym, -9),
+        (-1, -1): edge(has_xp & has_yp, 9),
+        (1, -1): edge(has_xm & has_yp, 7),
+        (-1, 1): edge(has_xp & has_ym, -7),
     }
     order, lines = [], []
     for dirs, face in (
@@ -887,7 +887,7 @@
     )(got1, xy)
     xp, xm = shift(xp, "gx", 1), shift(xm, "gx", -1)
     yp, ym = shift(yp, "gy", 1), shift(ym, "gy", -1)
-    got2 = lax.all_to_all(send2, ("gx", "gy"), 0, 0, tiled=True)
+    got2 = lax.all_to_all(send2, ("gy", "gx"), 0, 0, tiled=True)
     hbm = pl.BlockSpec(memory_space=pltpu.HBM)
     partly, value, step = pl.pallas_call(
         third_kernel,

time: 39.5 us -> 39.3 us (level)
  no operation moved by 1% of the time
where the time goes in v9:
time: 39.3 us; the launch traced here: 39 us
  starting transfers between devices  18 us (46%)
  blocking collectives  9.69 us (25%)
  Pallas kernels  9.05 us (23%)
  waiting for transfers between devices  1.61 us (4%)
  between operations  0.68 us (2%)
    all_to_all x1, starting transfers between devices, body(): got2 = lax.all_to_all(send2, ('gy', 'gx'), 0, 0, tiled=True)  11.5 us
    all_to_all x1, blocking collectives, body(): got1 = lax.all_to_all(send1, 'gz', 0, 0, tiled=True)  9.69 us
    ppermute x4, starting transfers between devices, shift(): return lax.ppermute(x, axis, [(i, (i + by) % size) for i in range(size)])  6.55 us
    pallas_call x1, Pallas kernels, body(): pl.pallas_call(first_kernel, out_shape=(array(19, 128, 128), array(2, 128...  2.85 us
    pallas_call x1, Pallas kernels, body(): pl.pallas_call(second_kernel, out_shape=array(32, 8, 128), in_specs=[vmem...  2.23 us
    pallas_call x1, Pallas kernels, body(): pl.pallas_call(third_kernel, out_shape=(array(19, 4, 32, 128), array(128,...  2.14 us
    all_to_all x1, waiting for transfers between devices, body(): got2 = lax.all_to_all(send2, ('gy', 'gx'), 0, 0, tiled=True)  1.5 us
    pallas_call x1, Pallas kernels, body(): pl.pallas_call(fourth_kernel, out_shape=(array(19, 4, 32, 128), array(6,...  1.06 us
  transfers between devices with their start and end apart: 5, of which 2 were waited for; matrix products, arithmetic and copies ran while one was open for 0% of the time, Pallas kernels for 7%

profile of v9, /device:TPU:2, one launch (start us, length us, event | category | flops | bytes accessed | tf_op | source)
XLA Modules:
  0.0 39.0 jit_solution(11378634945563640398)
XLA Ops:
  0.6 2.9 %collide.1 = (f32[19,128,128]{2,1,0:T(8,128)S(1)}, f32[2,128,128]{2,1,0:T(8,128)S(1)}, f32[8,5,8,128]{3,2,1,0:T(8,128)S(1)}, f32[5,32,128]{2,1,0:T(8,128)S(1)}, ...) custom-call(f32[19,128,128]{2,1,0:T(8,128)} %bitcast.8, ...), custom_call_target="tpu_custom_call" | custom-call | tf_op jit(solution)/shard_map/collide/pallas_call | solution.py:823
  3.5 9.7 %all_to_all.10.got1_ref.got_ref = f32[8,5,8,128]{3,2,1,0:T(8,128)S(1)} all-to-all(f32[8,5,8,128]{3,2,1,0:T(8,128)S(1)} %get-tuple-element.19), channel_id=1, replica_groups=mesh['gx'=8,'gy'=4,'gz'=8] {'gz'}, dimensions={0} | all-to-all | bytes 327680 | tf_op jit(solution)/shard_map/all_to_all | solution.py:875
  13.2 2.2 %bins.1 = f32[32,8,128]{2,1,0:T(8,128)} custom-call(f32[8,5,8,128]{3,2,1,0:T(8,128)S(1)} %all_to_all.10.got1_ref.got_ref, f32[8,128]{1,0:T(8,128)S(1)} %get-tuple-element.27.xy_ref), custom_call_target="tpu_custom_call" | custom-call | flops 805306368 | bytes 131072 | tf_op jit(solution)/shard_map/bins/pallas_call | solution.py:876
  15.4 11.5 %all-to-all-start.1 = ((f32[32,8,128]{2,1,0:T(8,128)}), f32[32,8,128]{2,1,0:T(8,128)S(1)}, u32[]{:S(2)}, u32[]{:S(2)}) async-start(f32[32,8,128]{2,1,0:T(8,128)} %bins.1), calls=%async_computation.1 | async-start | bytes 262144 | tf_op jit(solution)/shard_map/all_to_all | solution.py:890
  26.9 1.9 %collective-permute-start = (f32[5,32,128]{2,1,0:T(8,128)S(1)}, f32[5,32,128]{2,1,0:T(8,128)S(1)}, u32[]{:S(2)}, u32[]{:S(2)}) collective-permute-start(f32[5,32,128]{2,1,0:T(8,128)S(1)} %get-tuple-element.22), channel_id=1, source_target_pairs={{0,32},{32,64},{64,96},{96,128},{128,160},{160,192},{192,224},{224... | collective-permute-start | bytes 245768 | tf_op jit(solution)/shard_map/ppermute | solution.py:873
  28.8 1.4 %collective-permute-start.1 = (f32[5,32,128]{2,1,0:T(8,128)S(1)}, f32[5,32,128]{2,1,0:T(8,128)S(1)}, u32[]{:S(2)}, u32[]{:S(2)}) collective-permute-start(f32[5,32,128]{2,1,0:T(8,128)S(1)} %get-tuple-element.23), channel_id=1, source_target_pairs={{0,224},{32,0},{64,32},{96,64},{128,96},{160,128},{192,160},{224,1... | collective-permute-start | bytes 245768 | tf_op jit(solution)/shard_map/ppermute | solution.py:873
  30.2 1.8 %collective-permute-start.2 = (f32[24,128]{1,0:T(8,128)S(1)}, f32[24,128]{1,0:T(8,128)S(1)}, u32[]{:S(2)}, u32[]{:S(2)}) collective-permute-start(f32[24,128]{1,0:T(8,128)S(1)} %get-tuple-element.24), channel_id=1, source_target_pairs={{0,8},{8,16},{16,24},{24,0},{1,9},{9,17},{17,25},{25,1},{2,10},{10... | collective-permute-start | bytes 36872 | tf_op jit(solution)/shard_map/ppermute | solution.py:873
  32.0 1.4 %collective-permute-start.3 = (f32[24,128]{1,0:T(8,128)S(1)}, f32[24,128]{1,0:T(8,128)S(1)}, u32[]{:S(2)}, u32[]{:S(2)}) collective-permute-start(f32[24,128]{1,0:T(8,128)S(1)} %get-tuple-element.25), channel_id=1, source_target_pairs={{0,24},{8,0},{16,8},{24,16},{1,25},{9,1},{17,9},{25,17},{2,26},{10... | collective-permute-start | bytes 36872 | tf_op jit(solution)/shard_map/ppermute | solution.py:873
  33.4 2.1 %move.1 = (f32[19,4,32,128]{3,2,1,0:T(8,128)}, f32[128,128]{1,0:T(8,128)S(1)}, f32[2,8,128]{2,1,0:T(8,128)S(1)}) custom-call(f32[19,128,128]{2,1,0:T(8,128)S(1)} %get-tuple-element.16.post_ref, f32[2,128,128]{2,1,0:T(8,128)S(1)} %get-tuple-element.17.bounce_ref, f32[8,128]{1,0:T(8,128)S(1)} %get-tuple-element.18.wall_ref, ...), custom_call_target="tpu_custom_call" | custom-call | flops 1245184 | bytes 2490368 | tf_op jit(solution)/shard_map/move/pallas_call | solution.py:892
  35.6 0.0 collective-permute-done.2.yp_ref
  35.6 0.1 collective-permute-done.3.ym_ref
  35.7 0.0 collective-permute-done.xp_ref
  35.7 0.0 collective-permute-done.1.xm_ref
  35.7 0.8 %faces.1.partly_hbm = f32[19,4,32,128]{3,2,1,0:T(8,128)} custom-call(f32[19,4,32,128]{3,2,1,0:T(8,128)} %get-tuple-element.20.partly_hbm, f32[19,128,128]{2,1,0:T(8,128)S(1)} %get-tuple-element.16.post_ref, f32[2,128,128]{2,1,0:T(8,128)S(1)} %get-tuple-element.17.bounce_ref, ...), custom_call_target="tpu_custom_call", output_to_operand_aliasing={{}: (0, {})} | custom-call | tf_op jit(solution)/shard_map/faces/pallas_call | solution.py:917
  36.5 1.5 %all-to-all-done.1.got2_ref = f32[32,8,128]{2,1,0:T(8,128)S(1)} async-done(((f32[32,8,128]{2,1,0:T(8,128)}), f32[32,8,128]{2,1,0:T(8,128)S(1)}, u32[]{:S(2)}, u32[]{:S(2)}) %all-to-all-start.1) | async-done | bytes 131104 | tf_op jit(solution)/shard_map/all_to_all | solution.py:890
  38.0 1.1 %close.1 = (f32[19,4,32,128]{3,2,1,0:T(8,128)}, f32[6,128]{1,0:T(8,128)}, f32[8,6]{1,0:T(8,128)}) custom-call(f32[19,4,32,128]{3,2,1,0:T(8,128)} %faces.1.partly_hbm, f32[19,128,128]{2,1,0:T(8,128)S(1)} %get-tuple-element.16.post_ref, f32[2,128,128]{2,1,0:T(8,128)S(1)} %get-tuple-element.17.bounce_ref, ...), custom_call_target="tpu_custom_call", output_to_operand_aliasing={{0}: (0, {})} | custom-call | tf_op jit(solution)/shard_map/close/pallas_call | solution.py:927
Async XLA Ops:
  15.4 22.5 %all-to-all-start.1 = ((f32[32,8,128]{2,1,0:T(8,128)}), f32[32,8,128]{2,1,0:T(8,128)S(1)}, u32[]{:S(2)}, u32[]{:S(2)}) async-start(f32[32,8,128]{2,1,0:T(8,128)} %bins.1), calls=%async_computation.1 | async-start | bytes 262144 | tf_op jit(solution)/shard_map/all_to_all | solution.py:890
  26.9 8.8 %collective-permute-start = (f32[5,32,128]{2,1,0:T(8,128)S(1)}, f32[5,32,128]{2,1,0:T(8,128)S(1)}, u32[]{:S(2)}, u32[]{:S(2)}) collective-permute-start(f32[5,32,128]{2,1,0:T(8,128)S(1)} %get-tuple-element.22), channel_id=1, source_target_pairs={{0,32},{32,64},{64,96},{96,128},{128,160},{160,192},{192,224},{224... | collective-permute-start | bytes 245768 | tf_op jit(solution)/shard_map/ppermute | solution.py:873
  28.8 6.9 %collective-permute-start.1 = (f32[5,32,128]{2,1,0:T(8,128)S(1)}, f32[5,32,128]{2,1,0:T(8,128)S(1)}, u32[]{:S(2)}, u32[]{:S(2)}) collective-permute-start(f32[5,32,128]{2,1,0:T(8,128)S(1)} %get-tuple-element.23), channel_id=1, source_target_pairs={{0,224},{32,0},{64,32},{96,64},{128,96},{160,128},{192,160},{224,1... | collective-permute-start | bytes 245768 | tf_op jit(solution)/shard_map/ppermute | solution.py:873
  30.2 5.4 %collective-permute-start.2 = (f32[24,128]{1,0:T(8,128)S(1)}, f32[24,128]{1,0:T(8,128)S(1)}, u32[]{:S(2)}, u32[]{:S(2)}) collective-permute-start(f32[24,128]{1,0:T(8,128)S(1)} %get-tuple-element.24), channel_id=1, source_target_pairs={{0,8},{8,16},{16,24},{24,0},{1,9},{9,17},{17,25},{25,1},{2,10},{10... | collective-permute-start | bytes 36872 | tf_op jit(solution)/shard_map/ppermute | solution.py:873
  32.0 3.7 %collective-permute-start.3 = (f32[24,128]{1,0:T(8,128)S(1)}, f32[24,128]{1,0:T(8,128)S(1)}, u32[]{:S(2)}, u32[]{:S(2)}) collective-permute-start(f32[24,128]{1,0:T(8,128)S(1)} %get-tuple-element.25), channel_id=1, source_target_pairs={{0,24},{8,0},{16,8},{24,16},{1,25},{9,1},{17,9},{25,17},{2,26},{10... | collective-permute-start | bytes 36872 | tf_op jit(solution)/shard_map/ppermute | solution.py:873

commit v10 on v9

--- a/solution.py
+++ b/solution.py
@@ -194,6 +194,19 @@
     return lax.dot_general(a, b, (((1,), (1,)), ((), ())), preferred_element_type=F32)
 
 
+PLACE_X = (0, 4, 1, 5, 2, 6, 3, 7)
+PLACE_Y = (0, 1, 2, 3)
+PLACE_Z = (0, 4, 2, 6, 1, 5, 3, 7)
+
+
+def listed(table, index):
+    return sum(jnp.where(index == n, value, 0) for n, value in enumerate(table))
+
+
+def peer_at(x, y):
+    return listed(PLACE_Y, y) * 8 + listed(PLACE_X, x)
+
+
 def flat(x):
     return jnp.concatenate([x[s : s + 1] for s in range(8)], axis=1)
 
@@ -406,7 +419,7 @@
         for n, record in enumerate(records):
             send_ref[j, n] = record
         face = jnp.where(upward == j, columns[0:8], columns[8:16])
-        send_ref[j, 4] = jnp.where(iota((8, 128), 0) == 5, body_row, face)
+        send_ref[PLACE_Z[j], 4] = jnp.where(iota((8, 128), 0) == 5, body_row, face)
     own = owner_ref[pl.ds((place_x * 4 + place_y) * 8 + place_z, 1), :]
     own_ref[...] = jnp.zeros((8, 128), F32)
     for a in range(3):
@@ -423,6 +436,8 @@
     one = jnp.ones((16, 128), BF16)
     none = jnp.zeros((16, 128), BF16)
 
+    order = [PLACE_Z.index(n) for n in range(8)]
+
     def gather(peer, carry):
         strength, direction = got_ref[peer, 0], got_ref[peer, 1]
         cell, store = got_ref[peer, 2].astype(I32), got_ref[peer, 3].astype(I32)
@@ -431,7 +446,7 @@
         place = (
             lax.shift_right_logical(cell, 12) + (place_x * 4 - 16),
             (lax.shift_right_logical(cell, 7) & 31) + (place_y * 32 - 64),
-            (cell & 127) + (peer * 128 - 512),
+            (cell & 127) + (listed(order, peer) * 128 - 512),
         )
         arm = [(place[a].astype(F32) + 0.5 * speed[a]) * (1.0 / 128.0) for a in range(3)]
         push = [speed[a] * strength for a in range(3)]
@@ -469,13 +484,13 @@
             upper = total_ref[16 * c : 16 * c + 16, lanes]
             both = upper + total_ref[96 + 16 * c : 112 + 16 * c, lanes]
             for h in range(16):
-                send_ref[(2 * h + e) % 4 * 8 + (2 * h + e) // 4, c : c + 1, :] = both[h : h + 1]
+                send_ref[PLACE_Y[(2 * h + e) % 4] * 8 + PLACE_X[(2 * h + e) // 4], c : c + 1, :] = both[h : h + 1]
     last = jnp.concatenate([body_row, jnp.zeros((1, 128), F32)], axis=0)
     for j in range(32):
         send_ref[j, 6:8, :] = last
 
-    below = got_ref[lax.rem(place_z + 7, 8), 4]
-    above = got_ref[lax.rem(place_z + 1, 8), 4]
+    below = got_ref[listed(PLACE_Z, lax.rem(place_z + 7, 8)), 4]
+    above = got_ref[listed(PLACE_Z, lax.rem(place_z + 1, 8)), 4]
     lane = iota((1, 128), 1)
 
     def turned(x, by):
@@ -486,23 +501,22 @@
     in_row = lane & 31
     to_yp = jnp.where(in_row == 0, turned(below[3:4], 97), turned(above[3:4], 98))
     to_ym = jnp.where(in_row == 0, below[4:5], turned(above[4:5], 1))
-    me = place_y * 8 + place_x
     has_xp, has_xm = place_x < 7, place_x > 0
     has_yp, has_ym = place_y < 3, place_y > 0
-    for there, step, line in (
-        (has_xp, 1, to_xp),
-        (has_xm, -1, to_xm),
-        (has_yp, 8, to_yp),
-        (has_ym, -8, to_ym),
-        (has_xp & has_yp, 9, xy_ref[0:1, :]),
-        (has_xm & has_ym, -9, xy_ref[1:2, :]),
-        (has_xp & has_ym, -7, xy_ref[2:3, :]),
-        (has_xm & has_yp, 7, xy_ref[3:4, :]),
+    for there, dx, dy, line in (
+        (has_xp, 1, 0, to_xp),
+        (has_xm, -1, 0, to_xm),
+        (has_yp, 0, 1, to_yp),
+        (has_ym, 0, -1, to_ym),
+        (has_xp & has_yp, 1, 1, xy_ref[0:1, :]),
+        (has_xm & has_ym, -1, -1, xy_ref[1:2, :]),
+        (has_xp & has_ym, 1, -1, xy_ref[2:3, :]),
+        (has_xm & has_yp, -1, 1, xy_ref[3:4, :]),
     ):
 
         @pl.when(there)
-        def _(step=step, line=line):
-            send_ref[me + step, 7:8, :] = line
+        def _(dx=dx, dy=dy, line=line):
+            send_ref[peer_at(place_x + dx, place_y + dy), 7:8, :] = line
 
 
 def arrivals(lines):
@@ -565,8 +579,8 @@
         spread += groups(cell & 127, part)
     laid = rows_dot(hot(lax.shift_right_logical(cell, 7)), jnp.concatenate(spread, axis=0))
     value_ref[...] = bounce_ref[1] - (laid[:, 0:128] + laid[:, 128:256])
-    below = got1_ref[lax.rem(place_z + 7, 8), 4]
-    above = got1_ref[lax.rem(place_z + 1, 8), 4]
+    below = got1_ref[listed(PLACE_Z, lax.rem(place_z + 7, 8)), 4]
+    above = got1_ref[listed(PLACE_Z, lax.rem(place_z + 1, 8)), 4]
     order = ZP + ZM
     lines = []
     for dirs, face in ((ZP, below), (ZM, above)):
@@ -692,7 +706,6 @@
     place_x, place_y, place_z = (lax.axis_index(a) for a in ("gx", "gy", "gz"))
     has_xp, has_xm = place_x < 7, place_x > 0
     has_yp, has_ym = place_y < 3, place_y > 0
-    me = place_y * 8 + place_x
     copies = []
 
     def send(source, target):
@@ -719,24 +732,24 @@
     next_ref[...] = (step_ref[1] + step_ref[0] * body_load / 32768.0)[:, 0:6]
     send(next_ref, next_hbm)
 
-    def edge(there, step):
-        line = got2_ref[jnp.where(there, me + step, me), 7:8, :]
+    def edge(there, dx, dy):
+        line = got2_ref[peer_at(place_x + dx, place_y + dy), 7:8, :]
         return jnp.where(there, line, 0.0)
 
     lane = iota((1, 128), 1)
     row_in_plane = lane & 31
-    from_x = {1: edge(has_xm, -1), -1: edge(has_xp, 1)}
-    from_y = {1: edge(has_ym, -8), -1: edge(has_yp, 8)}
+    from_x = {1: edge(has_xm, -1, 0), -1: edge(has_xp, 1, 0)}
+    from_y = {1: edge(has_ym, 0, -1), -1: edge(has_yp, 0, 1)}
     from_xy = {
-        (1, 1): edge(has_xm & has_ym, -9),
-        (-1, -1): edge(has_xp & has_yp, 9),
-        (1, -1): edge(has_xm & has_yp, 7),
-        (-1, 1): edge(has_xp & has_ym, -7),
+        (1, 1): edge(has_xm & has_ym, -1, -1),
+        (-1, -1): edge(has_xp & has_yp, 1, 1),
+        (1, -1): edge(has_xm & has_yp, -1, 1),
+        (-1, 1): edge(has_xp & has_ym, 1, -1),
     }
     order, lines = [], []
     for dirs, face in (
-        (ZP, got1_ref[lax.rem(place_z + 7, 8), 4]),
-        (ZM, got1_ref[lax.rem(place_z + 1, 8), 4]),
+        (ZP, got1_ref[listed(PLACE_Z, lax.rem(place_z + 7, 8)), 4]),
+        (ZM, got1_ref[listed(PLACE_Z, lax.rem(place_z + 1, 8)), 4]),
     ):
         for n, i in enumerate(dirs):
             cx, cy, cz = (int(v) for v in speeds[i])
@@ -872,7 +885,8 @@
         size = lax.axis_size(axis)
         return lax.ppermute(x, axis, [(i, (i + by) % size) for i in range(size)])
 
-    got1 = lax.all_to_all(send1, "gz", 0, 0, tiled=True)
+    along_z = [[PLACE_Z.index(n) for n in range(8)]]
+    got1 = lax.all_to_all(send1, "gz", 0, 0, axis_index_groups=along_z, tiled=True)
     send2 = pl.pallas_call(
         second_kernel,
         out_shape=array(32, 8, 128),
@@ -887,7 +901,8 @@
     )(got1, xy)
     xp, xm = shift(xp, "gx", 1), shift(xm, "gx", -1)
     yp, ym = shift(yp, "gy", 1), shift(ym, "gy", -1)
-    got2 = lax.all_to_all(send2, ("gy", "gx"), 0, 0, tiled=True)
+    across = [[PLACE_Y.index(n // 8) * 8 + PLACE_X.index(n % 8) for n in range(32)]]
+    got2 = lax.all_to_all(send2, ("gy", "gx"), 0, 0, axis_index_groups=across, tiled=True)
     hbm = pl.BlockSpec(memory_space=pltpu.HBM)
     partly, value, step = pl.pallas_call(
         third_kernel,

time: 39.3 us -> 38.4 us (0.977)
  blocking collectives: 9.69 us -> 9.07 us
  waiting for transfers between devices: 1.61 us -> 1.18 us
    all_to_all x1, blocking collectives: 9.69 us -> 9.07 us  [body(): lax.all_to_all(send1, 'gz', 0, 0, axis_index_groups=along_z, tiled=True)]
    all_to_all x1, waiting for transfers between devices: 1.5 us -> 1.06 us  [body(): lax.all_to_all(send2, ('gy', 'gx'), 0, 0, axis_index_groups=across, tiled...]
  transfers between devices with their start and end apart: 5 -> 5, of which waited for: 2 -> 2; matrix products, arithmetic and copies ran while one was open for 0% -> 0% of each run, Pallas kernels for 7% -> 8%
where the time goes in v10:
time: 38.4 us; the launch traced here: 38.1 us
  starting transfers between devices  18.1 us (47%)
  Pallas kernels  9.13 us (24%)
  blocking collectives  9.07 us (24%)
  waiting for transfers between devices  1.18 us (3%)
  between operations  0.68 us (2%)
    all_to_all x1, starting transfers between devices, body(): lax.all_to_all(send2, ('gy', 'gx'), 0, 0, axis_index_groups=across, tiled...  11.5 us
    all_to_all x1, blocking collectives, body(): lax.all_to_all(send1, 'gz', 0, 0, axis_index_groups=along_z, tiled=True)  9.07 us
    ppermute x4, starting transfers between devices, shift(): return lax.ppermute(x, axis, [(i, (i + by) % size) for i in range(size)])  6.55 us
    pallas_call x1, Pallas kernels, body(): pl.pallas_call(first_kernel, out_shape=(array(19, 128, 128), array(2, 128...  2.85 us
    pallas_call x1, Pallas kernels, body(): pl.pallas_call(second_kernel, out_shape=array(32, 8, 128), in_specs=[vmem...  2.27 us
    pallas_call x1, Pallas kernels, body(): pl.pallas_call(third_kernel, out_shape=(array(19, 4, 32, 128), array(128,...  2.14 us
    pallas_call x1, Pallas kernels, body(): pl.pallas_call(fourth_kernel, out_shape=(array(19, 4, 32, 128), array(6,...  1.1 us
    all_to_all x1, waiting for transfers between devices, body(): lax.all_to_all(send2, ('gy', 'gx'), 0, 0, axis_index_groups=across, tiled...  1.06 us
  transfers between devices with their start and end apart: 5, of which 2 were waited for; matrix products, arithmetic and copies ran while one was open for 0% of the time, Pallas kernels for 8%

profile of v10, /device:TPU:2, one launch (start us, length us, event | category | flops | bytes accessed | tf_op | source)
XLA Modules:
  0.0 38.1 jit_solution(315933156215059602)
XLA Ops:
  0.6 2.9 %collide.1 = (f32[19,128,128]{2,1,0:T(8,128)S(1)}, f32[2,128,128]{2,1,0:T(8,128)S(1)}, f32[8,5,8,128]{3,2,1,0:T(8,128)S(1)}, f32[5,32,128]{2,1,0:T(8,128)S(1)}, ...) custom-call(f32[19,128,128]{2,1,0:T(8,128)} %bitcast.8, ...), custom_call_target="tpu_custom_call" | custom-call | tf_op jit(solution)/shard_map/collide/pallas_call | solution.py:836
  3.5 9.1 %all_to_all.10.got1_ref.got_ref = f32[8,5,8,128]{3,2,1,0:T(8,128)S(1)} all-to-all(f32[8,5,8,128]{3,2,1,0:T(8,128)S(1)} %get-tuple-element.19), channel_id=1, replica_groups={{0,4,2,6,1,5,3,7},{8,12,10,14,9,13,11,15},{16,20,18,22,17,21,19,23},{24..., dimensions={0} | all-to-all | bytes 327680 | tf_op jit(solution)/shard_map/all_to_all | solution.py:889
  12.6 2.3 %bins.1 = f32[32,8,128]{2,1,0:T(8,128)} custom-call(f32[8,5,8,128]{3,2,1,0:T(8,128)S(1)} %all_to_all.10.got1_ref.got_ref, f32[8,128]{1,0:T(8,128)S(1)} %get-tuple-element.27.xy_ref), custom_call_target="tpu_custom_call" | custom-call | flops 805306368 | bytes 131072 | tf_op jit(solution)/shard_map/bins/pallas_call | solution.py:890
  14.8 11.5 %all-to-all-start.1 = ((f32[32,8,128]{2,1,0:T(8,128)}), f32[32,8,128]{2,1,0:T(8,128)S(1)}, u32[]{:S(2)}, u32[]{:S(2)}) async-start(f32[32,8,128]{2,1,0:T(8,128)} %bins.1), calls=%async_computation.1 | async-start | bytes 262144 | tf_op jit(solution)/shard_map/all_to_all | solution.py:905
  26.4 1.9 %collective-permute-start = (f32[5,32,128]{2,1,0:T(8,128)S(1)}, f32[5,32,128]{2,1,0:T(8,128)S(1)}, u32[]{:S(2)}, u32[]{:S(2)}) collective-permute-start(f32[5,32,128]{2,1,0:T(8,128)S(1)} %get-tuple-element.22), channel_id=1, source_target_pairs={{0,32},{32,64},{64,96},{96,128},{128,160},{160,192},{192,224},{224... | collective-permute-start | bytes 245768 | tf_op jit(solution)/shard_map/ppermute | solution.py:886
  28.2 1.4 %collective-permute-start.1 = (f32[5,32,128]{2,1,0:T(8,128)S(1)}, f32[5,32,128]{2,1,0:T(8,128)S(1)}, u32[]{:S(2)}, u32[]{:S(2)}) collective-permute-start(f32[5,32,128]{2,1,0:T(8,128)S(1)} %get-tuple-element.23), channel_id=1, source_target_pairs={{0,224},{32,0},{64,32},{96,64},{128,96},{160,128},{192,160},{224,1... | collective-permute-start | bytes 245768 | tf_op jit(solution)/shard_map/ppermute | solution.py:886
  29.7 1.8 %collective-permute-start.2 = (f32[24,128]{1,0:T(8,128)S(1)}, f32[24,128]{1,0:T(8,128)S(1)}, u32[]{:S(2)}, u32[]{:S(2)}) collective-permute-start(f32[24,128]{1,0:T(8,128)S(1)} %get-tuple-element.24), channel_id=1, source_target_pairs={{0,8},{8,16},{16,24},{24,0},{1,9},{9,17},{17,25},{25,1},{2,10},{10... | collective-permute-start | bytes 36872 | tf_op jit(solution)/shard_map/ppermute | solution.py:886
  31.5 1.4 %collective-permute-start.3 = (f32[24,128]{1,0:T(8,128)S(1)}, f32[24,128]{1,0:T(8,128)S(1)}, u32[]{:S(2)}, u32[]{:S(2)}) collective-permute-start(f32[24,128]{1,0:T(8,128)S(1)} %get-tuple-element.25), channel_id=1, source_target_pairs={{0,24},{8,0},{16,8},{24,16},{1,25},{9,1},{17,9},{25,17},{2,26},{10... | collective-permute-start | bytes 36872 | tf_op jit(solution)/shard_map/ppermute | solution.py:886
  32.9 2.1 %move.1 = (f32[19,4,32,128]{3,2,1,0:T(8,128)}, f32[128,128]{1,0:T(8,128)S(1)}, f32[2,8,128]{2,1,0:T(8,128)S(1)}) custom-call(f32[19,128,128]{2,1,0:T(8,128)S(1)} %get-tuple-element.16.post_ref, f32[2,128,128]{2,1,0:T(8,128)S(1)} %get-tuple-element.17.bounce_ref, f32[8,128]{1,0:T(8,128)S(1)} %get-tuple-element.18.wall_ref, ...), custom_call_target="tpu_custom_call" | custom-call | flops 1245184 | bytes 2490368 | tf_op jit(solution)/shard_map/move/pallas_call | solution.py:907
  35.1 0.0 collective-permute-done.2.yp_ref
  35.1 0.1 collective-permute-done.3.ym_ref
  35.2 0.0 collective-permute-done.xp_ref
  35.2 0.0 collective-permute-done.1.xm_ref
  35.2 0.8 %faces.1.partly_hbm = f32[19,4,32,128]{3,2,1,0:T(8,128)} custom-call(f32[19,4,32,128]{3,2,1,0:T(8,128)} %get-tuple-element.20.partly_hbm, f32[19,128,128]{2,1,0:T(8,128)S(1)} %get-tuple-element.16.post_ref, f32[2,128,128]{2,1,0:T(8,128)S(1)} %get-tuple-element.17.bounce_ref, ...), custom_call_target="tpu_custom_call", output_to_operand_aliasing={{}: (0, {})} | custom-call | tf_op jit(solution)/shard_map/faces/pallas_call | solution.py:932
  36.0 1.1 %all-to-all-done.1.got2_ref = f32[32,8,128]{2,1,0:T(8,128)S(1)} async-done(((f32[32,8,128]{2,1,0:T(8,128)}), f32[32,8,128]{2,1,0:T(8,128)S(1)}, u32[]{:S(2)}, u32[]{:S(2)}) %all-to-all-start.1) | async-done | bytes 131104 | tf_op jit(solution)/shard_map/all_to_all | solution.py:905
  37.0 1.1 %close.1 = (f32[19,4,32,128]{3,2,1,0:T(8,128)}, f32[6,128]{1,0:T(8,128)}, f32[8,6]{1,0:T(8,128)}) custom-call(f32[19,4,32,128]{3,2,1,0:T(8,128)} %faces.1.partly_hbm, f32[19,128,128]{2,1,0:T(8,128)S(1)} %get-tuple-element.16.post_ref, f32[2,128,128]{2,1,0:T(8,128)S(1)} %get-tuple-element.17.bounce_ref, ...), custom_call_target="tpu_custom_call", output_to_operand_aliasing={{0}: (0, {})} | custom-call | tf_op jit(solution)/shard_map/close/pallas_call | solution.py:942
Async XLA Ops:
  14.8 22.2 %all-to-all-start.1 = ((f32[32,8,128]{2,1,0:T(8,128)}), f32[32,8,128]{2,1,0:T(8,128)S(1)}, u32[]{:S(2)}, u32[]{:S(2)}) async-start(f32[32,8,128]{2,1,0:T(8,128)} %bins.1), calls=%async_computation.1 | async-start | bytes 262144 | tf_op jit(solution)/shard_map/all_to_all | solution.py:905
  26.4 8.8 %collective-permute-start = (f32[5,32,128]{2,1,0:T(8,128)S(1)}, f32[5,32,128]{2,1,0:T(8,128)S(1)}, u32[]{:S(2)}, u32[]{:S(2)}) collective-permute-start(f32[5,32,128]{2,1,0:T(8,128)S(1)} %get-tuple-element.22), channel_id=1, source_target_pairs={{0,32},{32,64},{64,96},{96,128},{128,160},{160,192},{192,224},{224... | collective-permute-start | bytes 245768 | tf_op jit(solution)/shard_map/ppermute | solution.py:886
  28.2 7.0 %collective-permute-start.1 = (f32[5,32,128]{2,1,0:T(8,128)S(1)}, f32[5,32,128]{2,1,0:T(8,128)S(1)}, u32[]{:S(2)}, u32[]{:S(2)}) collective-permute-start(f32[5,32,128]{2,1,0:T(8,128)S(1)} %get-tuple-element.23), channel_id=1, source_target_pairs={{0,224},{32,0},{64,32},{96,64},{128,96},{160,128},{192,160},{224,1... | collective-permute-start | bytes 245768 | tf_op jit(solution)/shard_map/ppermute | solution.py:886
  29.7 5.4 %collective-permute-start.2 = (f32[24,128]{1,0:T(8,128)S(1)}, f32[24,128]{1,0:T(8,128)S(1)}, u32[]{:S(2)}, u32[]{:S(2)}) collective-permute-start(f32[24,128]{1,0:T(8,128)S(1)} %get-tuple-element.24), channel_id=1, source_target_pairs={{0,8},{8,16},{16,24},{24,0},{1,9},{9,17},{17,25},{25,1},{2,10},{10... | collective-permute-start | bytes 36872 | tf_op jit(solution)/shard_map/ppermute | solution.py:886
  31.5 3.7 %collective-permute-start.3 = (f32[24,128]{1,0:T(8,128)S(1)}, f32[24,128]{1,0:T(8,128)S(1)}, u32[]{:S(2)}, u32[]{:S(2)}) collective-permute-start(f32[24,128]{1,0:T(8,128)S(1)} %get-tuple-element.25), channel_id=1, source_target_pairs={{0,24},{8,0},{16,8},{24,16},{1,25},{9,1},{17,9},{25,17},{2,26},{10... | collective-permute-start | bytes 36872 | tf_op jit(solution)/shard_map/ppermute | solution.py:886

commit v11 on v10

--- a/solution.py
+++ b/solution.py
@@ -196,7 +196,7 @@
 
 PLACE_X = (0, 4, 1, 5, 2, 6, 3, 7)
 PLACE_Y = (0, 1, 2, 3)
-PLACE_Z = (0, 4, 2, 6, 1, 5, 3, 7)
+PLACE_Z = (0, 2, 4, 6, 1, 3, 5, 7)
 
 
 def listed(table, index):

time: 38.4 us -> 38.5 us (level); the launches traced: 38.1 us -> 37.8 us
  no operation moved by 1% of the time
where the time goes in v11:
time: 38.5 us; the launch traced here: 37.8 us
  starting transfers between devices  18.1 us (47%)
  Pallas kernels  9.13 us (24%)
  blocking collectives  8.86 us (23%)
  waiting for transfers between devices  1.03 us (3%)
  between operations  0.68 us (2%)
    all_to_all x1, starting transfers between devices, body(): lax.all_to_all(send2, ('gy', 'gx'), 0, 0, axis_index_groups=across, tiled...  11.5 us
    all_to_all x1, blocking collectives, body(): lax.all_to_all(send1, 'gz', 0, 0, axis_index_groups=along_z, tiled=True)  8.86 us
    ppermute x4, starting transfers between devices, shift(): return lax.ppermute(x, axis, [(i, (i + by) % size) for i in range(size)])  6.55 us
    pallas_call x1, Pallas kernels, body(): pl.pallas_call(first_kernel, out_shape=(array(19, 128, 128), array(2, 128...  2.85 us
    pallas_call x1, Pallas kernels, body(): pl.pallas_call(second_kernel, out_shape=array(32, 8, 128), in_specs=[vmem...  2.28 us
    pallas_call x1, Pallas kernels, body(): pl.pallas_call(third_kernel, out_shape=(array(19, 4, 32, 128), array(128,...  2.14 us
    pallas_call x1, Pallas kernels, body(): pl.pallas_call(fourth_kernel, out_shape=(array(19, 4, 32, 128), array(6,...  1.1 us
    all_to_all x1, waiting for transfers between devices, body(): lax.all_to_all(send2, ('gy', 'gx'), 0, 0, axis_index_groups=across, tiled...  0.83 us
  transfers between devices with their start and end apart: 5, of which 2 were waited for; matrix products, arithmetic and copies ran while one was open for 0% of the time, Pallas kernels for 8%

profile of v11, /device:TPU:2, one launch (start us, length us, event | category | flops | bytes accessed | tf_op | source)
XLA Modules:
  0.0 37.8 jit_solution(15903412508681882119)
XLA Ops:
  0.6 2.9 %collide.1 = (f32[19,128,128]{2,1,0:T(8,128)S(1)}, f32[2,128,128]{2,1,0:T(8,128)S(1)}, f32[8,5,8,128]{3,2,1,0:T(8,128)S(1)}, f32[5,32,128]{2,1,0:T(8,128)S(1)}, ...) custom-call(f32[19,128,128]{2,1,0:T(8,128)} %bitcast.8, ...), custom_call_target="tpu_custom_call" | custom-call | tf_op jit(solution)/shard_map/collide/pallas_call | solution.py:836
  3.5 8.9 %all_to_all.10.got1_ref.got_ref = f32[8,5,8,128]{3,2,1,0:T(8,128)S(1)} all-to-all(f32[8,5,8,128]{3,2,1,0:T(8,128)S(1)} %get-tuple-element.19), channel_id=1, replica_groups={{0,4,1,5,2,6,3,7},{8,12,9,13,10,14,11,15},{16,20,17,21,18,22,19,23},{24..., dimensions={0} | all-to-all | bytes 327680 | tf_op jit(solution)/shard_map/all_to_all | solution.py:889
  12.3 2.3 %bins.1 = f32[32,8,128]{2,1,0:T(8,128)} custom-call(f32[8,5,8,128]{3,2,1,0:T(8,128)S(1)} %all_to_all.10.got1_ref.got_ref, f32[8,128]{1,0:T(8,128)S(1)} %get-tuple-element.27.xy_ref), custom_call_target="tpu_custom_call" | custom-call | flops 805306368 | bytes 131072 | tf_op jit(solution)/shard_map/bins/pallas_call | solution.py:890
  14.6 11.5 %all-to-all-start.1 = ((f32[32,8,128]{2,1,0:T(8,128)}), f32[32,8,128]{2,1,0:T(8,128)S(1)}, u32[]{:S(2)}, u32[]{:S(2)}) async-start(f32[32,8,128]{2,1,0:T(8,128)} %bins.1), calls=%async_computation.1 | async-start | bytes 262144 | tf_op jit(solution)/shard_map/all_to_all | solution.py:905
  26.1 1.9 %collective-permute-start = (f32[5,32,128]{2,1,0:T(8,128)S(1)}, f32[5,32,128]{2,1,0:T(8,128)S(1)}, u32[]{:S(2)}, u32[]{:S(2)}) collective-permute-start(f32[5,32,128]{2,1,0:T(8,128)S(1)} %get-tuple-element.22), channel_id=1, source_target_pairs={{0,32},{32,64},{64,96},{96,128},{128,160},{160,192},{192,224},{224... | collective-permute-start | bytes 245768 | tf_op jit(solution)/shard_map/ppermute | solution.py:886
  28.0 1.4 %collective-permute-start.1 = (f32[5,32,128]{2,1,0:T(8,128)S(1)}, f32[5,32,128]{2,1,0:T(8,128)S(1)}, u32[]{:S(2)}, u32[]{:S(2)}) collective-permute-start(f32[5,32,128]{2,1,0:T(8,128)S(1)} %get-tuple-element.23), channel_id=1, source_target_pairs={{0,224},{32,0},{64,32},{96,64},{128,96},{160,128},{192,160},{224,1... | collective-permute-start | bytes 245768 | tf_op jit(solution)/shard_map/ppermute | solution.py:886
  29.5 1.8 %collective-permute-start.2 = (f32[24,128]{1,0:T(8,128)S(1)}, f32[24,128]{1,0:T(8,128)S(1)}, u32[]{:S(2)}, u32[]{:S(2)}) collective-permute-start(f32[24,128]{1,0:T(8,128)S(1)} %get-tuple-element.24), channel_id=1, source_target_pairs={{0,8},{8,16},{16,24},{24,0},{1,9},{9,17},{17,25},{25,1},{2,10},{10... | collective-permute-start | bytes 36872 | tf_op jit(solution)/shard_map/ppermute | solution.py:886
  31.3 1.4 %collective-permute-start.3 = (f32[24,128]{1,0:T(8,128)S(1)}, f32[24,128]{1,0:T(8,128)S(1)}, u32[]{:S(2)}, u32[]{:S(2)}) collective-permute-start(f32[24,128]{1,0:T(8,128)S(1)} %get-tuple-element.25), channel_id=1, source_target_pairs={{0,24},{8,0},{16,8},{24,16},{1,25},{9,1},{17,9},{25,17},{2,26},{10... | collective-permute-start | bytes 36872 | tf_op jit(solution)/shard_map/ppermute | solution.py:886
  32.7 2.1 %move.1 = (f32[19,4,32,128]{3,2,1,0:T(8,128)}, f32[128,128]{1,0:T(8,128)S(1)}, f32[2,8,128]{2,1,0:T(8,128)S(1)}) custom-call(f32[19,128,128]{2,1,0:T(8,128)S(1)} %get-tuple-element.16.post_ref, f32[2,128,128]{2,1,0:T(8,128)S(1)} %get-tuple-element.17.bounce_ref, f32[8,128]{1,0:T(8,128)S(1)} %get-tuple-element.18.wall_ref, ...), custom_call_target="tpu_custom_call" | custom-call | flops 1245184 | bytes 2490368 | tf_op jit(solution)/shard_map/move/pallas_call | solution.py:907
  34.8 0.0 collective-permute-done.2.yp_ref
  34.9 0.2 collective-permute-done.3.ym_ref
  35.0 0.0 collective-permute-done.xp_ref
  35.0 0.0 collective-permute-done.1.xm_ref
  35.1 0.8 %faces.1.partly_hbm = f32[19,4,32,128]{3,2,1,0:T(8,128)} custom-call(f32[19,4,32,128]{3,2,1,0:T(8,128)} %get-tuple-element.20.partly_hbm, f32[19,128,128]{2,1,0:T(8,128)S(1)} %get-tuple-element.16.post_ref, f32[2,128,128]{2,1,0:T(8,128)S(1)} %get-tuple-element.17.bounce_ref, ...), custom_call_target="tpu_custom_call", output_to_operand_aliasing={{}: (0, {})} | custom-call | tf_op jit(solution)/shard_map/faces/pallas_call | solution.py:932
  35.8 0.8 %all-to-all-done.1.got2_ref = f32[32,8,128]{2,1,0:T(8,128)S(1)} async-done(((f32[32,8,128]{2,1,0:T(8,128)}), f32[32,8,128]{2,1,0:T(8,128)S(1)}, u32[]{:S(2)}, u32[]{:S(2)}) %all-to-all-start.1) | async-done | bytes 131104 | tf_op jit(solution)/shard_map/all_to_all | solution.py:905
  36.7 1.1 %close.1 = (f32[19,4,32,128]{3,2,1,0:T(8,128)}, f32[6,128]{1,0:T(8,128)}, f32[8,6]{1,0:T(8,128)}) custom-call(f32[19,4,32,128]{3,2,1,0:T(8,128)} %faces.1.partly_hbm, f32[19,128,128]{2,1,0:T(8,128)S(1)} %get-tuple-element.16.post_ref, f32[2,128,128]{2,1,0:T(8,128)S(1)} %get-tuple-element.17.bounce_ref, ...), custom_call_target="tpu_custom_call", output_to_operand_aliasing={{0}: (0, {})} | custom-call | tf_op jit(solution)/shard_map/close/pallas_call | solution.py:942
Async XLA Ops:
  14.6 22.0 %all-to-all-start.1 = ((f32[32,8,128]{2,1,0:T(8,128)}), f32[32,8,128]{2,1,0:T(8,128)S(1)}, u32[]{:S(2)}, u32[]{:S(2)}) async-start(f32[32,8,128]{2,1,0:T(8,128)} %bins.1), calls=%async_computation.1 | async-start | bytes 262144 | tf_op jit(solution)/shard_map/all_to_all | solution.py:905
  26.1 8.9 %collective-permute-start = (f32[5,32,128]{2,1,0:T(8,128)S(1)}, f32[5,32,128]{2,1,0:T(8,128)S(1)}, u32[]{:S(2)}, u32[]{:S(2)}) collective-permute-start(f32[5,32,128]{2,1,0:T(8,128)S(1)} %get-tuple-element.22), channel_id=1, source_target_pairs={{0,32},{32,64},{64,96},{96,128},{128,160},{160,192},{192,224},{224... | collective-permute-start | bytes 245768 | tf_op jit(solution)/shard_map/ppermute | solution.py:886
  28.0 7.0 %collective-permute-start.1 = (f32[5,32,128]{2,1,0:T(8,128)S(1)}, f32[5,32,128]{2,1,0:T(8,128)S(1)}, u32[]{:S(2)}, u32[]{:S(2)}) collective-permute-start(f32[5,32,128]{2,1,0:T(8,128)S(1)} %get-tuple-element.23), channel_id=1, source_target_pairs={{0,224},{32,0},{64,32},{96,64},{128,96},{160,128},{192,160},{224,1... | collective-permute-start | bytes 245768 | tf_op jit(solution)/shard_map/ppermute | solution.py:886
  29.5 5.4 %collective-permute-start.2 = (f32[24,128]{1,0:T(8,128)S(1)}, f32[24,128]{1,0:T(8,128)S(1)}, u32[]{:S(2)}, u32[]{:S(2)}) collective-permute-start(f32[24,128]{1,0:T(8,128)S(1)} %get-tuple-element.24), channel_id=1, source_target_pairs={{0,8},{8,16},{16,24},{24,0},{1,9},{9,17},{17,25},{25,1},{2,10},{10... | collective-permute-start | bytes 36872 | tf_op jit(solution)/shard_map/ppermute | solution.py:886
  31.3 3.8 %collective-permute-start.3 = (f32[24,128]{1,0:T(8,128)S(1)}, f32[24,128]{1,0:T(8,128)S(1)}, u32[]{:S(2)}, u32[]{:S(2)}) collective-permute-start(f32[24,128]{1,0:T(8,128)S(1)} %get-tuple-element.25), channel_id=1, source_target_pairs={{0,24},{8,0},{16,8},{24,16},{1,25},{9,1},{17,9},{25,17},{2,26},{10... | collective-permute-start | bytes 36872 | tf_op jit(solution)/shard_map/ppermute | solution.py:886
